TPU v7x, 32 devices: a whole 2x2x4 slice. The times are simulated.
32 devices in a mesh: grp: 2 (over x), seq: 4 (over z), mlp: 4 (over y, core).
Axes of the slice: x: 2, y: 2, z: 4, core: 2. Of those that a mesh axis runs over, the one named last changes fastest.
Arguments:
- tokens: bfloat16 [8, 4096, 768], P(('grp', 'mlp'), 'seq'), may hold values from -6 to 6
- step_index: int32 [8, 4], P(('grp', 'mlp')), may hold values from 0 to 1023, as said below
- time_table: bfloat16 [1024, 128], replicated, may hold values from -5 to 5
- ada_weight: bfloat16 [128, 4608], replicated, may hold values from -0.5 to 0.5
- ada_bias: bfloat16 [4608], replicated, may hold values from -3 to 3
- first_gain: bfloat16 [768], replicated, may hold values from 0.099609375 to 1.8984375
- qkv_weight: bfloat16 [768, 2304], replicated, may hold values from -0.21875 to 0.21875
- out_weight: bfloat16 [768, 768], replicated, may hold values from -1.75 to 1.75
- second_gain: bfloat16 [768], replicated, may hold values from 0.099609375 to 1.8984375
- up_weight: bfloat16 [768, 3072], P(None, 'mlp'), may hold values from -0.21875 to 0.21875
- up_bias: bfloat16 [3072], P('mlp'), may hold values from -3 to 3
- down_weight: bfloat16 [3072, 768], P('mlp'), may hold values from -0.109375 to 0.109375
- down_bias: bfloat16 [768], replicated, may hold values from -3 to 3
- cotangent: bfloat16 [8, 4096, 768], P(('grp', 'mlp'), 'seq'), may hold values from -6 to 6
Outputs:
- output: bfloat16 [8, 4096, 768], P(('grp', 'mlp'), 'seq')
- input_grad: float32 [8, 4096, 768], P(('grp', 'mlp'), 'seq')
- table_grad: float32 [1024, 128], P(('seq', 'mlp'))
- ada_weight_grad: float32 [128, 4608], P(None, ('seq', 'mlp'))
- ada_bias_grad: float32 [4608], P(('seq', 'mlp'))
- first_gain_grad: float32 [768], P(('seq', 'mlp'))
- qkv_weight_grad: float32 [768, 2304], P(('seq', 'mlp'))
- out_weight_grad: float32 [768, 768], P(('seq', 'mlp'))
- second_gain_grad: float32 [768], P(('seq', 'mlp'))
- up_weight_grad: float32 [768, 3072], P('seq', 'mlp')
- up_bias_grad: float32 [3072], P(('seq', 'mlp'))
- down_weight_grad: float32 [3072, 768], P('mlp', 'seq')
- down_bias_grad: float32 [768], P(('seq', 'mlp'))
Inputs may be any that keep to these rules, and one draw needn't show every extreme that they name: `step_index`: in each line of the second group (the last 4 rows) the four entries are equal.
All inputs are finite; a program needn't handle non-finite values.
Results may differ from a plain program's by a relative error of at most 0.014.
The roundings to bfloat16 on the way count: a program that leaves them out, or rounds other values in their place, can miss the bound.
Values may be sent and summed in bfloat16 or wider, within the bound.
A program may use at most 384 MiB of HBM per device.

v0:
```python
import math

import jax
import jax.numpy as jnp
from jax import lax
from jax.sharding import PartitionSpec as P

HD = 64


highest = lax.Precision.HIGHEST


def shifted(value, axis, steps):
    count = lax.axis_size(axis)
    pairs = [(source, (source + steps) % count) for source in range(count)]
    return lax.ppermute(value, axis, pairs)


def layer_norm(values, norm_gain):
    centred = values - jnp.mean(values, axis=-1, keepdims=True)
    spread = jnp.mean(centred * centred, axis=-1, keepdims=True)
    return centred * lax.rsqrt(spread + 1e-05) * norm_gain


def modulate(values, norm_gain, shift_part, scale_part):
    return layer_norm(values, norm_gain) * (1.0 + scale_part) + shift_part


def gelu_tanh(values):
    return jax.nn.gelu(values, approximate=True)


def rotate_pairs(values, positions):
    half_dim = HD // 2
    frequency = jnp.exp(jnp.arange(half_dim, dtype=jnp.float32) * (-2.0 * math.log(10000.0) / HD))
    angles = positions.astype(jnp.float32)[:, None] * frequency[None, :]
    cosine = jnp.cos(angles)[:, None, :]
    sine_part = jnp.sin(angles)[:, None, :]
    leading = values[..., :half_dim]
    trailing = values[..., half_dim:]
    return jnp.concatenate(
        [leading * cosine - trailing * sine_part, trailing * cosine + leading * sine_part], axis=-1
    )


def shards(
    tokens,
    step_index,
    time_table,
    ada_weight,
    ada_bias,
    first_gain,
    qkv_weight,
    out_weight,
    second_gain,
    up_weight,
    up_bias,
    down_weight,
    down_bias,
    cotangent,
):
    seq_count = lax.axis_size("seq")
    seq_place = lax.axis_index("seq")
    group_index = lax.axis_index("grp")
    mlp_place = lax.axis_index("mlp")
    tok_rows = tokens.shape[1]
    model_width = tokens.shape[2]
    head_count = model_width // HD
    score_scale = 1.0 / math.sqrt(HD)
    line_len = tok_rows * seq_count
    seq_length = jnp.where(group_index == 0, line_len // 4, line_len).astype(jnp.int32)
    row_ids = jnp.arange(tok_rows, dtype=jnp.int32)
    own_pos = seq_place * tok_rows + row_ids
    positions = own_pos % seq_length
    quarter = seq_place // (seq_count // 4)
    step_value = jnp.sum(jnp.where(jnp.arange(4, dtype=jnp.int32) == quarter, step_index[0], 0))
    table_pick = jnp.arange(time_table.shape[0], dtype=jnp.int32) == step_value
    embedded = jnp.dot(
        table_pick.astype(jnp.bfloat16)[None, :], time_table, preferred_element_type=jnp.float32
    )[0]
    condition, silu_back = jax.vjp(jax.nn.silu, embedded)
    cond_low = condition.astype(jnp.bfloat16)
    modulation = jnp.dot(cond_low[None, :], ada_weight, preferred_element_type=jnp.float32)[
        0
    ] + ada_bias.astype(jnp.float32)
    shift_one, scale_one, gate_one, shift_two, scale_two, gate_two = jnp.split(modulation, 6)
    inputs = tokens[0].astype(jnp.float32)
    normed, first_back = jax.vjp(
        modulate, inputs, first_gain.astype(jnp.float32), shift_one, scale_one
    )
    normed_low = normed.astype(jnp.bfloat16)
    mixed_rows = jnp.dot(normed_low, qkv_weight, preferred_element_type=jnp.float32)

    def rotate_all(mixed_in):
        query_part = rotate_pairs(
            mixed_in[:, :model_width].reshape(tok_rows, head_count, HD), positions
        )
        key_part = rotate_pairs(
            mixed_in[:, model_width : 2 * model_width].reshape(tok_rows, head_count, HD), positions
        )
        return (
            query_part,
            key_part,
            mixed_in[:, 2 * model_width :].reshape(tok_rows, head_count, HD),
        )

    rotated, rotate_back = jax.vjp(rotate_all, mixed_rows)
    queries = rotated[0].astype(jnp.bfloat16)
    key_rows = rotated[1].astype(jnp.bfloat16)
    value_rows = rotated[2].astype(jnp.bfloat16)
    start_state = (
        jnp.full((head_count, tok_rows), -1e30, jnp.float32),
        jnp.zeros((head_count, tok_rows), jnp.float32),
        jnp.zeros((head_count, tok_rows, HD), jnp.float32),
    )
    key_piece = lax.all_gather(key_rows.reshape(tok_rows, model_width), "seq", axis=0, tiled=True)
    value_piece = lax.all_gather(
        value_rows.reshape(tok_rows, model_width), "seq", axis=0, tiled=True
    )
    piece_rows = key_piece.shape[0]
    sub_rows = math.gcd(piece_rows, 512)

    def one_block(block_index, block_state):
        run_max, run_total, run_acc = block_state
        offset = block_index * sub_rows
        key_block = lax.dynamic_slice_in_dim(key_piece, offset, sub_rows, 0).reshape(
            sub_rows, head_count, HD
        )
        value_block = lax.dynamic_slice_in_dim(value_piece, offset, sub_rows, 0).reshape(
            sub_rows, head_count, HD
        )
        key_pos = offset + jnp.arange(sub_rows, dtype=jnp.int32)
        same_seq = (own_pos // seq_length)[:, None] == (key_pos // seq_length)[None, :]
        scores = (
            jnp.einsum("qhd,khd->hqk", queries, key_block, preferred_element_type=jnp.float32)
            * score_scale
        )
        masked = jnp.where(same_seq[None], scores, -1e30)
        new_max = jnp.maximum(run_max, jnp.max(masked, axis=-1))
        shrink = jnp.exp(run_max - new_max)
        weights = jnp.where(same_seq[None], jnp.exp(masked - new_max[..., None]), 0.0)
        run_total = run_total * shrink + jnp.sum(weights, axis=-1)
        run_acc = run_acc * shrink[..., None] + jnp.einsum(
            "hqk,khd->hqd",
            weights.astype(jnp.bfloat16),
            value_block,
            preferred_element_type=jnp.float32,
        )
        return (new_max, run_total, run_acc)

    run_max, run_total, run_acc = lax.fori_loop(0, piece_rows // sub_rows, one_block, start_state)
    log_total = run_max + jnp.log(run_total)
    attended3 = jnp.transpose(run_acc / run_total[..., None], (1, 0, 2))
    attended_low = attended3.reshape(tok_rows, model_width).astype(jnp.bfloat16)
    branch = jnp.dot(attended_low, out_weight, preferred_element_type=jnp.float32)
    middle = inputs + gate_one * branch
    hidden, second_back = jax.vjp(
        modulate, middle, second_gain.astype(jnp.float32), shift_two, scale_two
    )
    hidden_low = hidden.astype(jnp.bfloat16)
    gathered = lax.all_gather(hidden_low, "mlp", axis=0, tiled=True)
    pre_act = jnp.dot(gathered, up_weight, preferred_element_type=jnp.float32) + up_bias.astype(
        jnp.float32
    )
    activated, gelu_back = jax.vjp(gelu_tanh, pre_act)
    act_low = activated.astype(jnp.bfloat16)
    feed_terms = jnp.dot(act_low, down_weight, preferred_element_type=jnp.float32)
    feed_out = lax.psum_scatter(
        feed_terms, "mlp", scatter_dimension=0, tiled=True
    ) + down_bias.astype(jnp.float32)
    output = (middle + gate_two * feed_out).astype(jnp.bfloat16)[None]
    grad_out = cotangent[0].astype(jnp.float32)
    gate_two_grad = jnp.sum(grad_out * feed_out, axis=0)
    grad_feed = (gate_two * grad_out).astype(jnp.bfloat16)
    down_bias_grad = jnp.sum(grad_feed, axis=0, dtype=jnp.float32)
    grad_rows = lax.all_gather(grad_feed, "mlp", axis=0, tiled=True)
    down_grad = jnp.einsum("tf,td->fd", act_low, grad_rows, preferred_element_type=jnp.float32)
    grad_act = jnp.einsum("td,fd->tf", grad_rows, down_weight, preferred_element_type=jnp.float32)
    grad_pre = gelu_back(grad_act)[0].astype(jnp.bfloat16)
    up_grad = jnp.einsum("td,tf->df", gathered, grad_pre, preferred_element_type=jnp.float32)
    local_units = up_weight.shape[1]
    bias_slot = lax.dynamic_update_slice_in_dim(
        jnp.zeros((local_units * lax.axis_size("mlp"),), jnp.float32),
        jnp.sum(grad_pre, axis=0, dtype=jnp.float32),
        mlp_place * local_units,
        0,
    )
    hidden_terms = jnp.einsum("tf,df->td", grad_pre, up_weight, preferred_element_type=jnp.float32)
    grad_hidden = lax.psum_scatter(hidden_terms, "mlp", scatter_dimension=0, tiled=True)
    middle_part, second_gain_grad, shift_two_grad, scale_two_grad = second_back(grad_hidden)
    middle_grad = grad_out + middle_part
    gate_one_grad = jnp.sum(middle_grad * branch, axis=0)
    grad_branch = (gate_one * middle_grad).astype(jnp.bfloat16)
    out_grad = jnp.einsum(
        "td,te->de", attended_low, grad_branch, preferred_element_type=jnp.float32
    )
    grad_attended = jnp.einsum(
        "te,de->td", grad_branch, out_weight, preferred_element_type=jnp.float32
    ).astype(jnp.bfloat16)
    grad_heads = grad_attended.reshape(tok_rows, head_count, HD)
    row_delta = jnp.transpose(jnp.sum(grad_heads.astype(jnp.float32) * attended3, axis=-1))

    def pair_grads(
        query_set, grad_set, total_set, delta_set, query_anchor, key_set, value_set, key_anchor
    ):
        query_pos = query_anchor * tok_rows + row_ids
        key_pos = key_anchor * tok_rows + row_ids
        same_seq = (query_pos // seq_length)[:, None] == (key_pos // seq_length)[None, :]
        scores = (
            jnp.einsum("qhd,khd->hqk", query_set, key_set, preferred_element_type=jnp.float32)
            * score_scale
        )
        prob_rows = jnp.where(same_seq[None], jnp.exp(scores - total_set[..., None]), 0.0)
        value_part = jnp.einsum(
            "hqk,qhd->khd",
            prob_rows.astype(jnp.bfloat16),
            grad_set,
            preferred_element_type=jnp.float32,
        )
        prob_grad = jnp.einsum(
            "qhd,khd->hqk", grad_set, value_set, preferred_element_type=jnp.float32
        )
        score_grad = (prob_rows * (prob_grad - delta_set[..., None])).astype(jnp.bfloat16)
        query_part = (
            jnp.einsum("hqk,khd->qhd", score_grad, key_set, preferred_element_type=jnp.float32)
            * score_scale
        )
        key_part = (
            jnp.einsum("hqk,qhd->khd", score_grad, query_set, preferred_element_type=jnp.float32)
            * score_scale
        )
        return (query_part, key_part, value_part)

    zero_heads = jnp.zeros((tok_rows, head_count, HD), jnp.float32)

    def key_turn(running):
        key_set, value_set, key_acc, value_acc, anchor, query_acc = running
        query_part, key_part, value_part = pair_grads(
            queries, grad_heads, log_total, row_delta, seq_place, key_set, value_set, anchor
        )
        moved_rows = shifted((key_set, value_set), "seq", 1)
        moved_grads = shifted((key_acc + key_part, value_acc + value_part), "seq", 1)
        return (
            moved_rows[0],
            moved_rows[1],
            moved_grads[0],
            moved_grads[1],
            (anchor - 1) % seq_count,
            query_acc + query_part,
        )

    def two_key_turns(turn_index, running):
        return key_turn(key_turn(running))

    finished = lax.fori_loop(
        0,
        seq_count // 2,
        two_key_turns,
        (key_rows, value_rows, zero_heads, zero_heads, seq_place, zero_heads),
    )
    query_grad, key_grad, value_grad = (finished[5], finished[2], finished[3])
    mixed_grad = rotate_back((query_grad, key_grad, value_grad))[0].astype(jnp.bfloat16)
    qkv_grad = jnp.einsum("td,te->de", normed_low, mixed_grad, preferred_element_type=jnp.float32)
    grad_normed = jnp.einsum(
        "te,de->td", mixed_grad, qkv_weight, preferred_element_type=jnp.float32
    )
    input_part, first_gain_grad, shift_one_grad, scale_one_grad = first_back(grad_normed)
    input_grad = (middle_grad + input_part)[None]
    mod_grad = jnp.concatenate(
        [
            shift_one_grad,
            scale_one_grad,
            gate_one_grad,
            shift_two_grad,
            scale_two_grad,
            gate_two_grad,
        ]
    )
    ada_grad = cond_low.astype(jnp.float32)[:, None] * mod_grad[None, :]
    cond_grad = jnp.dot(ada_weight.astype(jnp.float32), mod_grad, precision=highest)
    table_local = table_pick.astype(jnp.float32)[:, None] * silu_back(cond_grad)[0][None, :]
    layer_sums = (
        lax.psum_scatter(table_local, ("seq", "mlp"), scatter_dimension=0, tiled=True),
        lax.psum_scatter(ada_grad, ("seq", "mlp"), scatter_dimension=1, tiled=True),
        lax.psum_scatter(mod_grad, ("seq", "mlp"), scatter_dimension=0, tiled=True),
        lax.psum_scatter(first_gain_grad, ("seq", "mlp"), scatter_dimension=0, tiled=True),
        lax.psum_scatter(qkv_grad, ("seq", "mlp"), scatter_dimension=0, tiled=True),
        lax.psum_scatter(out_grad, ("seq", "mlp"), scatter_dimension=0, tiled=True),
        lax.psum_scatter(second_gain_grad, ("seq", "mlp"), scatter_dimension=0, tiled=True),
        lax.psum_scatter(bias_slot, ("seq", "mlp"), scatter_dimension=0, tiled=True),
        lax.psum_scatter(down_bias_grad, ("seq", "mlp"), scatter_dimension=0, tiled=True),
    )
    feed_summed = (
        lax.psum_scatter(up_grad, "seq", scatter_dimension=0, tiled=True),
        lax.psum_scatter(down_grad, "seq", scatter_dimension=1, tiled=True),
    )
    totals = lax.psum(
        (
            layer_sums[0],
            layer_sums[1],
            layer_sums[2],
            layer_sums[3],
            layer_sums[4],
            layer_sums[5],
            layer_sums[6],
            layer_sums[7],
            layer_sums[8],
            feed_summed[0],
            feed_summed[1],
        ),
        "grp",
    )
    return (
        output,
        input_grad,
        totals[0],
        totals[1],
        totals[2],
        totals[3],
        totals[4],
        totals[5],
        totals[6],
        totals[9],
        totals[7],
        totals[10],
        totals[8],
    )


def solution(mesh):
    in_specs = (
        P(("grp", "mlp"), "seq", None),
        P(("grp", "mlp"), None),
        P(),
        P(),
        P(),
        P(),
        P(),
        P(),
        P(),
        P(None, "mlp"),
        P("mlp"),
        P("mlp", None),
        P(),
        P(("grp", "mlp"), "seq", None),
    )
    out_specs = (
        P(("grp", "mlp"), "seq", None),
        P(("grp", "mlp"), "seq", None),
        P(("seq", "mlp"), None),
        P(None, ("seq", "mlp")),
        P(("seq", "mlp")),
        P(("seq", "mlp")),
        P(("seq", "mlp"), None),
        P(("seq", "mlp"), None),
        P(("seq", "mlp")),
        P("seq", "mlp"),
        P(("seq", "mlp")),
        P("mlp", "seq"),
        P(("seq", "mlp")),
    )
    return jax.shard_map(shards, mesh=mesh, in_specs=in_specs, out_specs=out_specs, check_vma=False)
```

profile of v0, /device:TPU:0, one launch (start us, length us, event | category | flops | bytes accessed | tf_op | source)
XLA Modules:
  0.0 2184.1 jit_solution(7230947800409142819)
XLA Ops:
  54.1 95.5 %all-gather.7.cloned.1.call-done = bf16[4096,768]{1,0:T(8,128)(2,1)} async-done(((bf16[1024,768]{1,0:T(8,128)(2,1)}), bf16[4096,768]{1,0:T(8,128)(2,1)}) %all-gather.7.cloned.1.call-update) | async-done | bytes 6291472 | tf_op jit(solution)/shard_map/all_gather | solution.py:118
  149.6 115.2 %all-gather.5.cloned.1.call-done = bf16[4096,768]{0,1:T(8,128)(2,1)} async-done(((bf16[1024,768]{0,1:T(8,128)(2,1)}), bf16[4096,768]{0,1:T(8,128)(2,1)}) %all-gather.5.cloned.1.call-update) | async-done | bytes 6291472 | tf_op jit(solution)/shard_map/all_gather | solution.py:117
  264.8 355.8 %while.49 = (s32[]{:T(128)}, f32[12,1024]{1,0:T(8,128)}, f32[12,1024]{1,0:T(8,128)}, f32[12,1024,64]{1,2,0:T(8,128)}, s32[]{:T(128)}, /*index=5*/s32[]{:T(128)},...) while((s32[]{:T(128)}, f32[12,1024]{1,0:T(8,128)}, ...), condition=%wide.region_6.7_spmd.clone.clone.clone, body=%wide.region_3.6_spmd.clone.clone.clone.sunk | while | flops 1695361536 | bytes 123550128 | solution.py:152
  271.8 12.0 fusion.225
  283.9 11.8 fusion.226
  295.8 11.8 fusion.228
  316.3 12.0 fusion.225
  328.4 11.8 fusion.226
  340.2 11.8 fusion.228
  360.8 12.0 fusion.225
  372.9 11.8 fusion.226
  384.7 11.8 fusion.228
  405.2 12.0 fusion.225
  417.3 11.8 fusion.226
  429.2 11.8 fusion.228
  449.7 12.0 fusion.225
  461.8 11.8 fusion.226
  473.7 11.8 fusion.228
  494.2 12.0 fusion.225
  506.3 11.8 fusion.226
  518.2 11.8 fusion.228
  538.7 12.0 fusion.225
  562.6 11.8 fusion.228
  583.2 12.0 fusion.225
  607.1 11.8 fusion.228
  638.0 37.1 %all-gather.9.cloned.1.call-done = bf16[4096,768]{0,1:T(8,128)(2,1)} async-done(((bf16[1024,768]{0,1:T(8,128)(2,1)}), bf16[4096,768]{0,1:T(8,128)(2,1)}) %all-gather.9.cloned.1.call-update) | async-done | bytes 6291472 | tf_op jit(solution)/shard_map/all_gather | solution.py:162
  686.1 36.8 %all-gather.11.cloned.1.call-done = bf16[4096,768]{0,1:T(8,128)(2,1)} async-done(((bf16[1024,768]{0,1:T(8,128)(2,1)}), bf16[4096,768]{0,1:T(8,128)(2,1)}) %all-gather.11.cloned.1.call-update) | async-done | bytes 6291472 | tf_op jit(solution)/shard_map/all_gather | solution.py:177
  723.0 20.7 convert_reduce_fusion
  754.3 11.8 fusion.116
  766.2 12.3 fusion.119
  794.2 59.4 %reduce-scatter.11.cloned.1.call-done = f32[1024,768]{0,1:T(8,128)} async-done(((f32[4096,768]{0,1:T(8,128)}), f32[1024,768]{0,1:T(8,128)}) %reduce-scatter.11.cloned.1.call-update) | async-done | bytes 3145744 | tf_op jit(solution)/shard_map/reduce_scatter | solution.py:190
  871.3 928.0 %while.48 = (s32[]{:T(128)}, bf16[1024,12,64]{0,2,1:T(8,128)(2,1)}, bf16[1024,12,64]{0,2,1:T(8,128)(2,1)}, f32[1024,12,64]{0,2,1:T(8,128)}, f32[1024,12,64]{0,2,...) while((s32[]{:T(128)}, bf16[1024,12,64]{0,2,1:T(8,128)(2,1)}, ...), condition=%wide.region_15.16_spmd.clone.clone, body=%wide.region_14.15_spmd.clone.clone.sunk | while | flops 16368561152 | bytes 616227584 | solution.py:256
  896.9 21.8 fusion.218
  921.4 30.3 %multiply_convert_fusion.6 = bf16[12,1024,1024]{2,1,0:T(8,128)(2,1)} fusion(f32[12,1024,1024]{2,1,0:T(8,128)} %fusion.218, f32[12,1024]{1,0:T(8,128)} %get-tuple-element.1151, f32[12,1024]{1,0:T(8,128)} %get-tuple-element.1149, pred[1024,1024]{1,0:T(8,128)(4,1)} %get-tuple-element.1040, bf16[1024,12,64]{0,2,1:T(8,128)(2,1)} %get-tuple-element.1150, ...), kind=kOutput, calls=%fused_computation.5.clone.1 | convolution fusion | flops 1686110208 | bytes 79790080 | tf_op jit(solution)/shard_map/while/body/eval_jaxpr/qhd,khd->hqk/dot_general | solution.py:221
  951.7 15.9 bitcast_add_fusion.11
  969.2 21.4 bitcast_add_fusion.13
  991.5 21.1 fusion.219
  1012.6 30.2 %multiply_convert_fusion.7 = bf16[12,1024,1024]{2,1,0:T(8,128)(2,1)} fusion(f32[12,1024,1024]{2,1,0:T(8,128)} %fusion.219, f32[12,1024]{1,0:T(8,128)} %get-tuple-element.1151, f32[12,1024]{1,0:T(8,128)} %get-tuple-element.1149, pred[1024,1024]{1,0:T(8,128)(4,1)} %get-tuple-element.1041, bf16[1024,12,64]{0,2,1:T(8,128)(2,1)} %get-tuple-element.1150, ...), kind=kOutput, calls=%fused_computation.3.clone.1 | convolution fusion | flops 1686110208 | bytes 79790080 | tf_op jit(solution)/shard_map/while/body/eval_jaxpr/qhd,khd->hqk/dot_general | solution.py:221
  1042.9 52.8 %collective-permute-done.4 = f32[1024,12,64]{0,2,1:T(8,128)} collective-permute-done((f32[1024,12,64]{0,2,1:T(8,128)}, f32[1024,12,64]{0,2,1:T(8,128)}, u32[]{:S(2)}, u32[]{:S(2)}) %collective-permute-start.4) | collective-permute-done | bytes 3145760 | tf_op jit(solution)/shard_map/while/body/eval_jaxpr/ppermute | solution.py:17
  1095.7 15.7 bitcast_add_fusion.12
  1115.7 62.9 %collective-permute-done.6 = f32[1024,12,64]{0,2,1:T(8,128)} collective-permute-done((f32[1024,12,64]{0,2,1:T(8,128)}, f32[1024,12,64]{0,2,1:T(8,128)}, u32[]{:S(2)}, u32[]{:S(2)}) %collective-permute-start.6) | collective-permute-done | bytes 3145760 | tf_op jit(solution)/shard_map/while/body/eval_jaxpr/ppermute | solution.py:17
  1178.6 21.2 bitcast_add_fusion.14
  1199.8 14.1 fusion.220
  1215.0 14.6 bitcast_add_fusion.15
  1229.7 117.5 %collective-permute-done.3 = bf16[1024,12,64]{0,2,1:T(8,128)(2,1)} collective-permute-done((bf16[1024,12,64]{0,2,1:T(8,128)(2,1)}, bf16[1024,12,64]{0,2,1:T(8,128)(2,1)}, u32[]{:S(2)}, u32[]{:S(2)}) %collective-permute-start.3) | collective-permute-done | bytes 1572896 | tf_op jit(solution)/shard_map/while/body/eval_jaxpr/ppermute | solution.py:17
  1347.1 33.2 %collective-permute-done.1 = bf16[1024,12,64]{0,2,1:T(8,128)(2,1)} collective-permute-done((bf16[1024,12,64]{0,2,1:T(8,128)(2,1)}, bf16[1024,12,64]{0,2,1:T(8,128)(2,1)}, u32[]{:S(2)}, u32[]{:S(2)}) %collective-permute-start.1) | collective-permute-done | bytes 1572896 | tf_op jit(solution)/shard_map/while/body/eval_jaxpr/ppermute | solution.py:17
  1380.4 21.0 fusion.218
  1404.1 30.2 %multiply_convert_fusion.6 = bf16[12,1024,1024]{2,1,0:T(8,128)(2,1)} fusion(f32[12,1024,1024]{2,1,0:T(8,128)} %fusion.218, f32[12,1024]{1,0:T(8,128)} %get-tuple-element.1151, f32[12,1024]{1,0:T(8,128)} %get-tuple-element.1149, pred[1024,1024]{1,0:T(8,128)(4,1)} %get-tuple-element.1040, bf16[1024,12,64]{0,2,1:T(8,128)(2,1)} %get-tuple-element.1150, ...), kind=kOutput, calls=%fused_computation.5.clone.1 | convolution fusion | flops 1686110208 | bytes 79790080 | tf_op jit(solution)/shard_map/while/body/eval_jaxpr/qhd,khd->hqk/dot_general | solution.py:221
  1434.3 15.8 bitcast_add_fusion.11
  1451.5 21.4 bitcast_add_fusion.13
  1476.3 21.0 fusion.219
  1497.3 30.2 %multiply_convert_fusion.7 = bf16[12,1024,1024]{2,1,0:T(8,128)(2,1)} fusion(f32[12,1024,1024]{2,1,0:T(8,128)} %fusion.219, f32[12,1024]{1,0:T(8,128)} %get-tuple-element.1151, f32[12,1024]{1,0:T(8,128)} %get-tuple-element.1149, pred[1024,1024]{1,0:T(8,128)(4,1)} %get-tuple-element.1041, bf16[1024,12,64]{0,2,1:T(8,128)(2,1)} %get-tuple-element.1150, ...), kind=kOutput, calls=%fused_computation.3.clone.1 | convolution fusion | flops 1686110208 | bytes 79790080 | tf_op jit(solution)/shard_map/while/body/eval_jaxpr/qhd,khd->hqk/dot_general | solution.py:221
  1527.5 15.8 bitcast_add_fusion.12
  1543.4 47.3 %collective-permute-done.6 = f32[1024,12,64]{0,2,1:T(8,128)} collective-permute-done((f32[1024,12,64]{0,2,1:T(8,128)}, f32[1024,12,64]{0,2,1:T(8,128)}, u32[]{:S(2)}, u32[]{:S(2)}) %collective-permute-start.6) | collective-permute-done | bytes 3145760 | tf_op jit(solution)/shard_map/while/body/eval_jaxpr/ppermute | solution.py:17
  1590.6 21.2 bitcast_add_fusion.14
  1612.4 14.1 fusion.220
  1629.0 15.6 bitcast_add_fusion.15
  1644.6 114.5 %collective-permute-done.3 = bf16[1024,12,64]{0,2,1:T(8,128)(2,1)} collective-permute-done((bf16[1024,12,64]{0,2,1:T(8,128)(2,1)}, bf16[1024,12,64]{0,2,1:T(8,128)(2,1)}, u32[]{:S(2)}, u32[]{:S(2)}) %collective-permute-start.3) | collective-permute-done | bytes 1572896 | tf_op jit(solution)/shard_map/while/body/eval_jaxpr/ppermute | solution.py:17
  1759.1 32.2 %collective-permute-done.1 = bf16[1024,12,64]{0,2,1:T(8,128)(2,1)} collective-permute-done((bf16[1024,12,64]{0,2,1:T(8,128)(2,1)}, bf16[1024,12,64]{0,2,1:T(8,128)(2,1)}, u32[]{:S(2)}, u32[]{:S(2)}) %collective-permute-start.1) | collective-permute-done | bytes 1572896 | tf_op jit(solution)/shard_map/while/body/eval_jaxpr/ppermute | solution.py:17
  1867.0 19.7 reduce-scatter.19.cloned.1.call-done
  1886.7 66.7 %reduce-scatter.15.cloned.1.call-done = f32[128,288]{0,1:T(8,128)} async-done(((f32[128,4608]{0,1:T(8,128)}), f32[128,288]{0,1:T(8,128)}) %reduce-scatter.15.cloned.1.call-update) | async-done | bytes 147472 | tf_op jit(solution)/shard_map/reduce_scatter | solution.py:285
  1953.4 93.1 %reduce-scatter.17.cloned.1.call-done = f32[48,2304]{1,0:T(8,128)} async-done(((f32[768,2304]{1,0:T(8,128)}), f32[48,2304]{1,0:T(8,128)}) %reduce-scatter.17.cloned.1.call-update) | async-done | bytes 442384 | tf_op jit(solution)/shard_map/reduce_scatter | solution.py:288
  2050.6 61.1 %all-reduce.12 = (f32[4608]{0:T(1024)}, f32[768]{0:T(1024)}, f32[768]{0:T(1024)}, f32[3072]{0:T(1024)}, f32[768]{0:T(1024)}) all-reduce(f32[4608]{0:T(1024)} %constant_dynamic-update-slice_fusion, f32[768]{0:T(1024)} %get-tuple-element.778, ...), channel_id=6, replica_groups=mesh['grp'=2,'seq'=4,'mlp'=4] {'seq','mlp'}, use_global_device_ids=true, to_apply=%region_28.29.clone | all-reduce | flops 9984 | bytes 79872
  2132.4 36.1 %all-reduce.17.cloned.1.call-done = (f32[128,288]{0,1:T(8,128)}, f32[48,2304]{1,0:T(8,128)}, f32[48,768]{1,0:T(8,128)}, f32[192,768]{1,0:T(8,128)}, f32[768,192]{0,1:T(8,128)}) async-done(((f32[128,288]{0,1:T(8,128)}, f32[48,2304]{1,0:T(8,128)}, f32[48,768]{1,0:T(8,128)}, f32[192,768]{1,0:T(8,128)}, f32[768,192]{0,1:T(8,128)}), (f32[128,288]{0,1:T(8,128)}, f32[48,2304]{1,0:T(8,128)}, f32[48,768]{1,0:T(8,128)}, ...) | async-done | bytes 1916944 | tf_op jit(solution)/shard_map/psum | solution.py:298
  (478 shorter events, 336.0 us)
Async XLA Ops:
  7.2 15.0 copy-start
  7.2 142.4 %all-gather.7.cloned.1.call-start = ((), (), s32[]{:S(2)}) async-start(), calls=%async_computation.9 | async-start | bytes 7864320 | tf_op jit(solution)/shard_map/all_gather | solution.py:118
  8.1 14.1 copy-start.38
  31.4 233.4 %all-gather.5.cloned.1.call-start = ((), (), s32[]{:S(2)}) async-start(), calls=%async_computation.8 | async-start | bytes 7864320 | tf_op jit(solution)/shard_map/all_gather | solution.py:117
  45.9 629.2 %all-gather.9.cloned.1.call-start = ((), (), s32[]{:S(2)}) async-start(), calls=%async_computation.10 | async-start | bytes 7864320 | tf_op jit(solution)/shard_map/all_gather | solution.py:162
  271.8 12.1 copy-start.17
  271.8 12.1 copy-start.3
  316.3 12.1 copy-start.17
  316.3 12.1 copy-start.3
  360.7 12.1 copy-start.17
  360.8 12.1 copy-start.3
  405.2 12.1 copy-start.17
  405.2 12.1 copy-start.3
  449.7 12.1 copy-start.17
  449.7 12.1 copy-start.3
  494.2 12.1 copy-start.17
  494.2 12.1 copy-start.3
  538.7 12.1 copy-start.17
  538.7 12.1 copy-start.3
  583.1 12.1 copy-start.17
  583.2 12.1 copy-start.3
  630.4 92.6 %all-gather.11.cloned.1.call-start = ((), (), s32[]{:S(2)}) async-start(), calls=%async_computation.12 | async-start | bytes 7864320 | tf_op jit(solution)/shard_map/all_gather | solution.py:177
  636.7 216.8 %reduce-scatter.11.cloned.1.call-start = ((), (), s32[]{:S(2)}) async-start(), calls=%async_computation.13 | async-start | bytes 15728640 | tf_op jit(solution)/shard_map/reduce_scatter | solution.py:190
  723.0 23.4 %copy-start.64 = (bf16[768,768]{1,0:T(8,128)(2,1)S(1)}, bf16[768,768]{1,0:T(8,128)(2,1)}, u32[]{:S(2)}) copy-start(bf16[768,768]{1,0:T(8,128)(2,1)} %param.27) | copy-start | bytes 3538948
  754.3 1077.4 %reduce-scatter.9.cloned.1.call-start = ((), (), s32[]{:S(2)}) async-start(), calls=%async_computation.11 | async-start | bytes 15728640 | tf_op jit(solution)/shard_map/reduce_scatter | solution.py:169
  766.2 1100.8 %reduce-scatter.21.cloned.1.call-start = ((), (), s32[]{:S(2)}) async-start(), calls=%async_computation.18 | async-start | bytes 2949120 | tf_op jit(solution)/shard_map/reduce_scatter | solution.py:295
  778.5 1088.4 %reduce-scatter.23.cloned.1.call-start = ((), (), s32[]{:S(2)}) async-start(), calls=%async_computation.19 | async-start | bytes 2949120 | tf_op jit(solution)/shard_map/reduce_scatter | solution.py:296
  794.1 1092.6 %reduce-scatter.19.cloned.1.call-start = ((), (), s32[]{:S(2)}) async-start(), calls=%async_computation.17 | async-start | bytes 2506752 | tf_op jit(solution)/shard_map/reduce_scatter | solution.py:289
  894.1 118.5 %collective-permute-start.2 = (bf16[1024,12,64]{0,2,1:T(8,128)(2,1)}, bf16[1024,12,64]{0,2,1:T(8,128)(2,1)}, u32[]{:S(2)}, u32[]{:S(2)}) collective-permute-start(bf16[1024,12,64]{0,2,1:T(8,128)(2,1)} %get-tuple-element.1120), channel_id=1, source_target_pairs={{0,4},{4,8},{8,12},{12,0},{1,5},{5,9},{9,13},{13,1},{2,6},{6,10},{... | collective-permute-start | bytes 4718600 | tf_op jit(solution)/shard_map/while/body/eval_jaxpr/ppermute | solution.py:17
  895.4 96.2 %collective-permute-start = (bf16[1024,12,64]{0,2,1:T(8,128)(2,1)}, bf16[1024,12,64]{0,2,1:T(8,128)(2,1)}, u32[]{:S(2)}, u32[]{:S(2)}) collective-permute-start(bf16[1024,12,64]{0,2,1:T(8,128)(2,1)} %get-tuple-element.1119), channel_id=1, source_target_pairs={{0,4},{4,8},{8,12},{12,0},{1,5},{5,9},{9,13},{13,1},{2,6},{6,10},{... | collective-permute-start | bytes 4718600 | tf_op jit(solution)/shard_map/while/body/eval_jaxpr/ppermute | solution.py:17
  951.7 17.4 copy-start.8
  951.7 17.4 copy-start.29
  951.7 17.4 copy-start.40
  967.7 128.0 %collective-permute-start.4 = (f32[1024,12,64]{0,2,1:T(8,128)}, f32[1024,12,64]{0,2,1:T(8,128)}, u32[]{:S(2)}, u32[]{:S(2)}) collective-permute-start(f32[1024,12,64]{0,2,1:T(8,128)} %bitcast_add_fusion.11), channel_id=1, source_target_pairs={{0,4},{4,8},{8,12},{12,0},{1,5},{5,9},{9,13},{13,1},{2,6},{6,10},{... | collective-permute-start | bytes 9437192 | tf_op jit(solution)/shard_map/while/body/eval_jaxpr/ppermute | solution.py:17
  990.5 188.1 %collective-permute-start.6 = (f32[1024,12,64]{0,2,1:T(8,128)}, f32[1024,12,64]{0,2,1:T(8,128)}, u32[]{:S(2)}, u32[]{:S(2)}) collective-permute-start(f32[1024,12,64]{0,2,1:T(8,128)} %bitcast_add_fusion.13), channel_id=1, source_target_pairs={{0,4},{4,8},{8,12},{12,0},{1,5},{5,9},{9,13},{13,1},{2,6},{6,10},{... | collective-permute-start | bytes 9437192 | tf_op jit(solution)/shard_map/while/body/eval_jaxpr/ppermute | solution.py:17
  1042.9 135.7 %copy-start.7 = (pred[1024,1024]{1,0:T(8,128)(4,1)S(1)}, pred[1024,1024]{1,0:T(8,128)(4,1)}, u32[]{:S(2)}) copy-start(pred[1024,1024]{1,0:T(8,128)(4,1)} %get-tuple-element.1041) | copy-start | bytes 3145732 | tf_op jit(solution)/shard_map/while
  1042.9 135.7 %copy-start.30 = (bf16[1024,12,64]{0,2,1:T(8,128)(2,1)S(1)}, bf16[1024,12,64]{0,2,1:T(8,128)(2,1)}, u32[]{:S(2)}) copy-start(bf16[1024,12,64]{0,2,1:T(8,128)(2,1)} %get-tuple-element.1150) | copy-start | bytes 4718596 | tf_op jit(solution)/shard_map/while
  1042.9 135.7 %copy-start.41 = (f32[12,1024]{1,0:T(8,128)S(1)}, f32[12,1024]{1,0:T(8,128)}, u32[]{:S(2)}) copy-start(f32[12,1024]{1,0:T(8,128)} %get-tuple-element.1149) | copy-start | bytes 147460 | tf_op jit(solution)/shard_map/while
  1111.4 268.9 %collective-permute-start.5 = (f32[1024,12,64]{0,2,1:T(8,128)}, f32[1024,12,64]{0,2,1:T(8,128)}, u32[]{:S(2)}, u32[]{:S(2)}) collective-permute-start(f32[1024,12,64]{0,2,1:T(8,128)} %bitcast_add_fusion.12), channel_id=1, source_target_pairs={{0,4},{4,8},{8,12},{12,0},{1,5},{5,9},{9,13},{13,1},{2,6},{6,10},{... | collective-permute-start | bytes 9437192 | tf_op jit(solution)/shard_map/while/body/eval_jaxpr/ppermute | solution.py:17
  1199.8 180.5 %collective-permute-start.7 = (f32[1024,12,64]{0,2,1:T(8,128)}, f32[1024,12,64]{0,2,1:T(8,128)}, u32[]{:S(2)}, u32[]{:S(2)}) collective-permute-start(f32[1024,12,64]{0,2,1:T(8,128)} %bitcast_add_fusion.14), channel_id=1, source_target_pairs={{0,4},{4,8},{8,12},{12,0},{1,5},{5,9},{9,13},{13,1},{2,6},{6,10},{... | collective-permute-start | bytes 9437192 | tf_op jit(solution)/shard_map/while/body/eval_jaxpr/ppermute | solution.py:17
  1213.9 133.2 %collective-permute-start.3 = (bf16[1024,12,64]{0,2,1:T(8,128)(2,1)}, bf16[1024,12,64]{0,2,1:T(8,128)(2,1)}, u32[]{:S(2)}, u32[]{:S(2)}) collective-permute-start(bf16[1024,12,64]{0,2,1:T(8,128)(2,1)} %collective-permute-done.2), channel_id=1, source_target_pairs={{0,4},{4,8},{8,12},{12,0},{1,5},{5,9},{9,13},{13,1},{2,6},{6,10},{... | collective-permute-start | bytes 4718600 | tf_op jit(solution)/shard_map/while/body/eval_jaxpr/ppermute | solution.py:17
  1213.9 166.4 %collective-permute-start.1 = (bf16[1024,12,64]{0,2,1:T(8,128)(2,1)}, bf16[1024,12,64]{0,2,1:T(8,128)(2,1)}, u32[]{:S(2)}, u32[]{:S(2)}) collective-permute-start(bf16[1024,12,64]{0,2,1:T(8,128)(2,1)} %collective-permute-done), channel_id=1, source_target_pairs={{0,4},{4,8},{8,12},{12,0},{1,5},{5,9},{9,13},{13,1},{2,6},{6,10},{... | collective-permute-start | bytes 4718600 | tf_op jit(solution)/shard_map/while/body/eval_jaxpr/ppermute | solution.py:17
  1380.3 117.0 %collective-permute-start.2 = (bf16[1024,12,64]{0,2,1:T(8,128)(2,1)}, bf16[1024,12,64]{0,2,1:T(8,128)(2,1)}, u32[]{:S(2)}, u32[]{:S(2)}) collective-permute-start(bf16[1024,12,64]{0,2,1:T(8,128)(2,1)} %get-tuple-element.1120), channel_id=1, source_target_pairs={{0,4},{4,8},{8,12},{12,0},{1,5},{5,9},{9,13},{13,1},{2,6},{6,10},{... | collective-permute-start | bytes 4718600 | tf_op jit(solution)/shard_map/while/body/eval_jaxpr/ppermute | solution.py:17
  1380.3 96.0 %collective-permute-start = (bf16[1024,12,64]{0,2,1:T(8,128)(2,1)}, bf16[1024,12,64]{0,2,1:T(8,128)(2,1)}, u32[]{:S(2)}, u32[]{:S(2)}) collective-permute-start(bf16[1024,12,64]{0,2,1:T(8,128)(2,1)} %get-tuple-element.1119), channel_id=1, source_target_pairs={{0,4},{4,8},{8,12},{12,0},{1,5},{5,9},{9,13},{13,1},{2,6},{6,10},{... | collective-permute-start | bytes 4718600 | tf_op jit(solution)/shard_map/while/body/eval_jaxpr/ppermute | solution.py:17
  1434.2 17.3 copy-start.8
  1434.2 17.3 copy-start.29
  1434.3 17.3 copy-start.40
  1450.1 77.4 %collective-permute-start.4 = (f32[1024,12,64]{0,2,1:T(8,128)}, f32[1024,12,64]{0,2,1:T(8,128)}, u32[]{:S(2)}, u32[]{:S(2)}) collective-permute-start(f32[1024,12,64]{0,2,1:T(8,128)} %bitcast_add_fusion.11), channel_id=1, source_target_pairs={{0,4},{4,8},{8,12},{12,0},{1,5},{5,9},{9,13},{13,1},{2,6},{6,10},{... | collective-permute-start | bytes 9437192 | tf_op jit(solution)/shard_map/while/body/eval_jaxpr/ppermute | solution.py:17
  1472.9 117.7 %collective-permute-start.6 = (f32[1024,12,64]{0,2,1:T(8,128)}, f32[1024,12,64]{0,2,1:T(8,128)}, u32[]{:S(2)}, u32[]{:S(2)}) collective-permute-start(f32[1024,12,64]{0,2,1:T(8,128)} %bitcast_add_fusion.13), channel_id=1, source_target_pairs={{0,4},{4,8},{8,12},{12,0},{1,5},{5,9},{9,13},{13,1},{2,6},{6,10},{... | collective-permute-start | bytes 9437192 | tf_op jit(solution)/shard_map/while/body/eval_jaxpr/ppermute | solution.py:17
  1527.5 63.1 %copy-start.7 = (pred[1024,1024]{1,0:T(8,128)(4,1)S(1)}, pred[1024,1024]{1,0:T(8,128)(4,1)}, u32[]{:S(2)}) copy-start(pred[1024,1024]{1,0:T(8,128)(4,1)} %get-tuple-element.1041) | copy-start | bytes 3145732 | tf_op jit(solution)/shard_map/while
  1527.5 63.1 %copy-start.30 = (bf16[1024,12,64]{0,2,1:T(8,128)(2,1)S(1)}, bf16[1024,12,64]{0,2,1:T(8,128)(2,1)}, u32[]{:S(2)}) copy-start(bf16[1024,12,64]{0,2,1:T(8,128)(2,1)} %get-tuple-element.1150) | copy-start | bytes 4718596 | tf_op jit(solution)/shard_map/while
  1527.5 63.1 %copy-start.41 = (f32[12,1024]{1,0:T(8,128)S(1)}, f32[12,1024]{1,0:T(8,128)}, u32[]{:S(2)}) copy-start(f32[12,1024]{1,0:T(8,128)} %get-tuple-element.1149) | copy-start | bytes 147460 | tf_op jit(solution)/shard_map/while
  1543.3 248.1 %collective-permute-start.5 = (f32[1024,12,64]{0,2,1:T(8,128)}, f32[1024,12,64]{0,2,1:T(8,128)}, u32[]{:S(2)}, u32[]{:S(2)}) collective-permute-start(f32[1024,12,64]{0,2,1:T(8,128)} %bitcast_add_fusion.12), channel_id=1, source_target_pairs={{0,4},{4,8},{8,12},{12,0},{1,5},{5,9},{9,13},{13,1},{2,6},{6,10},{... | collective-permute-start | bytes 9437192 | tf_op jit(solution)/shard_map/while/body/eval_jaxpr/ppermute | solution.py:17
  1611.8 179.5 %collective-permute-start.7 = (f32[1024,12,64]{0,2,1:T(8,128)}, f32[1024,12,64]{0,2,1:T(8,128)}, u32[]{:S(2)}, u32[]{:S(2)}) collective-permute-start(f32[1024,12,64]{0,2,1:T(8,128)} %bitcast_add_fusion.14), channel_id=1, source_target_pairs={{0,4},{4,8},{8,12},{12,0},{1,5},{5,9},{9,13},{13,1},{2,6},{6,10},{... | collective-permute-start | bytes 9437192 | tf_op jit(solution)/shard_map/while/body/eval_jaxpr/ppermute | solution.py:17
  1626.5 132.7 %collective-permute-start.3 = (bf16[1024,12,64]{0,2,1:T(8,128)(2,1)}, bf16[1024,12,64]{0,2,1:T(8,128)(2,1)}, u32[]{:S(2)}, u32[]{:S(2)}) collective-permute-start(bf16[1024,12,64]{0,2,1:T(8,128)(2,1)} %collective-permute-done.2), channel_id=1, source_target_pairs={{0,4},{4,8},{8,12},{12,0},{1,5},{5,9},{9,13},{13,1},{2,6},{6,10},{... | collective-permute-start | bytes 4718600 | tf_op jit(solution)/shard_map/while/body/eval_jaxpr/ppermute | solution.py:17
  1629.0 162.4 %collective-permute-start.1 = (bf16[1024,12,64]{0,2,1:T(8,128)(2,1)}, bf16[1024,12,64]{0,2,1:T(8,128)(2,1)}, u32[]{:S(2)}, u32[]{:S(2)}) collective-permute-start(bf16[1024,12,64]{0,2,1:T(8,128)(2,1)} %collective-permute-done), channel_id=1, source_target_pairs={{0,4},{4,8},{8,12},{12,0},{1,5},{5,9},{9,13},{13,1},{2,6},{6,10},{... | collective-permute-start | bytes 4718600 | tf_op jit(solution)/shard_map/while/body/eval_jaxpr/ppermute | solution.py:17
  1824.1 129.3 %reduce-scatter.15.cloned.1.call-start = ((), (), s32[]{:S(2)}) async-start(), calls=%async_computation.15 | async-start | bytes 2506752 | tf_op jit(solution)/shard_map/reduce_scatter | solution.py:285
  1831.7 12.1 copy-start.56
  1831.7 13.4 copy-start.55
  1831.7 16.0 copy-start.63
  1851.0 195.5 %reduce-scatter.17.cloned.1.call-start = ((), (), s32[]{:S(2)}) async-start(), calls=%async_computation.16 | async-start | bytes 7520256 | tf_op jit(solution)/shard_map/reduce_scatter | solution.py:288
  1862.7 187.9 %copy-start.57 = (f32[768]{0:T(1024)S(1)}, f32[768]{0:T(1024)}, u32[]{:S(2)}) copy-start(f32[768]{0:T(1024)} %get-tuple-element.850) | copy-start | bytes 9220
  1862.7 259.4 %reduce-scatter.13.cloned.1.call-start = ((), (), s32[]{:S(2)}) async-start(), calls=%async_computation.14 | async-start | bytes 557056 | tf_op jit(solution)/shard_map/reduce_scatter | solution.py:284
  1866.9 301.7 %all-reduce.17.cloned.1.call-start = ((), (), s32[]{:S(2)}) async-start(), calls=%async_computation.20 | async-start | bytes 3833856 | tf_op jit(solution)/shard_map/psum | solution.py:298
  (86 other events, 554.6 us)
Sparse Core Ops, SparseCore 0:
  31.5 118.0 all-gather.6
  151.1 113.5 all-gather.4
  630.5 44.5 all-gather.8
  676.5 46.3 all-gather.10
  754.4 99.0 reduce-scatter.10
  856.0 99.0 reduce-scatter.8
  957.3 79.3 reduce-scatter.20
  1039.0 88.6 reduce-scatter.22
  1824.2 62.4 reduce-scatter.18
  1891.4 61.9 reduce-scatter.14
  1957.4 89.0 reduce-scatter.16
  2050.9 55.3 reduce-scatter.12
  2108.9 59.6 all-reduce.16
where the time goes:
time: 2190 us; the launch traced here: 2180 us
  waiting for transfers between devices  1020 us (47%)
  matrix products  714 us (33%)
  other arithmetic  178 us (8%)
  local copies, waits for them, and re-layouts  133 us (6%)
  blocking collectives  71.3 us (3%)
  loops' own time  31.9 us (1%)
    ppermute x16, waiting for transfers between devices, shifted(): return lax.ppermute(value, axis, pairs)  460 us
    dot_general x4, matrix products, pair_grads(): jnp.einsum('qhd,khd->hqk', grad_set, value_set, preferred_element_type=jn...  121 us
    all_gather x1, waiting for transfers between devices, shards(): lax.all_gather(key_rows.reshape(tok_rows, model_width), 'seq', axis=0, ti...  115 us
    dot_general x8, matrix products, one_block(): jnp.einsum('qhd,khd->hqk', queries, key_block, preferred_element_type=jnp...  96.3 us
    all_gather x1, waiting for transfers between devices, shards(): lax.all_gather(value_rows.reshape(tok_rows, model_width), 'seq', axis=0,...  95.5 us
    dot_general x8, matrix products, one_block(): jnp.einsum('hqk,khd->hqd', weights.astype(jnp.bfloat16), value_block, pre...  94.2 us
    reduce_sum x8, other arithmetic, one_block(): run_total = run_total * shrink + jnp.sum(weights, axis=-1)  94.1 us
    reduce_scatter x1, waiting for transfers between devices, shards(): lax.psum_scatter(qkv_grad, ('seq', 'mlp'), scatter_dimension=0, tiled=True)  93.1 us
  transfers between devices with their start and end apart: 29, of which 16 were waited for; matrix products, arithmetic and copies ran while one was open for 27% of the time, Pallas kernels for 0%

commit v1 on v0

--- a/solution.py
+++ b/solution.py
@@ -3,6 +3,8 @@
 import jax
 import jax.numpy as jnp
 from jax import lax
+from jax.experimental import pallas as pl
+from jax.experimental.pallas import tpu as pltpu
 from jax.sharding import PartitionSpec as P
 
 HD = 64
@@ -328,6 +330,806 @@
     )
 
 
+LOG_SCALE = math.log2(math.e) / math.sqrt(HD)
+NT = (((1,), (1,)), ((), ()))
+TN = (((0,), (0,)), ((), ()))
+F32 = jnp.float32
+BF16 = jnp.bfloat16
+WHOLE_VMEM = 60 * 1024 * 1024
+
+
+def params(*semantics):
+    return pltpu.CompilerParams(vmem_limit_bytes=WHOLE_VMEM, dimension_semantics=semantics)
+
+
+def low_lanes(value):
+    return lax.broadcasted_iota(jnp.int32, value.shape, 1) < HD
+
+
+def swap_heads(value):
+    return pltpu.roll(value, HD, 1)
+
+
+def exchange(top, bottom):
+    keep = low_lanes(top)
+    return (
+        jnp.where(keep, top, swap_heads(bottom)),
+        jnp.where(keep, swap_heads(top), bottom),
+    )
+
+
+def fold(value):
+    half = value.shape[0] // 2
+    top = value[:half]
+    return jnp.where(low_lanes(top), top, swap_heads(value[half:]))
+
+
+def unfold_into(target, base, packed, fill):
+    half = packed.shape[0]
+    value = packed.astype(F32)
+    keep = low_lanes(value)
+    target[base : base + half, :] = jnp.where(keep, value, fill).astype(BF16)
+    target[base + half : base + 2 * half, :] = jnp.where(keep, swap_heads(value), fill).astype(BF16)
+
+
+def turn(value, cosine, sine):
+    lane = lax.broadcasted_iota(jnp.int32, value.shape, 1) % HD
+    quarter = HD // 2
+    other = jnp.where(
+        lane < quarter, pltpu.roll(value, 2 * HD - quarter, 1), pltpu.roll(value, quarter, 1)
+    )
+    return value * cosine + other * sine
+
+
+def normalise(values):
+    centred = values - jnp.mean(values, axis=-1, keepdims=True)
+    spread = jnp.mean(centred * centred, axis=-1, keepdims=True)
+    inverse = lax.rsqrt(spread + 1e-05)
+    return centred * inverse, inverse
+
+
+def project_kernel(x_ref, vec_ref, w_ref, cos_ref, sin_ref, normed_ref, pack_ref):
+    rows = x_ref.shape[1]
+    width = x_ref.shape[2]
+    x = x_ref[...].reshape(2 * rows, width).astype(F32)
+    n, _ = normalise(x)
+    normed = n * vec_ref[0:1, :] * (1.0 + vec_ref[1:2, :]) + vec_ref[2:3, :]
+    normed = normed.astype(BF16)
+    normed_ref[...] = normed.reshape(2, rows, width)
+    cosine = cos_ref[...].reshape(2 * rows, 2 * HD)
+    sine = sin_ref[...].reshape(2 * rows, 2 * HD)
+    for part in range(3):
+        mixed = jnp.dot(
+            normed, w_ref[:, part * width : (part + 1) * width], preferred_element_type=F32
+        )
+        for pair in range(width // (2 * HD)):
+            value = mixed[:, pair * 2 * HD : (pair + 1) * 2 * HD]
+            if part < 2:
+                value = turn(value, cosine, sine)
+            even, odd = exchange(value[:rows], value[rows:])
+            pack_ref[2 * pair, part] = even.astype(BF16)
+            pack_ref[2 * pair + 1, part] = odd.astype(BF16)
+
+
+def project(x2, vecs, weight, cosine, sine, rows=256):
+    half, width = x2.shape[1:]
+    heads = width // HD
+    tok = lambda last: pl.BlockSpec((2, rows, last), lambda i: (0, i, 0))
+    return pl.pallas_call(
+        project_kernel,
+        grid=(half // rows,),
+        in_specs=[
+            tok(width),
+            pl.BlockSpec(vecs.shape, lambda i: (0, 0)),
+            pl.BlockSpec(weight.shape, lambda i: (0, 0)),
+            tok(2 * HD),
+            tok(2 * HD),
+        ],
+        out_specs=[tok(width), pl.BlockSpec((heads, 3, rows, 2 * HD), lambda i: (0, 0, i, 0))],
+        out_shape=[
+            jax.ShapeDtypeStruct((2, half, width), BF16),
+            jax.ShapeDtypeStruct((heads, 3, half, 2 * HD), BF16),
+        ],
+        compiler_params=params("arbitrary"),
+        name="project",
+    )(x2, vecs, weight, cosine, sine)
+
+
+def attend_rows(q, k_ref, v_ref, keys, out_put, log_put, block=512):
+    top = None
+    for start in range(0, keys, block):
+        s = lax.dot_general(q, k_ref[start : start + block, :], NT, preferred_element_type=F32)
+        s = s * LOG_SCALE
+        peak = jnp.max(s, axis=1, keepdims=True)
+        new_top = peak if top is None else jnp.maximum(top, peak)
+        p = jnp.exp2(s - new_top).astype(BF16)
+        part = jnp.dot(p, v_ref[start : start + block, :], preferred_element_type=F32)
+        acc = part if top is None else acc * jnp.exp2(top - new_top) + part
+        top = new_top
+    out_put(fold(acc / swap_heads(acc)).astype(BF16))
+    log_put((top + jnp.log2(acc)).T[HD : HD + 8])
+
+
+def load_forward(source, base, q_s, k_s, v_s):
+    unfold_into(q_s, base, source[0], 0.0)
+    unfold_into(k_s, base, source[1], 0.0)
+    unfold_into(v_s, base, source[2], 1.0)
+
+
+def full_step(step, pieces, o_ref, log_ref, q_s, k_s, v_s):
+    piece_rows = 2 * pieces[0].shape[1]
+    total = piece_rows * len(pieces)
+
+    @pl.when(step == 0)
+    def _():
+        for place, piece in enumerate(pieces):
+            load_forward(piece, place * piece_rows, q_s, k_s, v_s)
+
+    def put_out(value):
+        o_ref[step] = value
+
+    def put_log(value):
+        log_ref[step] = value
+
+    q = q_s[pl.ds(pl.multiple_of(step * piece_rows, piece_rows), piece_rows), :]
+    attend_rows(q, k_s, v_s, total, put_out, put_log)
+
+
+def forward_second_kernel(p0, p1, p2, p3, o_ref, log_ref, q_s, k_s, v_s):
+    full_step(pl.program_id(0), (p0, p1, p2, p3), o_ref, log_ref, q_s, k_s, v_s)
+
+
+def forward_first_kernel(
+    group_ref, pack_ref, p0, p1, p2, p3, o_ref, log_ref, ol_ref, logl_ref, q_s, k_s, v_s
+):
+    step = pl.program_id(0)
+    group = group_ref[0]
+
+    @pl.when(group == 0)
+    def _():
+        rows = 2 * p0.shape[1]
+        load_forward(pack_ref.at[0], 0, q_s, k_s, v_s)
+
+        def put_out(value):
+            ol_ref[step] = value
+
+        def put_log(value):
+            logl_ref[step] = value
+
+        attend_rows(q_s[0:rows, :], k_s, v_s, rows, put_out, put_log)
+
+    @pl.when((group == 1) & (step < 4))
+    def _():
+        full_step(step, (p0, p1, p2, p3), o_ref, log_ref, q_s, k_s, v_s)
+
+
+def whole(shape):
+    zeros = (0,) * len(shape)
+    return pl.BlockSpec(shape, lambda *_: zeros)
+
+
+def forward_scratch(half):
+    return [pltpu.VMEM((8 * half, 2 * HD), BF16)] * 3
+
+
+def forward_first(group, packs, pieces):
+    heads, _, half, lanes = packs.shape
+    o4, l4 = (4, half, lanes), (4, 8, 2 * half)
+    o12, l12 = (heads, half, lanes), (heads, 8, 2 * half)
+    shapes = [(o4, BF16), (l4, F32), (o12, BF16), (l12, F32)]
+    return pl.pallas_call(
+        forward_first_kernel,
+        grid_spec=pltpu.PrefetchScalarGridSpec(
+            num_scalar_prefetch=1,
+            grid=(heads,),
+            in_specs=[pl.BlockSpec((1, 3, half, lanes), lambda i, g: (i * (1 - g[0]), 0, 0, 0))]
+            + [whole(pieces[0].shape)] * 4,
+            out_specs=[whole(shape) for shape, _ in shapes],
+            scratch_shapes=forward_scratch(half),
+        ),
+        out_shape=[jax.ShapeDtypeStruct(shape, kind) for shape, kind in shapes],
+        compiler_params=params("arbitrary"),
+        cost_estimate=pl.CostEstimate(
+            flops=40_000_000_000, bytes_accessed=8_000_000, transcendentals=0
+        ),
+        name="forward_first",
+    )(group, packs, *pieces)
+
+
+def forward_second(pieces):
+    _, half, lanes = pieces[0].shape
+    shapes = [((4, half, lanes), BF16), ((4, 8, 2 * half), F32)]
+    return pl.pallas_call(
+        forward_second_kernel,
+        grid=(4,),
+        in_specs=[whole(pieces[0].shape)] * 4,
+        out_specs=[whole(shape) for shape, _ in shapes],
+        out_shape=[jax.ShapeDtypeStruct(shape, kind) for shape, kind in shapes],
+        scratch_shapes=forward_scratch(half),
+        compiler_params=params("arbitrary"),
+        cost_estimate=pl.CostEstimate(
+            flops=40_000_000_000, bytes_accessed=8_000_000, transcendentals=0
+        ),
+        name="forward_second",
+    )(*pieces)
+
+
+def tile_grads(q, do, k, v, log_row, delta_row):
+    s = lax.dot_general(k, q, NT, preferred_element_type=F32)
+    p = jnp.exp2(s * LOG_SCALE - log_row)
+    dp = lax.dot_general(v, do, NT, preferred_element_type=F32)
+    ds = (p * (dp - delta_row)).astype(BF16)
+    dv = jnp.dot(p.astype(BF16), do, preferred_element_type=F32)
+    dk = jnp.dot(ds, q, preferred_element_type=F32)
+    dq = lax.dot_general(k, ds, TN, preferred_element_type=F32)
+    return dq, dk, dv
+
+
+def load_backward(source, do, o, base, q_s, k_s, v_s, do_s, delta_s):
+    half = do.shape[0]
+    unfold_into(q_s, base, source[0], 0.0)
+    unfold_into(k_s, base, source[1], 0.0)
+    unfold_into(v_s, base, source[2], 0.0)
+    unfold_into(do_s, base, do, 0.0)
+    product = (do.astype(F32) * o.astype(F32)).T
+    first = jnp.sum(product[:HD], axis=0, keepdims=True)
+    second = jnp.sum(product[HD:], axis=0, keepdims=True)
+    delta_s[:, base : base + half] = jnp.broadcast_to(first, (8, half))
+    delta_s[:, base + half : base + 2 * half] = jnp.broadcast_to(second, (8, half))
+
+
+def full_back_step(step, piece_rows, log_ref, put, q_s, k_s, v_s, do_s, delta_s, dq_s):
+    scale = 1.0 / math.sqrt(HD)
+    block = pl.ds(pl.multiple_of(step * piece_rows, piece_rows), piece_rows)
+    k = k_s[block, :]
+    v = v_s[block, :]
+    dk = dv = None
+    parts = []
+    for place in range(4):
+        rows = slice(place * piece_rows, (place + 1) * piece_rows)
+        dq, dk_part, dv_part = tile_grads(
+            q_s[rows, :], do_s[rows, :], k, v, log_ref[place, 0:1, :], delta_s[0:1, rows]
+        )
+        dk = dk_part if dk is None else dk + dk_part
+        dv = dv_part if dv is None else dv + dv_part
+        dq_s[:, rows] = jnp.where(step == 0, dq, dq_s[:, rows] + dq)
+    put(step, 1, fold(dk * scale).astype(BF16))
+    put(step, 2, fold(dv).astype(BF16))
+
+    @pl.when(step == 3)
+    def _():
+        for place in range(4):
+            rows = slice(place * piece_rows, (place + 1) * piece_rows)
+            put(place, 0, fold(dq_s[:, rows].T * scale).astype(BF16))
+
+
+def backward_first_kernel(
+    group_ref, a0, a1, a2, a3, b0, b1, b2, b3, d0, d1, d2, d3,
+    oa_ref, ob_ref, la_ref, lb_ref, grad_ref, q_s, k_s, v_s, do_s, delta_s, dq_s, log_s,
+):
+    step = pl.program_id(0)
+    group = group_ref[0]
+    piece_rows = 2 * a0.shape[1]
+    dos = (d0, d1, d2, d3)
+    for value, pieces, o_ref, l_ref in (
+        (1, (a0, a1, a2, a3), oa_ref, la_ref),
+        (0, (b0, b1, b2, b3), ob_ref, lb_ref),
+    ):
+
+        @pl.when((step == 0) & (group == value))
+        def _(pieces=pieces, o_ref=o_ref, l_ref=l_ref):
+            for place in range(4):
+                load_backward(
+                    pieces[place], dos[place][...], o_ref[place], place * piece_rows,
+                    q_s, k_s, v_s, do_s, delta_s,
+                )
+            log_s[...] = l_ref[...]
+
+    def put(place, part, value):
+        grad_ref[place, part] = value
+
+    full_back_step(step, piece_rows, log_s, put, q_s, k_s, v_s, do_s, delta_s, dq_s)
+
+
+def backward_second_kernel(
+    group_ref, pack_ref, dol_ref, ol_ref, ll_ref, b0, b1, b2, b3, d0, d1, d2, d3,
+    o_ref, l_ref, grad_ref, gradl_ref, q_s, k_s, v_s, do_s, delta_s, dq_s,
+):
+    step = pl.program_id(0)
+    group = group_ref[0]
+    piece_rows = 2 * b0.shape[1]
+    scale = 1.0 / math.sqrt(HD)
+
+    @pl.when(group == 0)
+    def _():
+        load_backward(
+            pack_ref.at[0], dol_ref[0], ol_ref[0], 0, q_s, k_s, v_s, do_s, delta_s
+        )
+        rows = slice(0, piece_rows)
+        dq, dk, dv = tile_grads(
+            q_s[rows, :], do_s[rows, :], k_s[rows, :], v_s[rows, :],
+            ll_ref[0, 0:1, :], delta_s[0:1, rows],
+        )
+        gradl_ref[step, 0] = fold(dq.T * scale).astype(BF16)
+        gradl_ref[step, 1] = fold(dk * scale).astype(BF16)
+        gradl_ref[step, 2] = fold(dv).astype(BF16)
+
+    @pl.when((group == 1) & (step < 4))
+    def _():
+        @pl.when(step == 0)
+        def _():
+            for place, (piece, do) in enumerate(((b0, d0), (b1, d1), (b2, d2), (b3, d3))):
+                load_backward(
+                    piece, do[...], o_ref[place], place * piece_rows,
+                    q_s, k_s, v_s, do_s, delta_s,
+                )
+
+        def put(place, part, value):
+            grad_ref[place, part] = value
+
+        full_back_step(step, piece_rows, l_ref, put, q_s, k_s, v_s, do_s, delta_s, dq_s)
+
+
+def backward_scratch(half):
+    return [pltpu.VMEM((8 * half, 2 * HD), BF16)] * 4 + [
+        pltpu.VMEM((8, 8 * half), F32),
+        pltpu.VMEM((2 * HD, 8 * half), F32),
+    ]
+
+
+def backward_first(group, a, b, do, oa, ob, la, lb):
+    _, half, lanes = a[0].shape
+    operands = (*a, *b, *do, oa, ob, la, lb)
+    out = (4, 3, half, lanes)
+    return pl.pallas_call(
+        backward_first_kernel,
+        grid_spec=pltpu.PrefetchScalarGridSpec(
+            num_scalar_prefetch=1,
+            grid=(4,),
+            in_specs=[whole(value.shape) for value in operands],
+            out_specs=whole(out),
+            scratch_shapes=backward_scratch(half) + [pltpu.VMEM(la.shape, F32)],
+        ),
+        out_shape=jax.ShapeDtypeStruct(out, BF16),
+        compiler_params=params("arbitrary"),
+        cost_estimate=pl.CostEstimate(
+            flops=60_000_000_000, bytes_accessed=8_000_000, transcendentals=0
+        ),
+        name="backward_first",
+    )(group, *operands)
+
+
+def backward_second(group, packs, dol, ol, ll, b, do, ob, lb):
+    heads, _, half, lanes = packs.shape
+    each = lambda shape: pl.BlockSpec(
+        (1,) + shape[1:], lambda i, g: (i * (1 - g[0]),) + (0,) * (len(shape) - 1)
+    )
+    operands = (*b, *do, ob, lb)
+    outs = [(4, 3, half, lanes), (heads, 3, half, lanes)]
+    return pl.pallas_call(
+        backward_second_kernel,
+        grid_spec=pltpu.PrefetchScalarGridSpec(
+            num_scalar_prefetch=1,
+            grid=(heads,),
+            in_specs=[each(packs.shape), each(dol.shape), each(ol.shape), each(ll.shape)]
+            + [whole(value.shape) for value in operands],
+            out_specs=[whole(shape) for shape in outs],
+            scratch_shapes=backward_scratch(half),
+        ),
+        out_shape=[jax.ShapeDtypeStruct(shape, BF16) for shape in outs],
+        compiler_params=params("arbitrary"),
+        cost_estimate=pl.CostEstimate(
+            flops=60_000_000_000, bytes_accessed=8_000_000, transcendentals=0
+        ),
+        name="backward_second",
+    )(group, packs, dol, ol, ll, *operands)
+
+
+def middle_kernel(
+    x_ref, cot_ref, att_ref, vec_ref, upb_ref, ow_ref, up_ref, down_ref,
+    out_ref, attlow_ref, hidden_ref, act_ref, gfeed_ref, gpre_ref, mgrad_ref, gbranch_ref,
+    gatt_ref, sums_ref, upsum_ref, att_s, slope_s,
+):
+    step = pl.program_id(0)
+    rows, width = x_ref.shape[1:]
+    both = 2 * rows
+    pairs = width // (2 * HD)
+    gate_one, gain, scale, shift = (vec_ref[i : i + 1, :] for i in range(4))
+    gate_two, down_bias = vec_ref[4:5, :], vec_ref[5:6, :]
+    for pair in range(pairs):
+        lanes = slice(pair * 2 * HD, (pair + 1) * 2 * HD)
+        top, bottom = exchange(
+            att_ref[2 * pair].astype(F32), att_ref[2 * pair + 1].astype(F32)
+        )
+        att_s[:rows, lanes] = top.astype(BF16)
+        att_s[rows:, lanes] = bottom.astype(BF16)
+    att = att_s[...]
+    attlow_ref[...] = att.reshape(2, rows, width)
+    branch = jnp.dot(att, ow_ref[...], preferred_element_type=F32)
+    middle = x_ref[...].reshape(both, width).astype(F32) + gate_one * branch
+    n, inverse = normalise(middle)
+    hidden = (n * gain * (1.0 + scale) + shift).astype(BF16)
+    hidden_ref[...] = hidden.reshape(2, rows, width)
+    units = up_ref.shape[1]
+    chunk = math.gcd(units, 768)
+    feed = None
+    for start in range(0, units, chunk):
+        cols = slice(start, start + chunk)
+        pre = jnp.dot(hidden, up_ref[:, cols], preferred_element_type=F32) + upb_ref[0:1, cols]
+        square = pre * pre
+        root = math.sqrt(2.0 / math.pi)
+        tanh = jnp.tanh(pre * (root + (root * 0.044715) * square))
+        half_up = 0.5 + 0.5 * tanh
+        act = (pre * half_up).astype(BF16)
+        slope_s[:, cols] = half_up + (0.5 * pre) * (1.0 - tanh * tanh) * (
+            root + (3.0 * root * 0.044715) * square
+        )
+        act_ref[:, :, cols] = act.reshape(2, rows, chunk)
+        part = jnp.dot(act, down_ref[cols, :], preferred_element_type=F32)
+        feed = part if feed is None else feed + part
+    feed = feed + down_bias
+    out_ref[...] = (middle + gate_two * feed).astype(BF16).reshape(2, rows, width)
+    cot = cot_ref[...].reshape(both, width).astype(F32)
+    gfeed = (gate_two * cot).astype(BF16)
+    gfeed_ref[...] = gfeed.reshape(2, rows, width)
+    ghidden = None
+    up_sums = []
+    for start in range(0, units, chunk):
+        cols = slice(start, start + chunk)
+        gact = lax.dot_general(gfeed, down_ref[cols, :], NT, preferred_element_type=F32)
+        gpre = (gact * slope_s[:, cols]).astype(BF16)
+        gpre_ref[:, :, cols] = gpre.reshape(2, rows, chunk)
+        up_sums.append(jnp.sum(gpre.astype(F32), axis=0, keepdims=True))
+        part = lax.dot_general(gpre, up_ref[:, cols], NT, preferred_element_type=F32)
+        ghidden = part if ghidden is None else ghidden + part
+    e = ghidden * ((1.0 + scale) * gain)
+    mgrad = cot + inverse * (
+        e - jnp.mean(e, axis=-1, keepdims=True) - n * jnp.mean(e * n, axis=-1, keepdims=True)
+    )
+    mgrad_ref[...] = mgrad.reshape(2, rows, width)
+    gbranch = (gate_one * mgrad).astype(BF16)
+    gbranch_ref[...] = gbranch.reshape(2, rows, width)
+    gatt = lax.dot_general(gbranch, ow_ref[...], NT, preferred_element_type=F32)
+    for pair in range(pairs):
+        value = gatt[:, pair * 2 * HD : (pair + 1) * 2 * HD]
+        even, odd = exchange(value[:rows], value[rows:])
+        gatt_ref[2 * pair] = even.astype(BF16)
+        gatt_ref[2 * pair + 1] = odd.astype(BF16)
+    add = lambda value: jnp.sum(value, axis=0, keepdims=True)
+
+    @pl.when(step == 0)
+    def _():
+        sums_ref[...] = jnp.zeros_like(sums_ref)
+        upsum_ref[...] = jnp.zeros_like(upsum_ref)
+
+    sums_ref[0:1, :] += add(ghidden)
+    sums_ref[1:2, :] += add(ghidden * n)
+    sums_ref[2:3, :] += add(cot * feed)
+    sums_ref[3:4, :] += add(gfeed.astype(F32))
+    sums_ref[4:5, :] += add(mgrad * branch)
+    for index, value in enumerate(up_sums):
+        upsum_ref[0:1, index * chunk : (index + 1) * chunk] += value
+
+
+def once(shape):
+    zeros = (0,) * len(shape)
+    return pl.BlockSpec(shape, lambda *_: zeros, pipeline_mode=pl.Buffered(1))
+
+
+def middle_pass(x2, cot2, att, vecs, up_bias, out_weight, up_full, down_full, rows=128):
+    half, width = x2.shape[1:]
+    heads = width // HD
+    units = up_full.shape[1]
+    tok = lambda last: pl.BlockSpec((2, rows, last), lambda i: (0, i, 0))
+    pack = pl.BlockSpec((heads, rows, 2 * HD), lambda i: (0, i, 0))
+    token = lambda last, kind: jax.ShapeDtypeStruct((2, half, last), kind)
+    return pl.pallas_call(
+        middle_kernel,
+        grid=(half // rows,),
+        in_specs=[
+            tok(width), tok(width), pack, whole(vecs.shape), whole(up_bias.shape),
+            once(out_weight.shape), once(up_full.shape), once(down_full.shape),
+        ],
+        out_specs=[
+            tok(width), tok(width), tok(width), tok(units), tok(width), tok(units), tok(width),
+            tok(width), pack, whole((8, width)), whole((8, units)),
+        ],
+        out_shape=[
+            token(width, BF16), token(width, BF16), token(width, BF16), token(units, BF16),
+            token(width, BF16), token(units, BF16), token(width, F32), token(width, BF16),
+            jax.ShapeDtypeStruct((heads, half, 2 * HD), BF16),
+            jax.ShapeDtypeStruct((8, width), F32),
+            jax.ShapeDtypeStruct((8, units), F32),
+        ],
+        scratch_shapes=[pltpu.VMEM((2 * rows, width), BF16), pltpu.VMEM((2 * rows, units), F32)],
+        compiler_params=params("arbitrary"),
+        name="middle_pass",
+    )(x2, cot2, att, vecs, up_bias, out_weight, up_full, down_full)
+
+
+def unrotate_kernel(pack_ref, cos_ref, sin_ref, mixed_ref):
+    rows = cos_ref.shape[1]
+    cosine = cos_ref[...].reshape(2 * rows, 2 * HD)
+    sine = -sin_ref[...].reshape(2 * rows, 2 * HD)
+    heads = pack_ref.shape[0]
+    width = heads * HD
+    for part in range(3):
+        for pair in range(heads // 2):
+            top, bottom = exchange(
+                pack_ref[2 * pair, part].astype(F32), pack_ref[2 * pair + 1, part].astype(F32)
+            )
+            value = jnp.concatenate([top, bottom], axis=0)
+            if part < 2:
+                value = turn(value, cosine, sine)
+            start = part * width + pair * 2 * HD
+            mixed_ref[:, :, start : start + 2 * HD] = value.astype(BF16).reshape(2, rows, 2 * HD)
+
+
+def unrotate(packs, cosine, sine, rows=128):
+    heads, _, half, lanes = packs.shape
+    tok = lambda last: pl.BlockSpec((2, rows, last), lambda i: (0, i, 0))
+    return pl.pallas_call(
+        unrotate_kernel,
+        grid=(half // rows,),
+        in_specs=[
+            pl.BlockSpec((heads, 3, rows, lanes), lambda i: (0, 0, i, 0)),
+            tok(lanes),
+            tok(lanes),
+        ],
+        out_specs=tok(3 * heads * HD),
+        out_shape=jax.ShapeDtypeStruct((2, half, 3 * heads * HD), BF16),
+        compiler_params=params("arbitrary"),
+        name="unrotate",
+    )(packs, cosine, sine)
+
+
+def input_kernel(mixed_ref, w_ref, x_ref, mgrad_ref, vec_ref, grad_ref, sums_ref):
+    step = pl.program_id(0)
+    rows, width = x_ref.shape[1:]
+    both = 2 * rows
+    gnormed = lax.dot_general(
+        mixed_ref[...].reshape(both, mixed_ref.shape[2]), w_ref[...], NT,
+        preferred_element_type=F32,
+    )
+    n, inverse = normalise(x_ref[...].reshape(both, width).astype(F32))
+    e = gnormed * ((1.0 + vec_ref[1:2, :]) * vec_ref[0:1, :])
+    grad = mgrad_ref[...].reshape(both, width) + inverse * (
+        e - jnp.mean(e, axis=-1, keepdims=True) - n * jnp.mean(e * n, axis=-1, keepdims=True)
+    )
+    grad_ref[...] = grad.reshape(2, rows, width)
+
+    @pl.when(step == 0)
+    def _():
+        sums_ref[...] = jnp.zeros_like(sums_ref)
+
+    sums_ref[0:1, :] += jnp.sum(gnormed, axis=0, keepdims=True)
+    sums_ref[1:2, :] += jnp.sum(gnormed * n, axis=0, keepdims=True)
+
+
+def input_pass(mixed, weight, x2, mgrad, vecs, rows=128):
+    half, width = x2.shape[1:]
+    tok = lambda last: pl.BlockSpec((2, rows, last), lambda i: (0, i, 0))
+    return pl.pallas_call(
+        input_kernel,
+        grid=(half // rows,),
+        in_specs=[
+            tok(mixed.shape[2]), once(weight.shape), tok(width), tok(width), whole(vecs.shape)
+        ],
+        out_specs=[tok(width), whole((8, width))],
+        out_shape=[
+            jax.ShapeDtypeStruct((2, half, width), F32),
+            jax.ShapeDtypeStruct((8, width), F32),
+        ],
+        compiler_params=params("arbitrary"),
+        cost_estimate=pl.CostEstimate(
+            flops=6_000_000_000, bytes_accessed=20_000_000, transcendentals=0
+        ),
+        name="input_pass",
+    )(mixed, weight, x2, mgrad, vecs)
+
+
+def along(value, steps):
+    pairs = [(place, (place + steps) % 4) for place in range(4)]
+    return lax.ppermute(value, "seq", pairs)
+
+
+def along_second(value, steps):
+    pairs = [(4 + place, 4 + (place + steps) % 4) for place in range(4)]
+    return lax.ppermute(value, ("grp", "seq"), pairs)
+
+
+def to_first(value):
+    return lax.ppermute(value, "grp", [(1, 0)])
+
+
+def to_second(value):
+    return lax.ppermute(value, "grp", [(0, 1)])
+
+
+def pick(stack, index):
+    return lax.dynamic_index_in_dim(stack, index, 0, keepdims=False)
+
+
+def four_shards(
+    tokens, step_index, time_table, ada_weight, ada_bias, first_gain, qkv_weight, out_weight,
+    second_gain, up_weight, up_bias, down_weight, down_bias, cotangent,
+):
+    place = lax.axis_index("seq")
+    group = lax.axis_index("grp")
+    mlp_count = lax.axis_size("mlp")
+    second = group == 1
+    token_rows, width = tokens.shape[1:]
+    half = token_rows // 2
+    heads = width // HD
+    slot = lambda steps: (place + steps) % 4
+    group_row = jnp.full((1,), group, jnp.int32)
+
+    up_full = lax.all_gather(up_weight, "mlp", axis=1, tiled=True)
+    down_full = lax.all_gather(down_weight, "mlp", axis=0, tiled=True)
+    up_bias_full = lax.all_gather(up_bias.astype(F32), "mlp", axis=0, tiled=True)
+
+    step_value = jnp.sum(jnp.where(jnp.arange(4, dtype=jnp.int32) == place, step_index[0], 0))
+    embedded = lax.dynamic_slice_in_dim(time_table, step_value, 1, 0)[0].astype(F32)
+    condition, silu_back = jax.vjp(jax.nn.silu, embedded)
+    cond_low = condition.astype(BF16)
+    modulation = jnp.dot(cond_low[None, :], ada_weight, preferred_element_type=F32)[
+        0
+    ] + ada_bias.astype(F32)
+    shift_one, scale_one, gate_one, shift_two, scale_two, gate_two = jnp.split(modulation, 6)
+
+    positions = jnp.arange(token_rows, dtype=jnp.int32) + jnp.where(second, place * token_rows, 0)
+    frequency = jnp.exp(jnp.arange(HD // 2, dtype=F32) * (-2.0 * math.log(10000.0) / HD))
+    angles = positions.astype(F32)[:, None] * frequency[None, :]
+    cosine, sine = jnp.cos(angles), jnp.sin(angles)
+    cosine = jnp.concatenate([cosine] * 4, axis=1).reshape(2, half, 2 * HD)
+    sine = jnp.concatenate([-sine, sine] * 2, axis=1).reshape(2, half, 2 * HD)
+
+    x2 = tokens.reshape(2, half, width)
+    blank = jnp.zeros((width,), F32)
+    gain_one = first_gain.astype(F32)
+    gain_two = second_gain.astype(F32)
+    vec_one = jnp.stack([gain_one, scale_one, shift_one] + [blank] * 5)
+    vec_two = jnp.stack(
+        [gate_one, gain_two, scale_two, shift_two, gate_two, down_bias.astype(F32), blank, blank]
+    )
+    normed, packs = project(x2, vec_one, qkv_weight, cosine, sine)
+
+    crossed = to_first(packs[8:])
+    a = [pick(packs, 2 * slot(0))] + [
+        along_second(pick(packs, 2 * slot(s)), s) for s in (1, 2, 3)
+    ]
+    b_from = jnp.where(second, packs[1:8:2], crossed)
+    b = [pick(b_from, slot(0))] + [along(pick(b_from, slot(s)), s) for s in (1, 2, 3)]
+    oa, la, o_own, l_own = forward_first(group_row, packs, a)
+    ob, lb = forward_second(b)
+
+    def home(pieces):
+        parts = [pieces[0]] + [along(pieces[s], -s) for s in (1, 2, 3)]
+        return jnp.roll(jnp.stack(parts), place, axis=0)
+
+    def join(from_a, from_b, from_first, own):
+        interleaved = jnp.stack([from_a, from_b], axis=1).reshape((8,) + from_a.shape[1:])
+        return jnp.where(second, jnp.concatenate([interleaved, from_first]), own)
+
+    a_home = home(oa)
+    b_home = home(ob)
+    att = join(a_home, b_home, to_second(b_home), o_own)
+
+    up_bias_row = jnp.broadcast_to(up_bias_full[None, :], (8, up_bias_full.shape[0]))
+    (
+        output, att_low, hidden, act, grad_feed, grad_pre, middle_grad, grad_branch, grad_att,
+        middle_sums, up_sums,
+    ) = middle_pass(
+        x2, cotangent.reshape(2, half, width), att, vec_two, up_bias_row, out_weight, up_full,
+        down_full,
+    )
+    flat = lambda value: value.reshape(token_rows, value.shape[2])
+    across = lambda left, right: lax.dot_general(
+        flat(left), flat(right), TN, preferred_element_type=F32
+    )
+
+    crossed_grad = to_first(grad_att[8:])
+    f_from = jnp.where(second, grad_att[0:8:2], crossed_grad)
+    do_f = [pick(f_from, slot(0))] + [along(pick(f_from, slot(s)), s) for s in (1, 2, 3)]
+    do_b = [pick(grad_att, 2 * slot(0) % 8 + 1)] + [
+        along_second(pick(grad_att, 2 * slot(s) + 1), s) for s in (1, 2, 3)
+    ]
+    out_grad = across(att_low, grad_branch)
+    up_grad = across(hidden, grad_pre)
+    down_grad = across(act, grad_feed)
+    grad_f = backward_first(group_row, a, b, do_f, oa, ob, la, lb)
+    grad_s, grad_own = backward_second(
+        group_row, packs, grad_att, o_own, l_own, b, do_b, ob, lb
+    )
+    f_home = home(grad_f)
+    s_home = home(grad_s)
+    grads = join(f_home, s_home, to_second(f_home), grad_own)
+    mixed_grad = unrotate(grads, cosine, sine)
+    qkv_grad = across(normed, mixed_grad)
+    input_grad, input_sums = input_pass(mixed_grad, qkv_weight, x2, middle_grad, vec_one)
+
+    shift_one_grad = input_sums[0]
+    first_gain_grad = (1.0 + scale_one) * input_sums[1]
+    scale_one_grad = gain_one * input_sums[1]
+    shift_two_grad = middle_sums[0]
+    second_gain_grad = (1.0 + scale_two) * middle_sums[1]
+    scale_two_grad = gain_two * middle_sums[1]
+    mod_grad = jnp.concatenate(
+        [
+            shift_one_grad, scale_one_grad, middle_sums[4], shift_two_grad, scale_two_grad,
+            middle_sums[2],
+        ]
+    )
+    cond_grad = jnp.dot(ada_weight.astype(F32), mod_grad, precision=highest)
+    table_row = silu_back(cond_grad)[0]
+    small = jnp.concatenate(
+        [
+            mod_grad, first_gain_grad, second_gain_grad, up_sums[0], middle_sums[3],
+            table_row, condition,
+        ]
+    )
+    step_row = jnp.full((1,), step_value, jnp.int32)
+    small_all = lax.all_gather(small, ("grp", "seq", "mlp"), axis=0)
+    steps_all = lax.all_gather(step_row, ("grp", "seq", "mlp"), axis=0, tiled=True)
+    rank = place * mlp_count + lax.axis_index("mlp")
+    ranks = 4 * mlp_count
+
+    def share(start, size):
+        each = size // ranks
+        return lax.dynamic_slice_in_dim(small_all, start + rank * each, each, 1)
+
+    mod_size = 6 * width
+    units = up_full.shape[1]
+    mod_share = share(0, mod_size)
+    start = mod_size
+    first_share = jnp.sum(share(start, width), axis=0)
+    start += width
+    second_share = jnp.sum(share(start, width), axis=0)
+    start += width
+    up_bias_share = jnp.sum(share(start, units), axis=0)
+    start += units
+    down_bias_share = jnp.sum(share(start, width), axis=0)
+    start += width
+    cond_size = condition.shape[0]
+    rows_all = small_all[:, start : start + cond_size]
+    cond_all = small_all[:, start + cond_size :].astype(BF16).astype(F32)
+    ada_share = lax.dot_general(cond_all, mod_share, TN, precision=highest)
+    table_each = time_table.shape[0] // ranks
+    own_rows = rank * table_each + jnp.arange(table_each, dtype=jnp.int32)
+    chosen = (own_rows[:, None] == steps_all[None, :]).astype(F32)
+    table_share = jnp.dot(chosen, rows_all, precision=highest)
+
+    both_axes = ("seq", "mlp")
+    big = (
+        lax.psum_scatter(qkv_grad, both_axes, scatter_dimension=0, tiled=True),
+        lax.psum_scatter(out_grad, both_axes, scatter_dimension=0, tiled=True),
+        lax.psum_scatter(
+            lax.psum_scatter(up_grad, "mlp", scatter_dimension=1, tiled=True),
+            "seq", scatter_dimension=0, tiled=True,
+        ),
+        lax.psum_scatter(
+            lax.psum_scatter(down_grad, "mlp", scatter_dimension=0, tiled=True),
+            "seq", scatter_dimension=1, tiled=True,
+        ),
+    )
+    qkv_total, out_total, up_total, down_total = lax.psum(big, "grp")
+    return (
+        output.reshape(1, token_rows, width),
+        input_grad.reshape(1, token_rows, width),
+        table_share,
+        ada_share,
+        jnp.sum(mod_share, axis=0),
+        first_share,
+        qkv_total,
+        out_total,
+        second_share,
+        up_total,
+        up_bias_share,
+        down_total,
+        down_bias_share,
+    )
+
+
 def solution(mesh):
     in_specs = (
         P(("grp", "mlp"), "seq", None),
@@ -360,4 +1162,5 @@
         P("mlp", "seq"),
         P(("seq", "mlp")),
     )
-    return jax.shard_map(shards, mesh=mesh, in_specs=in_specs, out_specs=out_specs, check_vma=False)
+    body = four_shards if mesh.shape["seq"] == 4 and mesh.shape["grp"] == 2 else shards
+    return jax.shard_map(body, mesh=mesh, in_specs=in_specs, out_specs=out_specs, check_vma=False)

time: 2190 us -> 830 us (0.38)
  matrix products: 714 us -> 36 us
  waiting for transfers between devices: 1020 us -> 388 us
  Pallas kernels: 0 us -> 206 us
  other arithmetic: 178 us -> 23.9 us
  local copies, waits for them, and re-layouts: 133 us -> 33.9 us
  starting transfers between devices: 19.7 us -> 73.6 us
  loops' own time: 31.9 us -> 0 us
  blocking collectives: 71.3 us -> 44.9 us
    dot_general x51 -> x8, matrix products: 714 us -> 36 us  [the longest x4 32.2 us: four_shards(): lax.dot_general(flat(left), flat(right), TN, preferred_element_type=F32)]
    ppermute x16 -> x28, waiting for transfers between devices: 460 us -> 108 us  [the longest x18 64.1 us: along(): return lax.ppermute(value, 'seq', pairs)]
    all_gather x4 -> x3, waiting for transfers between devices: 285 us -> 16.8 us  [the longest x1 16.8 us: four_shards(): small_all = lax.all_gather(small, ('grp', 'seq', 'mlp'), axis=0)]
    pallas_call x0 -> x8, Pallas kernels: none -> 206 us  [the longest x1 45.8 us: backward_first(): pl.pallas_call(backward_first_kernel, grid_spec=pltpu.PrefetchScalarGridS...]
    reduce_sum x19 -> x4, other arithmetic: 129 us -> 3.25 us  [the longest x1 1.29 us: four_shards(): jnp.sum(jnp.where(jnp.arange(4, dtype=jnp.int32) == place, step_index[0],...]
    ppermute x16 -> x28, starting transfers between devices: 18.8 us -> 73.2 us  [the longest x18 43.7 us: along(): return lax.ppermute(value, 'seq', pairs)]
    dynamic_slice x24 -> x0, local copies, waits for them, and re-layouts: 44.6 us -> none  [the longest x16 35.1 us: one_block(): lax.dynamic_slice_in_dim(value_piece, offset, sub_rows, 0)]
    reduce_scatter x8 -> x5, waiting for transfers between devices: 239 us -> 205 us  [the longest x1 90 us: four_shards(): lax.psum_scatter(qkv_grad, both_axes, scatter_dimension=0, tiled=True)]
  transfers between devices with their start and end apart: 29 -> 38, of which waited for: 16 -> 13; matrix products, arithmetic and copies ran while one was open for 27% -> 9% of each run, Pallas kernels for 0% -> 20%
where the time goes in v1:
time: 830 us; the launch traced here: 823 us
  waiting for transfers between devices  388 us (47%)
  Pallas kernels  206 us (25%)
  starting transfers between devices  73.6 us (9%)
  blocking collectives  44.9 us (5%)
  matrix products  36 us (4%)
  local copies, waits for them, and re-layouts  33.9 us (4%)
  other arithmetic  23.9 us (3%)
  between operations  17.2 us (2%)
    reduce_scatter x1, waiting for transfers between devices, four_shards(): lax.psum_scatter(qkv_grad, both_axes, scatter_dimension=0, tiled=True)  90 us
    reduce_scatter x1, waiting for transfers between devices, four_shards(): lax.psum_scatter(down_grad, 'mlp', scatter_dimension=0, tiled=True)  65 us
    ppermute x18, waiting for transfers between devices, along(): return lax.ppermute(value, 'seq', pairs)  64.1 us
    psum x1, waiting for transfers between devices, four_shards(): qkv_total, out_total, up_total, down_total = lax.psum(big, 'grp')  56.6 us
    reduce_scatter x1, waiting for transfers between devices, four_shards(): lax.psum_scatter(lax.psum_scatter(up_grad, 'mlp', scatter_dimension=1, ti...  49.9 us
    pallas_call x1, Pallas kernels, backward_first(): pl.pallas_call(backward_first_kernel, grid_spec=pltpu.PrefetchScalarGridS...  45.8 us
    ppermute x18, starting transfers between devices, along(): return lax.ppermute(value, 'seq', pairs)  43.7 us
    ppermute x2, waiting for transfers between devices, to_first(): return lax.ppermute(value, 'grp', [(1, 0)])  41.7 us
  transfers between devices with their start and end apart: 38, of which 13 were waited for; matrix products, arithmetic and copies ran while one was open for 9% of the time, Pallas kernels for 20%

profile of v1, /device:TPU:0, one launch (start us, length us, event | category | flops | bytes accessed | tf_op | source)
XLA Modules:
  0.0 822.9 jit_solution(13291922090875615954)
XLA Ops:
  13.6 1.9 fusion.30
  15.5 1.8 pad_maximum_fusion.2
  17.3 11.5 %project.1 = (bf16[2,512,768]{2,1,0:T(8,128)(2,1)}, bf16[12,3,512,128]{3,2,1,0:T(8,128)(2,1)}) custom-call(bf16[2,512,768]{2,1,0:T(8,128)(2,1)} %bitcast.135, f32[8,768]{1,0:T(8,128)} %stack.112.vec_ref, bf16[768,2304]{1,0:T(8,128)(2,1)} %w_ref.3, f32[2,512,128]{2,1,0:T(8,128)} %get-tuple-element.167.cos_ref, f32[2,512,128]{2,1,0:T(8,128)} %get-tuple-element.168.sin_ref), custom_call_target="tpu_custom_call" | custom-call | tf_op jit(solution)/shard_map/project/pallas_call | solution.py:418
  28.8 2.7 slice.98
  32.8 2.4 dynamic-slice_bitcast_fusion.4
  35.2 1.4 collective-permute-start
  36.6 1.4 collective-permute-start.1
  38.1 1.4 collective-permute-start.2
  39.6 30.8 %collective-permute-done.6 = bf16[4,3,512,128]{3,2,1,0:T(8,128)(2,1)S(1)} collective-permute-done((bf16[4,3,512,128]{3,2,1,0:T(8,128)(2,1)}, bf16[4,3,512,128]{3,2,1,0:T(8,128)(2,1)S(1)}, u32[]{:S(2)}, u32[]{:S(2)}) %collective-permute-start.6) | collective-permute-done | bytes 1572896 | tf_op jit(solution)/shard_map/ppermute | solution.py:942
  70.4 1.6 slice_select_fusion
  72.9 2.4 collective-permute-start.7
  75.2 2.6 collective-permute-start.8
  77.9 1.8 collective-permute-start.9
  79.6 25.0 %forward_first.1 = (bf16[4,512,128]{2,1,0:T(8,128)(2,1)}, f32[4,8,1024]{2,1,0:T(8,128)}, bf16[12,512,128]{2,1,0:T(8,128)(2,1)}, f32[12,8,1024]{2,1,0:T(8,128)}) custom-call(s32[1]{0:T(128)} %bitcast.2.group_ref, bf16[12,3,512,128]{3,2,1,0:T(8,128)(2,1)} %get-tuple-element.38.pack_ref, bf16[3,512,128]{2,1,0:T(8,128)(2,1)} %get-tuple-element.117.p0.a0, ...), custom_call_target="tpu_custom_call" | custom-call | flops 40000000000 | bytes 8000000 | tf_op jit(solution)/shard_map/forward_first/pallas_call | solution.py:520
  105.5 25.1 %forward_second.1 = (bf16[4,512,128]{2,1,0:T(8,128)(2,1)}, f32[4,8,1024]{2,1,0:T(8,128)}) custom-call(bf16[3,512,128]{2,1,0:T(8,128)(2,1)} %get-tuple-element.133.p0.b0, bf16[3,512,128]{2,1,0:T(8,128)(2,1)} %copy-done.24, bf16[3,512,128]{2,1,0:T(8,128)(2,1)} %copy-done.25, bf16[3,512,128]{2,1,0:T(8,128)(2,1)} %collective-permute-done.9.p3.b3), custom_call_target="tpu_custom_call" | custom-call | flops 40000000000 | bytes 8000000 | tf_op jit(solution)/shard_map/forward_second/pallas_call | solution.py:542
  131.8 7.8 collective-permute-start.10
  141.0 3.2 collective-permute-start.3
  145.3 4.6 collective-permute-start.5
  149.9 8.0 collective-permute-done.11
  158.5 14.3 %collective-permute-start.13 = (bf16[4,512,128]{2,1,0:T(8,128)(2,1)S(1)}, bf16[4,512,128]{2,1,0:T(8,128)(2,1)S(1)}, u32[]{:S(2)}, u32[]{:S(2)}) collective-permute-start(bf16[4,512,128]{2,1,0:T(8,128)(2,1)S(1)} %fusion.18), channel_id=1, source_target_pairs={{0,16},{1,17},{2,18},{3,19},{4,20},{5,21},{6,22},{7,23},{8,24},{9,... | collective-permute-start | bytes 1572872 | tf_op jit(solution)/shard_map/ppermute | solution.py:946
  173.6 5.1 all-gather.1
  180.2 2.0 collective-permute-done.13
  182.2 1.4 maximum_select_fusion.1.att_ref
  184.3 38.6 %middle_pass.1 = (bf16[2,512,768]{2,1,0:T(8,128)(2,1)}, bf16[2,512,768]{2,1,0:T(8,128)(2,1)}, bf16[2,512,768]{2,1,0:T(8,128)(2,1)}, bf16[2,512,3072]{2,1,0:T(8,1...) custom-call(bf16[2,512,768]{2,1,0:T(8,128)(2,1)} %bitcast.136, ...), custom_call_target="tpu_custom_call" | custom-call | tf_op jit(solution)/shard_map/middle_pass/pallas_call | solution.py:826
  222.9 9.9 %convolution_bitcast_fusion = f32[3072,768]{1,0:T(8,128)} fusion(bf16[2,512,3072]{2,1,0:T(8,128)(2,1)} %get-tuple-element.59, bf16[2,512,768]{2,1,0:T(8,128)(2,1)} %get-tuple-element.60), kind=kOutput, calls=%fused_computation | convolution fusion | flops 4831838208 | bytes 17301504 | tf_op jit(solution)/shard_map/dot_general | solution.py:1027
  232.9 1.3 copy-done.23
  234.2 11.2 %convolution_bitcast_fusion.1 = f32[768,3072]{1,0:T(8,128)} fusion(bf16[2,512,768]{2,1,0:T(8,128)(2,1)S(1)} %copy-done.23, bf16[2,512,3072]{2,1,0:T(8,128)(2,1)} %get-tuple-element.58), kind=kOutput, calls=%fused_computation.1 | convolution fusion | flops 4831838208 | bytes 17301504 | tf_op jit(solution)/shard_map/dot_general | solution.py:1027
  245.5 65.0 %reduce-scatter.17.cloned.1.call-done = f32[768,768]{1,0:T(8,128)} async-done(((f32[3072,768]{1,0:T(8,128)}), f32[768,768]{1,0:T(8,128)}) %reduce-scatter.17.cloned.1.call-update) | async-done | bytes 2359312 | tf_op jit(solution)/shard_map/reduce_scatter | solution.py:1111
  310.5 3.0 copy.46
  313.6 1.3 copy-done.3
  317.9 1.4 collective-permute-start.21
  319.3 1.3 collective-permute-start.22
  320.6 10.9 %collective-permute-done.14 = bf16[4,512,128]{2,1,0:T(8,128)(2,1)S(1)} collective-permute-done((bf16[4,512,128]{2,1,0:T(8,128)(2,1)}, bf16[4,512,128]{2,1,0:T(8,128)(2,1)S(1)}, u32[]{:S(2)}, u32[]{:S(2)}) %collective-permute-start.14) | collective-permute-done | bytes 524320 | tf_op jit(solution)/shard_map/ppermute | solution.py:942
  332.3 1.5 collective-permute-start.15
  333.8 2.4 collective-permute-start.16
  336.2 1.4 collective-permute-start.17
  337.6 2.9 convolution_bitcast_fusion.3
  340.6 1.3 collective-permute-start.23
  341.9 2.2 collective-permute-done.16.d2
  344.8 45.8 %backward_first.1 = bf16[4,3,512,128]{3,2,1,0:T(8,128)(2,1)} custom-call(s32[1]{0:T(128)} %bitcast.2.group_ref, bf16[3,512,128]{2,1,0:T(8,128)(2,1)} %get-tuple-element.117.p0.a0, bf16[3,512,128]{2,1,0:T(8,128)(2,1)} %collective-permute-done.p1.a1, bf16[3,512,128]{2,1,0:T(8,128)(2,1)} %collective-permute-done.1.p2.a2, ...), custom_call_target="tpu_custom_call" | custom-call | flops 60000002048 | bytes 8000000 | tf_op jit(solution)/shard_map/backward_first/pallas_call | solution.py:684
  390.6 1.5 slice_bitcast_fusion
  392.1 4.4 collective-permute-start.18
  397.6 41.0 %backward_second.1 = (bf16[4,3,512,128]{3,2,1,0:T(8,128)(2,1)}, bf16[12,3,512,128]{3,2,1,0:T(8,128)(2,1)}) custom-call(s32[1]{0:T(128)} %bitcast.2.group_ref, bf16[12,3,512,128]{3,2,1,0:T(8,128)(2,1)} %get-tuple-element.38.pack_ref, bf16[12,512,128]{2,1,0:T(8,128)(2,1)} %get-tuple-element.43.dol_ref, bf16[12,512,128]{2,1,0:T(8,128)(2,1)} %get-tuple-element.41.ol_ref, ...), custom_call_target="tpu_custom_call" | custom-call | flops 60000002048 | bytes 8000000 | tf_op jit(solution)/shard_map/backward_second/pallas_call | solution.py:709
  438.6 24.3 %collective-permute-done.19 = bf16[3,512,128]{2,1,0:T(8,128)(2,1)S(1)} collective-permute-done((bf16[3,512,128]{2,1,0:T(8,128)(2,1)S(1)}, bf16[3,512,128]{2,1,0:T(8,128)(2,1)S(1)}, u32[]{:S(2)}, u32[]{:S(2)}) %collective-permute-start.19) | collective-permute-done | bytes 393248 | tf_op jit(solution)/shard_map/ppermute | solution.py:933
  463.7 1.9 fusion.11
  465.6 4.3 collective-permute-start.27
  470.1 6.8 collective-permute-start.25
  476.9 1.9 collective-permute-start.26
  478.9 3.1 collective-permute-done.24
  482.0 26.4 %collective-permute-done.25 = bf16[3,512,128]{2,1,0:T(8,128)(2,1)S(1)} collective-permute-done((bf16[3,512,128]{2,1,0:T(8,128)(2,1)S(1)}, bf16[3,512,128]{2,1,0:T(8,128)(2,1)S(1)}, u32[]{:S(2)}, u32[]{:S(2)}) %collective-permute-start.25) | collective-permute-done | bytes 393248 | tf_op jit(solution)/shard_map/ppermute | solution.py:933
  508.4 1.9 fusion.4
  510.4 1.9 fusion.65
  512.6 2.8 maximum_select_fusion.pack_ref
  515.5 8.7 %unrotate.1.mixed_ref = bf16[2,512,2304]{2,1,0:T(8,128)(2,1)} custom-call(bf16[12,3,512,128]{3,2,1,0:T(8,128)(2,1)} %maximum_select_fusion.pack_ref, f32[2,512,128]{2,1,0:T(8,128)} %get-tuple-element.167.cos_ref, f32[2,512,128]{2,1,0:T(8,128)} %get-tuple-element.168.sin_ref), custom_call_target="tpu_custom_call" | custom-call | tf_op jit(solution)/shard_map/unrotate/pallas_call | solution.py:871
  524.2 8.2 convolution_bitcast_fusion.2
  534.2 10.3 %input_pass.1 = (f32[2,512,768]{2,1,0:T(8,128)}, f32[8,768]{1,0:T(8,128)}) custom-call(bf16[2,512,2304]{2,1,0:T(8,128)(2,1)} %unrotate.1.mixed_ref, bf16[768,2304]{1,0:T(8,128)(2,1)} %w_ref.3, bf16[2,512,768]{2,1,0:T(8,128)(2,1)} %bitcast.137, f32[2,512,768]{2,1,0:T(8,128)} %get-tuple-element.49.mgrad_ref, f32[8,768]{1,0:T(8,128)} %stack.112.vec_ref), custom_call_target="tpu_custom_call" | custom-call | flops 6000000000 | bytes 20000000 | tf_op jit(solution)/shard_map/input_pass/pallas_call | solution.py:912
  550.0 2.2 copy.47
  552.3 90.0 %reduce-scatter.9.cloned.1.call-done = f32[48,2304]{1,0:T(8,128)} async-done(((f32[768,2304]{1,0:T(8,128)}), f32[48,2304]{1,0:T(8,128)}) %reduce-scatter.9.cloned.1.call-update) | async-done | bytes 442384 | tf_op jit(solution)/shard_map/reduce_scatter | solution.py:1104
  642.3 49.9 %reduce-scatter.15.cloned.1.call-done = f32[192,768]{1,0:T(8,128)} async-done(((f32[768,768]{1,0:T(8,128)}), f32[192,768]{1,0:T(8,128)}) %reduce-scatter.15.cloned.1.call-update) | async-done | bytes 589840 | tf_op jit(solution)/shard_map/reduce_scatter | solution.py:1106
  693.0 39.7 %all-reduce = s32[32]{0:T(128)S(1)} all-reduce(s32[32]{0:T(128)S(1)} %dynamic-update-slice), channel_id=1, replica_groups=mesh['grp'=2,'seq'=4,'mlp'=4] {'grp','seq','mlp'}, use_global_device_ids=true, to_apply=%add | all-reduce | flops 32 | bytes 256
  732.7 16.8 %all-gather.10.cloned.1.call-done = f32[327680]{0:T(1024)} async-done(((f32[10240]{0:T(1024)}), f32[327680]{0:T(1024)}) %all-gather.10.cloned.1.call-update) | async-done | bytes 1310736 | tf_op jit(solution)/shard_map/all_gather | solution.py:1072
  749.4 1.5 reshape.174
  754.8 56.6 %all-reduce.4.cloned.1.call-done = (f32[48,2304]{1,0:T(8,128)}, f32[48,768]{1,0:T(8,128)}, f32[192,768]{1,0:T(8,128)}, f32[768,192]{1,0:T(8,128)}) async-done(((f32[48,2304]{1,0:T(8,128)}, f32[48,768]{1,0:T(8,128)}, f32[192,768]{1,0:T(8,128)}, f32[768,192]{1,0:T(8,128)}), (f32[48,2304]{1,0:T(8,128)}, f32[48,768]{1,0:T(8,128)}, f32[192,768]{1,0:T(8,128)}, f32[768,192]{1,0:T(8,128)})) %all-reduce.4.cloned.1.call-update) | async-done | bytes 1769488 | tf_op jit(solution)/shard_map/psum | solution.py:1115
  811.3 2.3 copy.41
  (179 shorter events, 35.3 us)
Async XLA Ops:
  7.2 4.1 copy-start
  7.2 5.0 copy-start.12
  7.2 5.7 copy-start.14
  7.2 176.4 %all-gather.6.cloned.1.call-start = ((), (), s32[]{:S(2)}) async-start(), calls=%async_computation.6 | async-start | bytes 5898240 | tf_op jit(solution)/shard_map/all_gather | solution.py:967
  8.0 175.7 %all-gather.8.cloned.1.call-start = ((), (), s32[]{:S(2)}) async-start(), calls=%async_computation.7 | async-start | bytes 5898240 | tf_op jit(solution)/shard_map/all_gather | solution.py:968
  31.5 38.9 %collective-permute-start.6 = (bf16[4,3,512,128]{3,2,1,0:T(8,128)(2,1)}, bf16[4,3,512,128]{3,2,1,0:T(8,128)(2,1)S(1)}, u32[]{:S(2)}, u32[]{:S(2)}) collective-permute-start(bf16[4,3,512,128]{3,2,1,0:T(8,128)(2,1)} %slice.98), channel_id=1, source_target_pairs={{16,0},{17,1},{18,2},{19,3},{20,4},{21,5},{22,6},{23,7},{24,8},{25... | collective-permute-start | bytes 4718600 | tf_op jit(solution)/shard_map/ppermute | solution.py:942
  35.2 42.6 %collective-permute-start = (bf16[3,512,128]{2,1,0:T(8,128)(2,1)}, bf16[3,512,128]{2,1,0:T(8,128)(2,1)}, u32[]{:S(2)}, u32[]{:S(2)}) collective-permute-start(bf16[3,512,128]{2,1,0:T(8,128)(2,1)} %get-tuple-element.116), channel_id=1, source_target_pairs={{16,20},{20,24},{24,28},{28,16},{17,21},{21,25},{25,29},{29,17},{1... | collective-permute-start | bytes 1179656 | tf_op jit(solution)/shard_map/ppermute | solution.py:938
  36.6 43.0 %collective-permute-start.1 = (bf16[3,512,128]{2,1,0:T(8,128)(2,1)S(1)}, bf16[3,512,128]{2,1,0:T(8,128)(2,1)}, u32[]{:S(2)}, u32[]{:S(2)}) collective-permute-start(bf16[3,512,128]{2,1,0:T(8,128)(2,1)S(1)} %get-tuple-element.115), channel_id=1, source_target_pairs={{16,24},{20,28},{24,16},{28,20},{17,25},{21,29},{25,17},{29,21},{1... | collective-permute-start | bytes 1179656 | tf_op jit(solution)/shard_map/ppermute | solution.py:938
  38.1 41.6 %collective-permute-start.2 = (bf16[3,512,128]{2,1,0:T(8,128)(2,1)S(1)}, bf16[3,512,128]{2,1,0:T(8,128)(2,1)}, u32[]{:S(2)}, u32[]{:S(2)}) collective-permute-start(bf16[3,512,128]{2,1,0:T(8,128)(2,1)S(1)} %get-tuple-element.114), channel_id=1, source_target_pairs={{16,28},{20,16},{24,20},{28,24},{17,29},{21,17},{25,21},{29,25},{1... | collective-permute-start | bytes 1179656 | tf_op jit(solution)/shard_map/ppermute | solution.py:938
  39.5 271.0 %reduce-scatter.17.cloned.1.call-start = ((), (), s32[]{:S(2)}) async-start(), calls=%async_computation.12 | async-start | bytes 11796480 | tf_op jit(solution)/shard_map/reduce_scatter | solution.py:1111
  72.9 31.7 %collective-permute-start.7 = (bf16[3,512,128]{2,1,0:T(8,128)(2,1)S(1)}, bf16[3,512,128]{2,1,0:T(8,128)(2,1)S(1)}, u32[]{:S(2)}, u32[]{:S(2)}) collective-permute-start(bf16[3,512,128]{2,1,0:T(8,128)(2,1)S(1)} %get-tuple-element.132), channel_id=1, source_target_pairs={{0,4},{4,8},{8,12},{12,0},{1,5},{5,9},{9,13},{13,1},{2,6},{6,10},{... | collective-permute-start | bytes 1179656 | tf_op jit(solution)/shard_map/ppermute | solution.py:933
  75.2 29.4 %collective-permute-start.8 = (bf16[3,512,128]{2,1,0:T(8,128)(2,1)S(1)}, bf16[3,512,128]{2,1,0:T(8,128)(2,1)S(1)}, u32[]{:S(2)}, u32[]{:S(2)}) collective-permute-start(bf16[3,512,128]{2,1,0:T(8,128)(2,1)S(1)} %get-tuple-element.131), channel_id=1, source_target_pairs={{0,8},{4,12},{8,0},{12,4},{1,9},{5,13},{9,1},{13,5},{2,10},{6,14},... | collective-permute-start | bytes 1179656 | tf_op jit(solution)/shard_map/ppermute | solution.py:933
  77.9 26.8 %collective-permute-start.9 = (bf16[3,512,128]{2,1,0:T(8,128)(2,1)S(1)}, bf16[3,512,128]{2,1,0:T(8,128)(2,1)}, u32[]{:S(2)}, u32[]{:S(2)}) collective-permute-start(bf16[3,512,128]{2,1,0:T(8,128)(2,1)S(1)} %get-tuple-element.130), channel_id=1, source_target_pairs={{0,12},{4,0},{8,4},{12,8},{1,13},{5,1},{9,5},{13,9},{2,14},{6,2},{... | collective-permute-start | bytes 1179656 | tf_op jit(solution)/shard_map/ppermute | solution.py:933
  104.6 0.8 copy-start.24
  104.6 0.9 copy-start.25
  105.5 34.8 %copy-start.7 = (bf16[4,512,128]{2,1,0:T(8,128)(2,1)S(1)}, bf16[4,512,128]{2,1,0:T(8,128)(2,1)}, u32[]{:S(2)}) copy-start(bf16[4,512,128]{2,1,0:T(8,128)(2,1)} %get-tuple-element.39.oa_ref) | copy-start | bytes 1572868
  130.6 42.3 %copy-start.18 = (bf16[768]{0:T(1024)(128)(2,1)S(1)}, bf16[768]{0:T(1024)(128)(2,1)}, u32[]{:S(2)}) copy-start(bf16[768]{0:T(1024)(128)(2,1)} %param.30) | copy-start | bytes 4612
  130.6 42.3 %copy-start.16 = (bf16[768]{0:T(1024)(128)(2,1)S(1)}, bf16[768]{0:T(1024)(128)(2,1)}, u32[]{:S(2)}) copy-start(bf16[768]{0:T(1024)(128)(2,1)} %param.26) | copy-start | bytes 4612
  130.6 42.3 %copy-start.19 = (bf16[768]{0:T(1024)(128)(2,1)S(1)}, bf16[768]{0:T(1024)(128)(2,1)}, u32[]{:S(2)}) copy-start(bf16[768]{0:T(1024)(128)(2,1)} %param.28) | copy-start | bytes 4612
  131.8 13.5 %collective-permute-start.10 = (bf16[512,128]{1,0:T(8,128)(2,1)S(1)}, bf16[512,128]{1,0:T(8,128)(2,1)S(1)}, u32[]{:S(2)}, u32[]{:S(2)}) collective-permute-start(bf16[512,128]{1,0:T(8,128)(2,1)S(1)} %get-tuple-element.144), channel_id=1, source_target_pairs={{0,12},{4,0},{8,4},{12,8},{1,13},{5,1},{9,5},{13,9},{2,14},{6,2},{... | collective-permute-start | bytes 393224 | tf_op jit(solution)/shard_map/ppermute | solution.py:933
  139.6 18.3 %collective-permute-start.11 = (bf16[512,128]{1,0:T(8,128)(2,1)S(1)}, bf16[512,128]{1,0:T(8,128)(2,1)S(1)}, u32[]{:S(2)}, u32[]{:S(2)}) collective-permute-start(bf16[512,128]{1,0:T(8,128)(2,1)S(1)} %get-tuple-element.143), channel_id=1, source_target_pairs={{0,8},{4,12},{8,0},{12,4},{1,9},{5,13},{9,1},{13,5},{2,10},{6,14},... | collective-permute-start | bytes 393224 | tf_op jit(solution)/shard_map/ppermute | solution.py:933
  139.6 18.3 %collective-permute-start.12 = (bf16[512,128]{1,0:T(8,128)(2,1)S(1)}, bf16[512,128]{1,0:T(8,128)(2,1)S(1)}, u32[]{:S(2)}, u32[]{:S(2)}) collective-permute-start(bf16[512,128]{1,0:T(8,128)(2,1)S(1)} %get-tuple-element.142), channel_id=1, source_target_pairs={{0,4},{4,8},{8,12},{12,0},{1,5},{5,9},{9,13},{13,1},{2,6},{6,10},{... | collective-permute-start | bytes 393224 | tf_op jit(solution)/shard_map/ppermute | solution.py:933
  141.0 37.8 %collective-permute-start.3 = (bf16[512,128]{1,0:T(8,128)(2,1)}, bf16[512,128]{1,0:T(8,128)(2,1)S(1)}, u32[]{:S(2)}, u32[]{:S(2)}) collective-permute-start(bf16[512,128]{1,0:T(8,128)(2,1)} %get-tuple-element.140), channel_id=1, source_target_pairs={{0,12},{4,0},{8,4},{12,8},{1,13},{5,1},{9,5},{13,9},{2,14},{6,2},{... | collective-permute-start | bytes 393224 | tf_op jit(solution)/shard_map/ppermute | solution.py:933
  144.2 34.6 %collective-permute-start.4 = (bf16[512,128]{1,0:T(8,128)(2,1)}, bf16[512,128]{1,0:T(8,128)(2,1)S(1)}, u32[]{:S(2)}, u32[]{:S(2)}) collective-permute-start(bf16[512,128]{1,0:T(8,128)(2,1)} %get-tuple-element.139), channel_id=1, source_target_pairs={{0,8},{4,12},{8,0},{12,4},{1,9},{5,13},{9,1},{13,5},{2,10},{6,14},... | collective-permute-start | bytes 393224 | tf_op jit(solution)/shard_map/ppermute | solution.py:933
  145.3 33.5 %collective-permute-start.5 = (bf16[512,128]{1,0:T(8,128)(2,1)S(1)}, bf16[512,128]{1,0:T(8,128)(2,1)S(1)}, u32[]{:S(2)}, u32[]{:S(2)}) collective-permute-start(bf16[512,128]{1,0:T(8,128)(2,1)S(1)} %get-tuple-element.138), channel_id=1, source_target_pairs={{0,4},{4,8},{8,12},{12,0},{1,5},{5,9},{9,13},{13,1},{2,6},{6,10},{... | collective-permute-start | bytes 393224 | tf_op jit(solution)/shard_map/ppermute | solution.py:933
  158.5 23.7 %collective-permute-start.13 = (bf16[4,512,128]{2,1,0:T(8,128)(2,1)S(1)}, bf16[4,512,128]{2,1,0:T(8,128)(2,1)S(1)}, u32[]{:S(2)}, u32[]{:S(2)}) collective-permute-start(bf16[4,512,128]{2,1,0:T(8,128)(2,1)S(1)} %fusion.18), channel_id=1, source_target_pairs={{0,16},{1,17},{2,18},{3,19},{4,20},{5,21},{6,22},{7,23},{8,24},{9,... | collective-permute-start | bytes 1572872 | tf_op jit(solution)/shard_map/ppermute | solution.py:946
  179.4 2.8 copy-start.1
  232.8 1.4 copy-start.23
  232.8 299.6 %reduce-scatter.13.cloned.1.call-start = ((), (), s32[]{:S(2)}) async-start(), calls=%async_computation.10 | async-start | bytes 11796480 | tf_op jit(solution)/shard_map/reduce_scatter | solution.py:1107
  245.5 304.6 %reduce-scatter.19.cloned.1.call-start = ((), (), s32[]{:S(2)}) async-start(), calls=%async_computation.14 | async-start | bytes 2949120
  313.5 1.4 copy-start.3
  313.5 238.7 %reduce-scatter.11.cloned.1.call-start = ((), (), s32[]{:S(2)}) async-start(), calls=%async_computation.9 | async-start | bytes 2506752 | tf_op jit(solution)/shard_map/reduce_scatter | solution.py:1105
  315.8 15.8 %collective-permute-start.14 = (bf16[4,512,128]{2,1,0:T(8,128)(2,1)}, bf16[4,512,128]{2,1,0:T(8,128)(2,1)S(1)}, u32[]{:S(2)}, u32[]{:S(2)}) collective-permute-start(bf16[4,512,128]{2,1,0:T(8,128)(2,1)} %slice.104), channel_id=1, source_target_pairs={{16,0},{17,1},{18,2},{19,3},{20,4},{21,5},{22,6},{23,7},{24,8},{25... | collective-permute-start | bytes 1572872 | tf_op jit(solution)/shard_map/ppermute | solution.py:942
  317.1 20.5 %copy-start.22 = (bf16[2,512,768]{2,1,0:T(8,128)(2,1)S(1)}, bf16[2,512,768]{2,1,0:T(8,128)(2,1)}, u32[]{:S(2)}) copy-start(bf16[2,512,768]{2,1,0:T(8,128)(2,1)} %get-tuple-element.56) | copy-start | bytes 4718596
  317.9 19.8 %copy-start.21 = (bf16[2,512,768]{2,1,0:T(8,128)(2,1)S(1)}, bf16[2,512,768]{2,1,0:T(8,128)(2,1)}, u32[]{:S(2)}) copy-start(bf16[2,512,768]{2,1,0:T(8,128)(2,1)} %get-tuple-element.55) | copy-start | bytes 4718596
  317.9 79.1 %collective-permute-start.21 = (bf16[512,128]{1,0:T(8,128)(2,1)}, bf16[512,128]{1,0:T(8,128)(2,1)}, u32[]{:S(2)}, u32[]{:S(2)}) collective-permute-start(bf16[512,128]{1,0:T(8,128)(2,1)} %get-tuple-element.128), channel_id=1, source_target_pairs={{16,20},{20,24},{24,28},{28,16},{17,21},{21,25},{25,29},{29,17},{1... | collective-permute-start | bytes 393224 | tf_op jit(solution)/shard_map/ppermute | solution.py:938
  319.3 78.3 %collective-permute-start.22 = (bf16[512,128]{1,0:T(8,128)(2,1)}, bf16[512,128]{1,0:T(8,128)(2,1)}, u32[]{:S(2)}, u32[]{:S(2)}) collective-permute-start(bf16[512,128]{1,0:T(8,128)(2,1)} %get-tuple-element.127), channel_id=1, source_target_pairs={{16,24},{20,28},{24,16},{28,20},{17,25},{21,29},{25,17},{29,21},{1... | collective-permute-start | bytes 393224 | tf_op jit(solution)/shard_map/ppermute | solution.py:938
  332.3 8.4 %collective-permute-start.15 = (bf16[512,128]{1,0:T(8,128)(2,1)S(1)}, bf16[512,128]{1,0:T(8,128)(2,1)S(1)}, u32[]{:S(2)}, u32[]{:S(2)}) collective-permute-start(bf16[512,128]{1,0:T(8,128)(2,1)S(1)} %get-tuple-element.136), channel_id=1, source_target_pairs={{0,4},{4,8},{8,12},{12,0},{1,5},{5,9},{9,13},{13,1},{2,6},{6,10},{... | collective-permute-start | bytes 393224 | tf_op jit(solution)/shard_map/ppermute | solution.py:933
  333.8 10.4 %collective-permute-start.16 = (bf16[512,128]{1,0:T(8,128)(2,1)S(1)}, bf16[512,128]{1,0:T(8,128)(2,1)S(1)}, u32[]{:S(2)}, u32[]{:S(2)}) collective-permute-start(bf16[512,128]{1,0:T(8,128)(2,1)S(1)} %get-tuple-element.135), channel_id=1, source_target_pairs={{0,8},{4,12},{8,0},{12,4},{1,9},{5,13},{9,1},{13,5},{2,10},{6,14},... | collective-permute-start | bytes 393224 | tf_op jit(solution)/shard_map/ppermute | solution.py:933
  336.2 8.0 collective-permute-start.17
  340.5 301.8 %reduce-scatter.9.cloned.1.call-start = ((), (), s32[]{:S(2)}) async-start(), calls=%async_computation.8 | async-start | bytes 7520256 | tf_op jit(solution)/shard_map/reduce_scatter | solution.py:1104
  340.6 3.5 copy-start.26
  340.6 56.9 %collective-permute-start.23 = (bf16[512,128]{1,0:T(8,128)(2,1)S(1)}, bf16[512,128]{1,0:T(8,128)(2,1)}, u32[]{:S(2)}, u32[]{:S(2)}) collective-permute-start(bf16[512,128]{1,0:T(8,128)(2,1)S(1)} %get-tuple-element.126), channel_id=1, source_target_pairs={{16,28},{20,16},{24,20},{28,24},{17,29},{21,17},{25,21},{29,25},{1... | collective-permute-start | bytes 393224 | tf_op jit(solution)/shard_map/ppermute | solution.py:938
  392.1 46.5 %collective-permute-start.18 = (bf16[3,512,128]{2,1,0:T(8,128)(2,1)S(1)}, bf16[3,512,128]{2,1,0:T(8,128)(2,1)S(1)}, u32[]{:S(2)}, u32[]{:S(2)}) collective-permute-start(bf16[3,512,128]{2,1,0:T(8,128)(2,1)S(1)} %get-tuple-element.124), channel_id=1, source_target_pairs={{0,12},{4,0},{8,4},{12,8},{1,13},{5,1},{9,5},{13,9},{2,14},{6,2},{... | collective-permute-start | bytes 1179656 | tf_op jit(solution)/shard_map/ppermute | solution.py:933
  396.5 66.4 %collective-permute-start.19 = (bf16[3,512,128]{2,1,0:T(8,128)(2,1)S(1)}, bf16[3,512,128]{2,1,0:T(8,128)(2,1)S(1)}, u32[]{:S(2)}, u32[]{:S(2)}) collective-permute-start(bf16[3,512,128]{2,1,0:T(8,128)(2,1)S(1)} %get-tuple-element.123), channel_id=1, source_target_pairs={{0,8},{4,12},{8,0},{12,4},{1,9},{5,13},{9,1},{13,5},{2,10},{6,14},... | collective-permute-start | bytes 1179656 | tf_op jit(solution)/shard_map/ppermute | solution.py:933
  396.9 66.0 %collective-permute-start.20 = (bf16[3,512,128]{2,1,0:T(8,128)(2,1)S(1)}, bf16[3,512,128]{2,1,0:T(8,128)(2,1)S(1)}, u32[]{:S(2)}, u32[]{:S(2)}) collective-permute-start(bf16[3,512,128]{2,1,0:T(8,128)(2,1)S(1)} %get-tuple-element.122), channel_id=1, source_target_pairs={{0,4},{4,8},{8,12},{12,0},{1,5},{5,9},{9,13},{13,1},{2,6},{6,10},{... | collective-permute-start | bytes 1179656 | tf_op jit(solution)/shard_map/ppermute | solution.py:933
  463.7 6.2 copy-start.2
  465.6 47.0 %collective-permute-start.27 = (bf16[4,3,512,128]{3,2,1,0:T(8,128)(2,1)S(1)}, bf16[4,3,512,128]{3,2,1,0:T(8,128)(2,1)S(1)}, u32[]{:S(2)}, u32[]{:S(2)}) collective-permute-start(bf16[4,3,512,128]{3,2,1,0:T(8,128)(2,1)S(1)} %fusion.11), channel_id=1, source_target_pairs={{0,16},{1,17},{2,18},{3,19},{4,20},{5,21},{6,22},{7,23},{8,24},{9,... | collective-permute-start | bytes 4718600 | tf_op jit(solution)/shard_map/ppermute | solution.py:946
  469.9 42.7 %slice-start = ((s8[4718592]{0:T(1024)(128)(4,1)}), s8[4194304]{0:T(1024)(128)(4,1)S(1)}, s32[]{:S(2)}) async-start(s8[4718592]{0:T(1024)(128)(4,1)} %bitcast.138), calls=%async_computation.16 | async-start | bytes 8388608
  470.0 11.9 %collective-permute-start.24 = (bf16[3,512,128]{2,1,0:T(8,128)(2,1)S(1)}, bf16[3,512,128]{2,1,0:T(8,128)(2,1)S(1)}, u32[]{:S(2)}, u32[]{:S(2)}) collective-permute-start(bf16[3,512,128]{2,1,0:T(8,128)(2,1)S(1)} %get-tuple-element.120), channel_id=1, source_target_pairs={{0,12},{4,0},{8,4},{12,8},{1,13},{5,1},{9,5},{13,9},{2,14},{6,2},{... | collective-permute-start | bytes 1179656 | tf_op jit(solution)/shard_map/ppermute | solution.py:933
  470.1 38.3 %collective-permute-start.25 = (bf16[3,512,128]{2,1,0:T(8,128)(2,1)S(1)}, bf16[3,512,128]{2,1,0:T(8,128)(2,1)S(1)}, u32[]{:S(2)}, u32[]{:S(2)}) collective-permute-start(bf16[3,512,128]{2,1,0:T(8,128)(2,1)S(1)} %get-tuple-element.119), channel_id=1, source_target_pairs={{0,8},{4,12},{8,0},{12,4},{1,9},{5,13},{9,1},{13,5},{2,10},{6,14},... | collective-permute-start | bytes 1179656 | tf_op jit(solution)/shard_map/ppermute | solution.py:933
  476.9 31.5 %collective-permute-start.26 = (bf16[3,512,128]{2,1,0:T(8,128)(2,1)S(1)}, bf16[3,512,128]{2,1,0:T(8,128)(2,1)S(1)}, u32[]{:S(2)}, u32[]{:S(2)}) collective-permute-start(bf16[3,512,128]{2,1,0:T(8,128)(2,1)S(1)} %get-tuple-element.118), channel_id=1, source_target_pairs={{0,4},{4,8},{8,12},{12,0},{1,5},{5,9},{9,13},{13,1},{2,6},{6,10},{... | collective-permute-start | bytes 1179656 | tf_op jit(solution)/shard_map/ppermute | solution.py:933
  508.4 1.9 copy-start.5
  510.3 2.3 slice-start.1
  515.5 8.7 %copy-start.20 = (bf16[2,512,768]{2,1,0:T(8,128)(2,1)S(1)}, bf16[2,512,768]{2,1,0:T(8,128)(2,1)}, u32[]{:S(2)}) copy-start(bf16[2,512,768]{2,1,0:T(8,128)(2,1)} %get-tuple-element.54) | copy-start | bytes 4718596
  532.4 1.7 copy-start.13
  532.4 159.8 %reduce-scatter.15.cloned.1.call-start = ((), (), s32[]{:S(2)}) async-start(), calls=%async_computation.11 | async-start | bytes 2949120 | tf_op jit(solution)/shard_map/reduce_scatter | solution.py:1106
  533.1 216.3 %all-gather.10.cloned.1.call-start = ((), (), s32[]{:S(2)}) async-start(), calls=%async_computation.13 | async-start | bytes 1351680 | tf_op jit(solution)/shard_map/all_gather | solution.py:1072
  534.2 11.2 %copy-start.15 = (bf16[768]{0:T(1024)(128)(2,1)S(1)}, bf16[768]{0:T(1024)(128)(2,1)}, u32[]{:S(2)}) copy-start(bf16[768]{0:T(1024)(128)(2,1)} %param.23) | copy-start | bytes 4612
  534.2 11.3 %copy-start.17 = (bf16[768]{0:T(1024)(128)(2,1)S(1)}, bf16[768]{0:T(1024)(128)(2,1)}, u32[]{:S(2)}) copy-start(bf16[768]{0:T(1024)(128)(2,1)} %param.26) | copy-start | bytes 4612
  550.0 261.4 %all-reduce.4.cloned.1.call-start = ((), (), s32[]{:S(2)}) async-start(), calls=%async_computation.15 | async-start | bytes 3932160 | tf_op jit(solution)/shard_map/psum | solution.py:1115
  811.3 2.3 copy-start.8
  811.3 3.1 copy-start.9
  811.3 3.7 copy-start.6
  (5 other events, 3.3 us)
Sparse Core Ops, SparseCore 0:
  9.6 40.1 all-gather.5
  51.4 37.4 all-gather.7
  232.9 77.4 reduce-scatter.16
  312.9 78.3 reduce-scatter.12
  393.5 73.6 reduce-scatter.18
  470.8 77.8 reduce-scatter.10
  553.2 89.0 reduce-scatter.8
  644.6 47.5 reduce-scatter.14
  695.6 53.8 all-gather.9
  751.8 59.5 all-reduce.3

commit v2 on v1

--- a/solution.py
+++ b/solution.py
@@ -450,108 +450,230 @@
     log_put((top + jnp.log2(acc)).T[HD : HD + 8])
 
 
-def load_forward(source, base, q_s, k_s, v_s):
-    unfold_into(q_s, base, source[0], 0.0)
+def load_values(source, base, k_s, v_s):
     unfold_into(k_s, base, source[1], 0.0)
     unfold_into(v_s, base, source[2], 1.0)
 
 
-def full_step(step, pieces, o_ref, log_ref, q_s, k_s, v_s):
-    piece_rows = 2 * pieces[0].shape[1]
-    total = piece_rows * len(pieces)
-
-    @pl.when(step == 0)
+def packed_queries(packed):
+    value = packed.astype(F32)
+    return jnp.concatenate([value, swap_heads(value)]).astype(BF16)
+
+
+def reach(src, dst, sems, index, group, place):
+    return pltpu.make_async_remote_copy(
+        src_ref=src, dst_ref=dst, send_sem=sems[0].at[index], recv_sem=sems[1].at[index],
+        device_id={"grp": group, "seq": place}, device_id_type=pl.DeviceIdType.MESH,
+    )
+
+
+def greet(group, place):
+    barrier = pltpu.get_barrier_semaphore()
+    for other in range(2):
+        for steps in range(4):
+            if other or steps:
+                pl.semaphore_signal(
+                    barrier, 1,
+                    device_id={"grp": (group + other) % 2, "seq": (place + steps) % 4},
+                    device_id_type=pl.DeviceIdType.MESH,
+                )
+    pl.semaphore_wait(barrier, 7)
+
+
+def forward_kernel(
+    packs, att, pieces, results, logs, logs_own, crossed, k_s, v_s, send_sems, recv_sems
+):
+    group = lax.axis_index("grp")
+    place = lax.axis_index("seq")
+    sems = (send_sems, recv_sems)
+    heads = packs.shape[0]
+    rows = 2 * packs.shape[2]
+    ahead = lambda s: (place + s) % 4
+    behind = lambda s: (place + 4 - s) % 4
+
+    def first(s):
+        return reach(packs.at[2 * ahead(s)], pieces.at[0, s], sems, s - 1, 1, ahead(s))
+
+    def second_values(s):
+        source = packs.at[2 * ahead(s) + 1, pl.ds(1, 2)]
+        return reach(source, pieces.at[1, s, pl.ds(1, 2)], sems, 2 + s, 1, ahead(s))
+
+    def second_queries(s):
+        source = packs.at[2 * ahead(s) + 1, 0]
+        return reach(source, pieces.at[1, s, 0], sems, 5 + s, 1, ahead(s))
+
+    def cross(s):
+        return reach(packs.at[8 + ahead(s)], crossed.at[s], sems, 9 + s, 0, place)
+
+    def onward(s):
+        return reach(crossed.at[s], pieces.at[1, s], sems, 12 + s, 0, ahead(s))
+
+    def home(kind, s, head):
+        start = (16, 20, 24)[kind]
+        return reach(
+            results.at[min(kind, 1), s], att.at[head], sems, start + s, 1, behind(s)
+        )
+
+    greet(group, place)
+
+    def full(kind, head, before, after):
+        sel = min(kind, 1)
+        for s in range(4):
+            load_values(pieces.at[sel, s], s * rows, k_s, v_s)
+
+        def step(s, carry):
+            before(s)
+
+            def put_out(value):
+                results[sel, s] = value
+
+            def put_log(value):
+                logs[sel, s] = value
+
+            q = packed_queries(pieces[sel, s, 0])
+            attend_rows(q, k_s, v_s, 4 * rows, put_out, put_log)
+            after(s)
+            return carry
+
+        lax.fori_loop(0, 4, step, 0)
+
+    @pl.when(group == 1)
     def _():
-        for place, piece in enumerate(pieces):
-            load_forward(piece, place * piece_rows, q_s, k_s, v_s)
-
-    def put_out(value):
-        o_ref[step] = value
-
-    def put_log(value):
-        log_ref[step] = value
-
-    q = q_s[pl.ds(pl.multiple_of(step * piece_rows, piece_rows), piece_rows), :]
-    attend_rows(q, k_s, v_s, total, put_out, put_log)
-
-
-def forward_second_kernel(p0, p1, p2, p3, o_ref, log_ref, q_s, k_s, v_s):
-    full_step(pl.program_id(0), (p0, p1, p2, p3), o_ref, log_ref, q_s, k_s, v_s)
-
-
-def forward_first_kernel(
-    group_ref, pack_ref, p0, p1, p2, p3, o_ref, log_ref, ol_ref, logl_ref, q_s, k_s, v_s
-):
-    step = pl.program_id(0)
-    group = group_ref[0]
+        for s in (1, 2, 3):
+            first(s).start()
+        for s in (1, 2, 3, 0):
+            cross(s).start()
+        pieces[0, 0] = packs[2 * place]
+        pieces[1, 0] = packs[2 * place + 1]
+        for s in (1, 2, 3):
+            first(s).wait_send()
+        for s in (1, 2, 3):
+            second_values(s).start()
+        for s in (1, 2, 3):
+            first(s).wait_recv()
+
+        def before(s):
+            @pl.when(s == 2)
+            def _():
+                for other in (1, 2, 3):
+                    second_queries(other).start()
+
+        def after(s):
+            @pl.when(s == 0)
+            def _():
+                att[2 * place] = results[0, 0]
+
+            @pl.when(s > 0)
+            def _():
+                home(0, s, 2 * place).start()
+
+        full(0, 2 * place, before, after)
+        for s in (1, 2, 3):
+            second_values(s).wait_recv()
 
     @pl.when(group == 0)
     def _():
-        rows = 2 * p0.shape[1]
-        load_forward(pack_ref.at[0], 0, q_s, k_s, v_s)
-
-        def put_out(value):
-            ol_ref[step] = value
-
-        def put_log(value):
-            logl_ref[step] = value
-
-        attend_rows(q_s[0:rows, :], k_s, v_s, rows, put_out, put_log)
-
-    @pl.when((group == 1) & (step < 4))
+        def local(head, carry):
+            load_values(packs.at[head], 0, k_s, v_s)
+
+            def put_out(value):
+                att[head] = value
+
+            def put_log(value):
+                logs_own[head] = value
+
+            attend_rows(packed_queries(packs[head, 0]), k_s, v_s, rows, put_out, put_log)
+            for s in (1, 2, 3):
+
+                @pl.when(head == 4 * s - 1)
+                def _(s=s):
+                    cross(s).wait_recv()
+                    onward(s).start()
+
+            return carry
+
+        lax.fori_loop(0, heads, local, 0)
+        cross(0).wait_recv()
+        pieces[1, 0] = crossed[0]
+        for s in (1, 2, 3):
+            onward(s).wait_recv()
+
+    def before(s):
+        @pl.when((group == 1) & (s > 0))
+        def _():
+            second_queries(s).wait_recv()
+
+    def after(s):
+        @pl.when((group == 1) & (s == 0))
+        def _():
+            att[2 * place + 1] = results[1, 0]
+
+        @pl.when((group == 1) & (s > 0))
+        def _():
+            home(1, s, 2 * place + 1).start()
+
+        @pl.when(group == 0)
+        def _():
+            home(2, s, 8 + place).start()
+
+    full(1, 0, before, after)
+
+    @pl.when(group == 1)
     def _():
-        full_step(step, (p0, p1, p2, p3), o_ref, log_ref, q_s, k_s, v_s)
-
-
-def whole(shape):
-    zeros = (0,) * len(shape)
-    return pl.BlockSpec(shape, lambda *_: zeros)
-
-
-def forward_scratch(half):
-    return [pltpu.VMEM((8 * half, 2 * HD), BF16)] * 3
-
-
-def forward_first(group, packs, pieces):
+        for s in (1, 2, 3):
+            second_values(s).wait_send()
+            second_queries(s).wait_send()
+            for kind in (0, 1):
+                home(kind, s, 2 * place + kind).wait_send()
+        for s in range(4):
+            cross(s).wait_send()
+        for s in (1, 2, 3):
+            for kind in (0, 1):
+                home(kind, s, 2 * ahead(s) + kind).wait_recv()
+        for s in range(4):
+            home(2, s, 8 + ahead(s)).wait_recv()
+
+    @pl.when(group == 0)
+    def _():
+        for s in (1, 2, 3):
+            onward(s).wait_send()
+        for s in range(4):
+            home(2, s, 8 + place).wait_send()
+
+
+def in_vmem(count):
+    return [pl.BlockSpec(memory_space=pltpu.VMEM)] * count
+
+
+def forward_attention(packs):
     heads, _, half, lanes = packs.shape
-    o4, l4 = (4, half, lanes), (4, 8, 2 * half)
-    o12, l12 = (heads, half, lanes), (heads, 8, 2 * half)
-    shapes = [(o4, BF16), (l4, F32), (o12, BF16), (l12, F32)]
+    shapes = [
+        ((heads, half, lanes), BF16),
+        ((2, 4, 3, half, lanes), BF16),
+        ((2, 4, half, lanes), BF16),
+        ((2, 4, 8, 2 * half), F32),
+        ((heads, 8, 2 * half), F32),
+    ]
     return pl.pallas_call(
-        forward_first_kernel,
-        grid_spec=pltpu.PrefetchScalarGridSpec(
-            num_scalar_prefetch=1,
-            grid=(heads,),
-            in_specs=[pl.BlockSpec((1, 3, half, lanes), lambda i, g: (i * (1 - g[0]), 0, 0, 0))]
-            + [whole(pieces[0].shape)] * 4,
-            out_specs=[whole(shape) for shape, _ in shapes],
-            scratch_shapes=forward_scratch(half),
+        forward_kernel,
+        in_specs=in_vmem(1),
+        out_specs=in_vmem(len(shapes)),
+        out_shape=[jax.ShapeDtypeStruct(shape, kind) for shape, kind in shapes],
+        scratch_shapes=[
+            pltpu.VMEM((4, 3, half, lanes), BF16),
+            pltpu.VMEM((8 * half, lanes), BF16),
+            pltpu.VMEM((8 * half, lanes), BF16),
+            pltpu.SemaphoreType.DMA((28,)),
+            pltpu.SemaphoreType.DMA((28,)),
+        ],
+        compiler_params=pltpu.CompilerParams(
+            collective_id=1, has_side_effects=True, vmem_limit_bytes=WHOLE_VMEM
         ),
-        out_shape=[jax.ShapeDtypeStruct(shape, kind) for shape, kind in shapes],
-        compiler_params=params("arbitrary"),
         cost_estimate=pl.CostEstimate(
-            flops=40_000_000_000, bytes_accessed=8_000_000, transcendentals=0
+            flops=100_000_000_000, bytes_accessed=8_000_000, transcendentals=0
         ),
-        name="forward_first",
-    )(group, packs, *pieces)
-
-
-def forward_second(pieces):
-    _, half, lanes = pieces[0].shape
-    shapes = [((4, half, lanes), BF16), ((4, 8, 2 * half), F32)]
-    return pl.pallas_call(
-        forward_second_kernel,
-        grid=(4,),
-        in_specs=[whole(pieces[0].shape)] * 4,
-        out_specs=[whole(shape) for shape, _ in shapes],
-        out_shape=[jax.ShapeDtypeStruct(shape, kind) for shape, kind in shapes],
-        scratch_shapes=forward_scratch(half),
-        compiler_params=params("arbitrary"),
-        cost_estimate=pl.CostEstimate(
-            flops=40_000_000_000, bytes_accessed=8_000_000, transcendentals=0
-        ),
-        name="forward_second",
-    )(*pieces)
+        name="forward_attention",
+    )(packs)
 
 
 def tile_grads(q, do, k, v, log_row, delta_row):
@@ -578,155 +700,227 @@
     delta_s[:, base + half : base + 2 * half] = jnp.broadcast_to(second, (8, half))
 
 
-def full_back_step(step, piece_rows, log_ref, put, q_s, k_s, v_s, do_s, delta_s, dq_s):
+def backward_kernel(
+    packs, gatt, att, pieces, results, logs, logs_own, back,
+    dos, crossed, staged, q_s, k_s, v_s, do_s, delta_s, dq_s, send_sems, recv_sems,
+):
+    group = lax.axis_index("grp")
+    place = lax.axis_index("seq")
+    sems = (send_sems, recv_sems)
+    heads = packs.shape[0]
+    rows = 2 * packs.shape[2]
     scale = 1.0 / math.sqrt(HD)
-    block = pl.ds(pl.multiple_of(step * piece_rows, piece_rows), piece_rows)
-    k = k_s[block, :]
-    v = v_s[block, :]
-    dk = dv = None
-    parts = []
-    for place in range(4):
-        rows = slice(place * piece_rows, (place + 1) * piece_rows)
-        dq, dk_part, dv_part = tile_grads(
-            q_s[rows, :], do_s[rows, :], k, v, log_ref[place, 0:1, :], delta_s[0:1, rows]
-        )
-        dk = dk_part if dk is None else dk + dk_part
-        dv = dv_part if dv is None else dv + dv_part
-        dq_s[:, rows] = jnp.where(step == 0, dq, dq_s[:, rows] + dq)
-    put(step, 1, fold(dk * scale).astype(BF16))
-    put(step, 2, fold(dv).astype(BF16))
-
-    @pl.when(step == 3)
+    ahead = lambda s: (place + s) % 4
+    behind = lambda s: (place + 4 - s) % 4
+    stores = (q_s, k_s, v_s, do_s, delta_s)
+
+    def first(s):
+        return reach(gatt.at[2 * ahead(s)], dos.at[0, s], sems, s - 1, 1, ahead(s))
+
+    def second(s):
+        return reach(gatt.at[2 * ahead(s) + 1], dos.at[1, s], sems, 2 + s, 1, ahead(s))
+
+    def cross(s):
+        return reach(gatt.at[8 + ahead(s)], crossed.at[s], sems, 6 + s, 0, place)
+
+    def onward(s):
+        return reach(crossed.at[s], dos.at[1, s], sems, 9 + s, 0, ahead(s))
+
+    def home_values(kind, s, head):
+        source = staged.at[min(kind, 1), s, pl.ds(1, 2)]
+        return reach(
+            source, back.at[head, pl.ds(1, 2)], sems, (13, 17, 21)[kind] + s, 1, behind(s)
+        )
+
+    def home_queries(kind, s, head):
+        source = staged.at[min(kind, 1), s, 0]
+        return reach(source, back.at[head, 0], sems, (25, 29, 33)[kind] + s, 1, behind(s))
+
+    greet(group, place)
+
+    def full(sel, put_values, put_queries):
+        for s in range(4):
+            load_backward(
+                pieces.at[sel, s], dos[sel, s], results[sel, s], s * rows, *stores
+            )
+
+        def step(s, carry):
+            block = pl.ds(pl.multiple_of(s * rows, rows), rows)
+            k = k_s[block, :]
+            v = v_s[block, :]
+            dk = dv = None
+            for index in range(4):
+                chunk = slice(index * rows, (index + 1) * rows)
+                dq, dk_part, dv_part = tile_grads(
+                    q_s[chunk, :], do_s[chunk, :], k, v, logs[sel, index, 0:1, :],
+                    delta_s[0:1, chunk],
+                )
+                dk = dk_part if dk is None else dk + dk_part
+                dv = dv_part if dv is None else dv + dv_part
+                dq_s[:, chunk] = jnp.where(s == 0, dq, dq_s[:, chunk] + dq)
+            staged[sel, s, 1] = fold(dk * scale).astype(BF16)
+            staged[sel, s, 2] = fold(dv).astype(BF16)
+            put_values(s)
+            return carry
+
+        lax.fori_loop(0, 4, step, 0)
+        for s in (3, 2, 1, 0):
+            chunk = slice(s * rows, (s + 1) * rows)
+            staged[sel, s, 0] = fold(dq_s[:, chunk].T * scale).astype(BF16)
+            put_queries(s)
+
+    @pl.when(group == 1)
     def _():
-        for place in range(4):
-            rows = slice(place * piece_rows, (place + 1) * piece_rows)
-            put(place, 0, fold(dq_s[:, rows].T * scale).astype(BF16))
-
-
-def backward_first_kernel(
-    group_ref, a0, a1, a2, a3, b0, b1, b2, b3, d0, d1, d2, d3,
-    oa_ref, ob_ref, la_ref, lb_ref, grad_ref, q_s, k_s, v_s, do_s, delta_s, dq_s, log_s,
-):
-    step = pl.program_id(0)
-    group = group_ref[0]
-    piece_rows = 2 * a0.shape[1]
-    dos = (d0, d1, d2, d3)
-    for value, pieces, o_ref, l_ref in (
-        (1, (a0, a1, a2, a3), oa_ref, la_ref),
-        (0, (b0, b1, b2, b3), ob_ref, lb_ref),
-    ):
-
-        @pl.when((step == 0) & (group == value))
-        def _(pieces=pieces, o_ref=o_ref, l_ref=l_ref):
-            for place in range(4):
-                load_backward(
-                    pieces[place], dos[place][...], o_ref[place], place * piece_rows,
-                    q_s, k_s, v_s, do_s, delta_s,
-                )
-            log_s[...] = l_ref[...]
-
-    def put(place, part, value):
-        grad_ref[place, part] = value
-
-    full_back_step(step, piece_rows, log_s, put, q_s, k_s, v_s, do_s, delta_s, dq_s)
-
-
-def backward_second_kernel(
-    group_ref, pack_ref, dol_ref, ol_ref, ll_ref, b0, b1, b2, b3, d0, d1, d2, d3,
-    o_ref, l_ref, grad_ref, gradl_ref, q_s, k_s, v_s, do_s, delta_s, dq_s,
-):
-    step = pl.program_id(0)
-    group = group_ref[0]
-    piece_rows = 2 * b0.shape[1]
-    scale = 1.0 / math.sqrt(HD)
+        for s in (1, 2, 3):
+            first(s).start()
+        for s in (1, 2, 3, 0):
+            cross(s).start()
+        for s in (1, 2, 3):
+            second(s).start()
+        dos[0, 0] = gatt[2 * place]
+        dos[1, 0] = gatt[2 * place + 1]
+        for s in (1, 2, 3):
+            first(s).wait_recv()
+        head = 2 * place
+
+        def put_values(s):
+            @pl.when(s == 0)
+            def _():
+                back[head, 1] = staged[0, 0, 1]
+                back[head, 2] = staged[0, 0, 2]
+
+            @pl.when(s > 0)
+            def _():
+                home_values(0, s, head).start()
+
+        def put_queries(s):
+            if s == 0:
+                back[head, 0] = staged[0, 0, 0]
+            else:
+                home_queries(0, s, head).start()
+
+        full(0, put_values, put_queries)
+        for s in (1, 2, 3):
+            second(s).wait_recv()
 
     @pl.when(group == 0)
     def _():
-        load_backward(
-            pack_ref.at[0], dol_ref[0], ol_ref[0], 0, q_s, k_s, v_s, do_s, delta_s
-        )
-        rows = slice(0, piece_rows)
-        dq, dk, dv = tile_grads(
-            q_s[rows, :], do_s[rows, :], k_s[rows, :], v_s[rows, :],
-            ll_ref[0, 0:1, :], delta_s[0:1, rows],
-        )
-        gradl_ref[step, 0] = fold(dq.T * scale).astype(BF16)
-        gradl_ref[step, 1] = fold(dk * scale).astype(BF16)
-        gradl_ref[step, 2] = fold(dv).astype(BF16)
-
-    @pl.when((group == 1) & (step < 4))
+        for s in (1, 2, 3):
+            cross(s).wait_recv()
+            onward(s).start()
+        cross(0).wait_recv()
+        dos[1, 0] = crossed[0]
+        for s in (1, 2, 3):
+            onward(s).wait_recv()
+
+    def put_values(s):
+        head = 2 * place + 1
+
+        @pl.when((group == 1) & (s == 0))
+        def _():
+            back[head, 1] = staged[1, 0, 1]
+            back[head, 2] = staged[1, 0, 2]
+
+        @pl.when((group == 1) & (s > 0))
+        def _():
+            home_values(1, s, head).start()
+
+        @pl.when(group == 0)
+        def _():
+            home_values(2, s, 8 + place).start()
+
+    def put_queries(s):
+        head = 2 * place + 1
+
+        @pl.when(group == 1)
+        def _():
+            if s == 0:
+                back[head, 0] = staged[1, 0, 0]
+            else:
+                home_queries(1, s, head).start()
+
+        @pl.when(group == 0)
+        def _():
+            home_queries(2, s, 8 + place).start()
+
+    full(1, put_values, put_queries)
+
+    @pl.when(group == 0)
     def _():
-        @pl.when(step == 0)
-        def _():
-            for place, (piece, do) in enumerate(((b0, d0), (b1, d1), (b2, d2), (b3, d3))):
-                load_backward(
-                    piece, do[...], o_ref[place], place * piece_rows,
-                    q_s, k_s, v_s, do_s, delta_s,
-                )
-
-        def put(place, part, value):
-            grad_ref[place, part] = value
-
-        full_back_step(step, piece_rows, l_ref, put, q_s, k_s, v_s, do_s, delta_s, dq_s)
-
-
-def backward_scratch(half):
-    return [pltpu.VMEM((8 * half, 2 * HD), BF16)] * 4 + [
-        pltpu.VMEM((8, 8 * half), F32),
-        pltpu.VMEM((2 * HD, 8 * half), F32),
-    ]
-
-
-def backward_first(group, a, b, do, oa, ob, la, lb):
-    _, half, lanes = a[0].shape
-    operands = (*a, *b, *do, oa, ob, la, lb)
-    out = (4, 3, half, lanes)
+        def local(head, carry):
+            load_backward(packs.at[head], gatt[head], att[head], 0, *stores)
+            own = slice(0, rows)
+            dq, dk, dv = tile_grads(
+                q_s[own, :], do_s[own, :], k_s[own, :], v_s[own, :],
+                logs_own[head, 0:1, :], delta_s[0:1, own],
+            )
+            back[head, 0] = fold(dq.T * scale).astype(BF16)
+            back[head, 1] = fold(dk * scale).astype(BF16)
+            back[head, 2] = fold(dv).astype(BF16)
+            return carry
+
+        lax.fori_loop(0, heads, local, 0)
+        for s in (1, 2, 3):
+            onward(s).wait_send()
+        for s in range(4):
+            home_values(2, s, 8 + place).wait_send()
+            home_queries(2, s, 8 + place).wait_send()
+
+    @pl.when(group == 1)
+    def _():
+        for s in (1, 2, 3):
+            first(s).wait_send()
+            second(s).wait_send()
+            for kind in (0, 1):
+                home_values(kind, s, 2 * place + kind).wait_send()
+                home_queries(kind, s, 2 * place + kind).wait_send()
+        for s in range(4):
+            cross(s).wait_send()
+        for s in (1, 2, 3):
+            for kind in (0, 1):
+                home_values(kind, s, 2 * ahead(s) + kind).wait_recv()
+                home_queries(kind, s, 2 * ahead(s) + kind).wait_recv()
+        for s in range(4):
+            home_values(2, s, 8 + ahead(s)).wait_recv()
+            home_queries(2, s, 8 + ahead(s)).wait_recv()
+
+
+def backward_attention(packs, gatt, att, pieces, results, logs, logs_own):
+    heads, _, half, lanes = packs.shape
     return pl.pallas_call(
-        backward_first_kernel,
-        grid_spec=pltpu.PrefetchScalarGridSpec(
-            num_scalar_prefetch=1,
-            grid=(4,),
-            in_specs=[whole(value.shape) for value in operands],
-            out_specs=whole(out),
-            scratch_shapes=backward_scratch(half) + [pltpu.VMEM(la.shape, F32)],
+        backward_kernel,
+        in_specs=in_vmem(7),
+        out_specs=pl.BlockSpec(memory_space=pltpu.VMEM),
+        out_shape=jax.ShapeDtypeStruct((heads, 3, half, lanes), BF16),
+        scratch_shapes=[
+            pltpu.VMEM((2, 4, half, lanes), BF16),
+            pltpu.VMEM((4, half, lanes), BF16),
+            pltpu.VMEM((2, 4, 3, half, lanes), BF16),
+        ]
+        + [pltpu.VMEM((8 * half, lanes), BF16)] * 4
+        + [
+            pltpu.VMEM((8, 8 * half), F32),
+            pltpu.VMEM((lanes, 8 * half), F32),
+            pltpu.SemaphoreType.DMA((37,)),
+            pltpu.SemaphoreType.DMA((37,)),
+        ],
+        compiler_params=pltpu.CompilerParams(
+            collective_id=2, has_side_effects=True, vmem_limit_bytes=WHOLE_VMEM
         ),
-        out_shape=jax.ShapeDtypeStruct(out, BF16),
-        compiler_params=params("arbitrary"),
         cost_estimate=pl.CostEstimate(
-            flops=60_000_000_000, bytes_accessed=8_000_000, transcendentals=0
+            flops=120_000_000_000, bytes_accessed=8_000_000, transcendentals=0
         ),
-        name="backward_first",
-    )(group, *operands)
-
-
-def backward_second(group, packs, dol, ol, ll, b, do, ob, lb):
-    heads, _, half, lanes = packs.shape
-    each = lambda shape: pl.BlockSpec(
-        (1,) + shape[1:], lambda i, g: (i * (1 - g[0]),) + (0,) * (len(shape) - 1)
-    )
-    operands = (*b, *do, ob, lb)
-    outs = [(4, 3, half, lanes), (heads, 3, half, lanes)]
-    return pl.pallas_call(
-        backward_second_kernel,
-        grid_spec=pltpu.PrefetchScalarGridSpec(
-            num_scalar_prefetch=1,
-            grid=(heads,),
-            in_specs=[each(packs.shape), each(dol.shape), each(ol.shape), each(ll.shape)]
-            + [whole(value.shape) for value in operands],
-            out_specs=[whole(shape) for shape in outs],
-            scratch_shapes=backward_scratch(half),
-        ),
-        out_shape=[jax.ShapeDtypeStruct(shape, BF16) for shape in outs],
-        compiler_params=params("arbitrary"),
-        cost_estimate=pl.CostEstimate(
-            flops=60_000_000_000, bytes_accessed=8_000_000, transcendentals=0
-        ),
-        name="backward_second",
-    )(group, packs, dol, ol, ll, *operands)
+        name="backward_attention",
+    )(packs, gatt, att, pieces, results, logs, logs_own)
+
+
+def whole(shape):
+    zeros = (0,) * len(shape)
+    return pl.BlockSpec(shape, lambda *_: zeros)
 
 
 def middle_kernel(
-    x_ref, cot_ref, att_ref, vec_ref, upb_ref, ow_ref, up_ref, down_ref,
+    x_ref, cot_ref, att_ref, vec_ref, ow_ref, feed_ref,
     out_ref, attlow_ref, hidden_ref, act_ref, gfeed_ref, gpre_ref, mgrad_ref, gbranch_ref,
     gatt_ref, sums_ref, upsum_ref, att_s, slope_s,
 ):
@@ -750,12 +944,12 @@
     n, inverse = normalise(middle)
     hidden = (n * gain * (1.0 + scale) + shift).astype(BF16)
     hidden_ref[...] = hidden.reshape(2, rows, width)
-    units = up_ref.shape[1]
-    chunk = math.gcd(units, 768)
+    shares, _, chunk = feed_ref.shape
     feed = None
-    for start in range(0, units, chunk):
-        cols = slice(start, start + chunk)
-        pre = jnp.dot(hidden, up_ref[:, cols], preferred_element_type=F32) + upb_ref[0:1, cols]
+    for index in range(shares):
+        cols = slice(index * chunk, (index + 1) * chunk)
+        pre = jnp.dot(hidden, feed_ref[index, :width], preferred_element_type=F32)
+        pre = pre + feed_ref[index, 2 * width : 2 * width + 1].astype(F32)
         square = pre * pre
         root = math.sqrt(2.0 / math.pi)
         tanh = jnp.tanh(pre * (root + (root * 0.044715) * square))
@@ -765,7 +959,7 @@
             root + (3.0 * root * 0.044715) * square
         )
         act_ref[:, :, cols] = act.reshape(2, rows, chunk)
-        part = jnp.dot(act, down_ref[cols, :], preferred_element_type=F32)
+        part = jnp.dot(act, feed_ref[index, width : 2 * width], preferred_element_type=F32)
         feed = part if feed is None else feed + part
     feed = feed + down_bias
     out_ref[...] = (middle + gate_two * feed).astype(BF16).reshape(2, rows, width)
@@ -774,13 +968,15 @@
     gfeed_ref[...] = gfeed.reshape(2, rows, width)
     ghidden = None
     up_sums = []
-    for start in range(0, units, chunk):
-        cols = slice(start, start + chunk)
-        gact = lax.dot_general(gfeed, down_ref[cols, :], NT, preferred_element_type=F32)
+    for index in range(shares):
+        cols = slice(index * chunk, (index + 1) * chunk)
+        gact = lax.dot_general(
+            gfeed, feed_ref[index, width : 2 * width], NT, preferred_element_type=F32
+        )
         gpre = (gact * slope_s[:, cols]).astype(BF16)
         gpre_ref[:, :, cols] = gpre.reshape(2, rows, chunk)
         up_sums.append(jnp.sum(gpre.astype(F32), axis=0, keepdims=True))
-        part = lax.dot_general(gpre, up_ref[:, cols], NT, preferred_element_type=F32)
+        part = lax.dot_general(gpre, feed_ref[index, :width], NT, preferred_element_type=F32)
         ghidden = part if ghidden is None else ghidden + part
     e = ghidden * ((1.0 + scale) * gain)
     mgrad = cot + inverse * (
@@ -816,10 +1012,10 @@
     return pl.BlockSpec(shape, lambda *_: zeros, pipeline_mode=pl.Buffered(1))
 
 
-def middle_pass(x2, cot2, att, vecs, up_bias, out_weight, up_full, down_full, rows=128):
+def middle_pass(x2, cot2, att, vecs, out_weight, feed_weights, rows=128):
     half, width = x2.shape[1:]
     heads = width // HD
-    units = up_full.shape[1]
+    units = feed_weights.shape[0] * feed_weights.shape[2]
     tok = lambda last: pl.BlockSpec((2, rows, last), lambda i: (0, i, 0))
     pack = pl.BlockSpec((heads, rows, 2 * HD), lambda i: (0, i, 0))
     token = lambda last, kind: jax.ShapeDtypeStruct((2, half, last), kind)
@@ -827,8 +1023,8 @@
         middle_kernel,
         grid=(half // rows,),
         in_specs=[
-            tok(width), tok(width), pack, whole(vecs.shape), whole(up_bias.shape),
-            once(out_weight.shape), once(up_full.shape), once(down_full.shape),
+            tok(width), tok(width), pack, whole(vecs.shape), once(out_weight.shape),
+            once(feed_weights.shape),
         ],
         out_specs=[
             tok(width), tok(width), tok(width), tok(units), tok(width), tok(units), tok(width),
@@ -844,7 +1040,7 @@
         scratch_shapes=[pltpu.VMEM((2 * rows, width), BF16), pltpu.VMEM((2 * rows, units), F32)],
         compiler_params=params("arbitrary"),
         name="middle_pass",
-    )(x2, cot2, att, vecs, up_bias, out_weight, up_full, down_full)
+    )(x2, cot2, att, vecs, out_weight, feed_weights)
 
 
 def unrotate_kernel(pack_ref, cos_ref, sin_ref, mixed_ref):
@@ -928,22 +1124,95 @@
     )(mixed, weight, x2, mgrad, vecs)
 
 
+def weight_grads_kernel(
+    pick_ref, hidden_ref, gfeed_ref, att_ref, gbranch_ref, act_ref, gpre_ref, out_ref,
+    hidden_s, gfeed_s, att_s,
+):
+    step = pl.program_id(0)
+
+    @pl.when(step == 0)
+    def _():
+        hidden_s[...] = hidden_ref[...].T
+        gfeed_s[...] = gfeed_ref[...].T
+        att_s[...] = att_ref[...].T
+
+    width = hidden_s.shape[0]
+    split = width // 4
+    part = split // 4
+    up = jnp.dot(hidden_s[...], gpre_ref[...], preferred_element_type=F32).astype(BF16)
+    down = jnp.dot(gfeed_s[...], act_ref[...], preferred_element_type=F32).astype(BF16)
+    offset = pick_ref[step] * part
+    rows = jnp.concatenate(
+        [
+            att_s[pl.ds(pl.multiple_of(offset + index * split, 16), part), :]
+            for index in range(4)
+        ]
+    )
+    out = jnp.dot(rows, gbranch_ref[...], preferred_element_type=F32).astype(BF16)
+    for index in range(4):
+        out_ref[0, index, :split] = up[index * split : (index + 1) * split]
+        out_ref[0, index, split : 2 * split] = down[index * split : (index + 1) * split]
+        out_ref[0, index, 2 * split :] = out[index * part : (index + 1) * part]
+
+
+def weight_grads(picked, hidden, gfeed, att, gbranch, act, gpre):
+    tokens, width = hidden.shape
+    block = pl.BlockSpec((tokens, act.shape[1] // 4), lambda i, p: (0, p[i]))
+    shape = (2, 4, width // 2 + width // 16, width)
+    return pl.pallas_call(
+        weight_grads_kernel,
+        grid_spec=pltpu.PrefetchScalarGridSpec(
+            num_scalar_prefetch=1,
+            grid=(2,),
+            in_specs=[once(hidden.shape)] * 4 + [block, block],
+            out_specs=pl.BlockSpec((1,) + shape[1:], lambda i, p: (i, 0, 0, 0)),
+            scratch_shapes=[pltpu.VMEM((width, tokens), BF16)] * 3,
+        ),
+        out_shape=jax.ShapeDtypeStruct(shape, BF16),
+        compiler_params=params("arbitrary"),
+        cost_estimate=pl.CostEstimate(
+            flops=6_000_000_000, bytes_accessed=20_000_000, transcendentals=0
+        ),
+        name="weight_grads",
+    )(picked, hidden, gfeed, att, gbranch, act, gpre)
+
+
+def swapped(value, axis, bit):
+    count = lax.axis_size(axis)
+    return lax.ppermute(value, axis, [(place, place ^ bit) for place in range(count)])
+
+
+def wide(value):
+    return value.astype(F32)
+
+
+def over_cores(sent, kept):
+    return (wide(kept) + wide(swapped(sent, "mlp", 1))).astype(BF16)
+
+
+def over_rows(value, row):
+    other = swapped(pick(value, 1 - row), "mlp", 2)
+    return (wide(pick(value, row)) + wide(other)).astype(BF16)
+
+
+def over_places(value, place):
+    total = wide(pick(value, place))
+    for steps in (1, 2, 3):
+        total = total + wide(along(pick(value, (place + steps) % 4), steps))
+    return total.astype(BF16)
+
+
+def over_groups(value):
+    return wide(value) + wide(swapped(value, "grp", 1))
+
+
+def tie(*values):
+    return lax.optimization_barrier(values)
+
+
 def along(value, steps):
     pairs = [(place, (place + steps) % 4) for place in range(4)]
     return lax.ppermute(value, "seq", pairs)
-
-
-def along_second(value, steps):
-    pairs = [(4 + place, 4 + (place + steps) % 4) for place in range(4)]
-    return lax.ppermute(value, ("grp", "seq"), pairs)
-
-
-def to_first(value):
-    return lax.ppermute(value, "grp", [(1, 0)])
-
-
-def to_second(value):
-    return lax.ppermute(value, "grp", [(0, 1)])
 
 
 def pick(stack, index):
@@ -964,9 +1233,11 @@
     slot = lambda steps: (place + steps) % 4
     group_row = jnp.full((1,), group, jnp.int32)
 
-    up_full = lax.all_gather(up_weight, "mlp", axis=1, tiled=True)
-    down_full = lax.all_gather(down_weight, "mlp", axis=0, tiled=True)
-    up_bias_full = lax.all_gather(up_bias.astype(F32), "mlp", axis=0, tiled=True)
+    share_units = up_weight.shape[1]
+    bias_rows = jnp.broadcast_to(up_bias[None, :], (16, share_units))
+    feed_weights = lax.all_gather(
+        jnp.concatenate([up_weight, down_weight, bias_rows]), "mlp", axis=0
+    )
 
     step_value = jnp.sum(jnp.where(jnp.arange(4, dtype=jnp.int32) == place, step_index[0], 0))
     embedded = lax.dynamic_slice_in_dim(time_table, step_value, 1, 0)[0].astype(F32)
@@ -994,58 +1265,39 @@
     )
     normed, packs = project(x2, vec_one, qkv_weight, cosine, sine)
 
-    crossed = to_first(packs[8:])
-    a = [pick(packs, 2 * slot(0))] + [
-        along_second(pick(packs, 2 * slot(s)), s) for s in (1, 2, 3)
-    ]
-    b_from = jnp.where(second, packs[1:8:2], crossed)
-    b = [pick(b_from, slot(0))] + [along(pick(b_from, slot(s)), s) for s in (1, 2, 3)]
-    oa, la, o_own, l_own = forward_first(group_row, packs, a)
-    ob, lb = forward_second(b)
-
-    def home(pieces):
-        parts = [pieces[0]] + [along(pieces[s], -s) for s in (1, 2, 3)]
-        return jnp.roll(jnp.stack(parts), place, axis=0)
-
-    def join(from_a, from_b, from_first, own):
-        interleaved = jnp.stack([from_a, from_b], axis=1).reshape((8,) + from_a.shape[1:])
-        return jnp.where(second, jnp.concatenate([interleaved, from_first]), own)
-
-    a_home = home(oa)
-    b_home = home(ob)
-    att = join(a_home, b_home, to_second(b_home), o_own)
-
-    up_bias_row = jnp.broadcast_to(up_bias_full[None, :], (8, up_bias_full.shape[0]))
+    att, pieces, results, logs, logs_own = forward_attention(packs)
     (
         output, att_low, hidden, act, grad_feed, grad_pre, middle_grad, grad_branch, grad_att,
         middle_sums, up_sums,
     ) = middle_pass(
-        x2, cotangent.reshape(2, half, width), att, vec_two, up_bias_row, out_weight, up_full,
-        down_full,
+        x2, cotangent.reshape(2, half, width), att, vec_two, out_weight, feed_weights
     )
     flat = lambda value: value.reshape(token_rows, value.shape[2])
-    across = lambda left, right: lax.dot_general(
-        flat(left), flat(right), TN, preferred_element_type=F32
-    )
-
-    crossed_grad = to_first(grad_att[8:])
-    f_from = jnp.where(second, grad_att[0:8:2], crossed_grad)
-    do_f = [pick(f_from, slot(0))] + [along(pick(f_from, slot(s)), s) for s in (1, 2, 3)]
-    do_b = [pick(grad_att, 2 * slot(0) % 8 + 1)] + [
-        along_second(pick(grad_att, 2 * slot(s) + 1), s) for s in (1, 2, 3)
-    ]
-    out_grad = across(att_low, grad_branch)
-    up_grad = across(hidden, grad_pre)
-    down_grad = across(act, grad_feed)
-    grad_f = backward_first(group_row, a, b, do_f, oa, ob, la, lb)
-    grad_s, grad_own = backward_second(
-        group_row, packs, grad_att, o_own, l_own, b, do_b, ob, lb
-    )
-    f_home = home(grad_f)
-    s_home = home(grad_s)
-    grads = join(f_home, s_home, to_second(f_home), grad_own)
+    core = lax.axis_index("mlp") % 2
+    row = lax.axis_index("mlp") // 2
+    factors = tuple(
+        flat(value) for value in (hidden, grad_feed, att_low, grad_branch, act, grad_pre)
+    )
+    feed_sent = weight_grads(jnp.stack([1 - core, 3 - core]).astype(jnp.int32), *factors)
+    feed_kept = weight_grads(jnp.stack([core, 2 + core]).astype(jnp.int32), *factors)
+    feed = over_cores(feed_sent, feed_kept)
+
+    feed, grad_att = tie(feed, grad_att)
+    feed = over_rows(feed, row)
+    grads = backward_attention(packs, grad_att, att, pieces, results, logs, logs_own)
+    feed, grads = tie(feed, grads)
+    feed = over_places(feed, place)
+    feed_total = over_groups(feed)
     mixed_grad = unrotate(grads, cosine, sine)
-    qkv_grad = across(normed, mixed_grad)
+    blocks = flat(normed).T.reshape(4, 2, 2, width // 16, token_rows)
+    blocks = jnp.transpose(blocks, (2, 1, 0, 3, 4)).reshape(2, width // 2, token_rows)
+    project_back = lambda part: jnp.dot(
+        part, flat(mixed_grad), preferred_element_type=F32
+    ).astype(BF16).reshape(2, 4, width // 16, 3 * width)
+    qkv = over_cores(
+        project_back(pick(blocks, 1 - core)), project_back(pick(blocks, core))
+    )
+    qkv_total = over_groups(over_places(over_rows(qkv, row), place))
     input_grad, input_sums = input_pass(mixed_grad, qkv_weight, x2, middle_grad, vec_one)
 
     shift_one_grad = input_sums[0]
@@ -1062,15 +1314,14 @@
     )
     cond_grad = jnp.dot(ada_weight.astype(F32), mod_grad, precision=highest)
     table_row = silu_back(cond_grad)[0]
+    cond_size = condition.shape[0]
     small = jnp.concatenate(
         [
             mod_grad, first_gain_grad, second_gain_grad, up_sums[0], middle_sums[3],
-            table_row, condition,
+            table_row, condition, jnp.full((cond_size,), step_value, F32),
         ]
     )
-    step_row = jnp.full((1,), step_value, jnp.int32)
     small_all = lax.all_gather(small, ("grp", "seq", "mlp"), axis=0)
-    steps_all = lax.all_gather(step_row, ("grp", "seq", "mlp"), axis=0, tiled=True)
     rank = place * mlp_count + lax.axis_index("mlp")
     ranks = 4 * mlp_count
 
@@ -1079,7 +1330,7 @@
         return lax.dynamic_slice_in_dim(small_all, start + rank * each, each, 1)
 
     mod_size = 6 * width
-    units = up_full.shape[1]
+    units = share_units * mlp_count
     mod_share = share(0, mod_size)
     start = mod_size
     first_share = jnp.sum(share(start, width), axis=0)
@@ -1090,29 +1341,19 @@
     start += units
     down_bias_share = jnp.sum(share(start, width), axis=0)
     start += width
-    cond_size = condition.shape[0]
     rows_all = small_all[:, start : start + cond_size]
-    cond_all = small_all[:, start + cond_size :].astype(BF16).astype(F32)
+    cond_all = small_all[:, start + cond_size : start + 2 * cond_size].astype(BF16).astype(F32)
+    steps_all = small_all[:, start + 2 * cond_size].astype(jnp.int32)
     ada_share = lax.dot_general(cond_all, mod_share, TN, precision=highest)
     table_each = time_table.shape[0] // ranks
     own_rows = rank * table_each + jnp.arange(table_each, dtype=jnp.int32)
     chosen = (own_rows[:, None] == steps_all[None, :]).astype(F32)
     table_share = jnp.dot(chosen, rows_all, precision=highest)
 
-    both_axes = ("seq", "mlp")
-    big = (
-        lax.psum_scatter(qkv_grad, both_axes, scatter_dimension=0, tiled=True),
-        lax.psum_scatter(out_grad, both_axes, scatter_dimension=0, tiled=True),
-        lax.psum_scatter(
-            lax.psum_scatter(up_grad, "mlp", scatter_dimension=1, tiled=True),
-            "seq", scatter_dimension=0, tiled=True,
-        ),
-        lax.psum_scatter(
-            lax.psum_scatter(down_grad, "mlp", scatter_dimension=0, tiled=True),
-            "seq", scatter_dimension=1, tiled=True,
-        ),
-    )
-    qkv_total, out_total, up_total, down_total = lax.psum(big, "grp")
+    split = width // 4
+    up_total = feed_total[:split]
+    down_total = feed_total[split : 2 * split].T
+    out_total = feed_total[2 * split :]
     return (
         output.reshape(1, token_rows, width),
         input_grad.reshape(1, token_rows, width),

time: 830 us -> 533 us (0.64)
  waiting for transfers between devices: 388 us -> 90.2 us
  Pallas kernels: 206 us -> 318 us
  blocking collectives: 44.9 us -> 0 us
  starting transfers between devices: 73.6 us -> 38 us
  matrix products: 36 us -> 14.2 us
  local copies, waits for them, and re-layouts: 33.9 us -> 17.8 us
    reduce_scatter x5 -> x0, waiting for transfers between devices: 205 us -> none  [the longest x1 90 us: four_shards(): lax.psum_scatter(qkv_grad, both_axes, scatter_dimension=0, tiled=True)]
    pallas_call x4, Pallas kernels: 137 us -> 249 us  [the longest x1 140 us: backward_attention(): pl.pallas_call(backward_kernel, in_specs=in_vmem(7), out_specs=pl.BlockSp...]
    psum x1 -> x0, waiting for transfers between devices: 56.6 us -> none  [four_shards(): qkv_total, out_total, up_total, down_total = lax.psum(big, 'grp')]
    unnamed x1 -> x0, blocking collectives: 39.7 us -> none
    ppermute x18 -> x6, starting transfers between devices: 43.7 us -> 8.04 us  [along(): return lax.ppermute(value, 'seq', pairs)]
    ppermute x10 -> x6, waiting for transfers between devices: 43.8 us -> 18.8 us  [swapped(): lax.ppermute(value, axis, [(place, place ^ bit) for place in range(count)])]
    dot_general x4 -> x2, matrix products: 32.2 us -> 10.4 us  [four_shards(): jnp.dot(part, flat(mixed_grad), preferred_element_type=F32).astype(BF16)]
    all_gather x1, waiting for transfers between devices: 16.8 us -> 2.46 us  [four_shards(): small_all = lax.all_gather(small, ('grp', 'seq', 'mlp'), axis=0)]
  transfers between devices with their start and end apart: 38 -> 14, of which waited for: 13 -> 9; matrix products, arithmetic and copies ran while one was open for 9% -> 7% of each run, Pallas kernels for 20% -> 47%
where the time goes in v2:
time: 533 us; the launch traced here: 527 us
  Pallas kernels  318 us (60%)
  waiting for transfers between devices  90.2 us (17%)
  starting transfers between devices  38 us (7%)
  other arithmetic  30.8 us (6%)
  local copies, waits for them, and re-layouts  17.8 us (3%)
  between operations  17.4 us (3%)
  matrix products  14.2 us (3%)
    pallas_call x1, Pallas kernels, backward_attention(): pl.pallas_call(backward_kernel, in_specs=in_vmem(7), out_specs=pl.BlockSp...  140 us
    pallas_call x1, Pallas kernels, forward_attention(): pl.pallas_call(forward_kernel, in_specs=in_vmem(1), out_specs=in_vmem(len...  81.7 us
    ppermute x6, waiting for transfers between devices, along(): return lax.ppermute(value, 'seq', pairs)  68.9 us
    pallas_call x1, Pallas kernels, middle_pass(): pl.pallas_call(middle_kernel, grid=(half // rows,), in_specs=[tok(width),...  38.1 us
    ppermute x6, starting transfers between devices, swapped(): lax.ppermute(value, axis, [(place, place ^ bit) for place in range(count)])  29.9 us
    pallas_call x2, Pallas kernels, weight_grads(): pl.pallas_call(weight_grads_kernel, grid_spec=pltpu.PrefetchScalarGridSpe...  26.7 us
    ppermute x6, waiting for transfers between devices, swapped(): lax.ppermute(value, axis, [(place, place ^ bit) for place in range(count)])  18.8 us
    pallas_call x1, Pallas kernels, project(): pl.pallas_call(project_kernel, grid=(half // rows,), in_specs=[tok(width)...  11.7 us
  transfers between devices with their start and end apart: 14, of which 9 were waited for; matrix products, arithmetic and copies ran while one was open for 7% of the time, Pallas kernels for 47%

profile of v2, /device:TPU:0, one launch (start us, length us, event | category | flops | bytes accessed | tf_op | source)
XLA Modules:
  0.0 526.5 jit_solution(1535743635919227798)
XLA Ops:
  7.2 0.8 broadcast_in_dim.9
  8.0 3.2 pad_maximum_fusion
  11.9 0.6 fusion.27
  14.5 1.0 convolution_reduce_fusion
  15.5 0.6 copy-done.3
  16.2 0.6 stack.64.vec_ref
  16.9 1.9 fusion.13
  18.8 1.8 pad_maximum_fusion.1
  20.6 11.7 %project.1 = (bf16[2,512,768]{2,1,0:T(8,128)(2,1)}, bf16[12,3,512,128]{3,2,1,0:T(8,128)(2,1)}) custom-call(bf16[2,512,768]{2,1,0:T(8,128)(2,1)} %bitcast.105, f32[8,768]{1,0:T(8,128)} %stack.64.vec_ref, bf16[768,2304]{1,0:T(8,128)(2,1)} %w_ref.3, f32[2,512,128]{2,1,0:T(8,128)} %get-tuple-element.102.cos_ref, f32[2,512,128]{2,1,0:T(8,128)} %get-tuple-element.103.sin_ref), custom_call_target="tpu_custom_call" | custom-call | tf_op jit(solution)/shard_map/project/pallas_call | solution.py:418
  32.4 0.6 stack.73.vec_ref
  33.6 81.7 %forward_attention.1 = (bf16[12,512,128]{2,1,0:T(8,128)(2,1)}, bf16[2,4,3,512,128]{4,3,2,1,0:T(8,128)(2,1)}, bf16[2,4,512,128]{3,2,1,0:T(8,128)(2,1)}, f32[2,4,8,1024]{3,2,1,0:T(8,128)}, f32[12,8,1024]{2,1,0:T(8,128)}) custom-call(bf16[12,3,512,128]{3,2,1,0:T(8,128)(2,1)} %get-tuple-element.37.packs), custom_call_target="tpu_custom_call" | custom-call | flops 99999997952 | bytes 8000000 | tf_op jit(solution)/shard_map/forward_attention/pallas_call | solution.py:657
  115.4 38.1 %middle_pass.1 = (bf16[2,512,768]{2,1,0:T(8,128)(2,1)}, bf16[2,512,768]{2,1,0:T(8,128)(2,1)}, bf16[2,512,768]{2,1,0:T(8,128)(2,1)}, bf16[2,512,3072]{2,1,0:T(8,1...) custom-call(bf16[2,512,768]{2,1,0:T(8,128)(2,1)} %bitcast.106, ...), custom_call_target="tpu_custom_call" | custom-call | tf_op jit(solution)/shard_map/middle_pass/pallas_call | solution.py:1022
  153.5 13.3 %weight_grads.3 = bf16[2,4,432,768]{3,2,1,0:T(8,128)(2,1)} custom-call(s32[2]{0:T(128)} %pad_add_fusion.1.pick_ref, bf16[1024,768]{1,0:T(8,128)(2,1)} %bitcast.111, bf16[1024,768]{1,0:T(8,128)(2,1)} %bitcast.113, bf16[1024,768]{1,0:T(8,128)(2,1)} %bitcast.109, bf16[1024,768]{1,0:T(8,128)(2,1)} %bitcast.115, bf16[1024,3072]{1,0:T(8,128)(2,1)} %bitcast.100, ...), custom_call_target="tpu_custom_call" | custom-call | flops 6000000000 | bytes 20000000 | tf_op jit(solution)/shard_map/weight_grads/pallas_call | solution.py:1162
  167.5 1.7 copy.31
  169.2 1.3 copy.32
  170.5 0.6 pad_add_fusion.pick_ref
  171.1 1.5 slice.51
  172.6 0.6 slice_reduce_fusion
  173.2 13.4 %weight_grads.2 = bf16[2,4,432,768]{3,2,1,0:T(8,128)(2,1)} custom-call(s32[2]{0:T(128)} %pad_add_fusion.pick_ref, bf16[1024,768]{1,0:T(8,128)(2,1)} %bitcast.112, bf16[1024,768]{1,0:T(8,128)(2,1)} %bitcast.114, bf16[1024,768]{1,0:T(8,128)(2,1)} %bitcast.110, bf16[1024,768]{1,0:T(8,128)(2,1)} %bitcast.116, bf16[1024,3072]{1,0:T(8,128)(2,1)} %bitcast.101, ...), custom_call_target="tpu_custom_call" | custom-call | flops 6000000000 | bytes 20000000 | tf_op jit(solution)/shard_map/weight_grads/pallas_call | solution.py:1162
  186.7 5.3 %add_convert_fusion = bf16[2,4,432,768]{3,2,1,0:T(8,128)(2,1)S(1)} fusion(bf16[2,4,432,768]{3,2,1,0:T(8,128)(2,1)} %collective-permute-done, bf16[2,4,432,768]{3,2,1,0:T(8,128)(2,1)} %weight_grads.2), kind=kLoop, calls=%fused_computation | loop fusion | flops 10616832 | bytes 15925248 | tf_op jit(solution)/shard_map/convert_element_type | solution.py:1190
  192.2 2.1 copy-done.1
  194.3 1.6 collective-permute-start.1
  195.9 140.2 %backward_attention.1.pack_ref = bf16[12,3,512,128]{3,2,1,0:T(8,128)(2,1)} custom-call(bf16[12,3,512,128]{3,2,1,0:T(8,128)(2,1)} %get-tuple-element.37.packs, bf16[12,512,128]{2,1,0:T(8,128)(2,1)} %get-tuple-element.48.gatt, bf16[12,512,128]{2,1,0:T(8,128)(2,1)} %get-tuple-element.38.att_ref.att, bf16[2,4,3,512,128]{4,3,2,1,0:T(8,128)(2,1)} %get-tuple-element.49.pieces, ...), custom_call_target="tpu_custom_call" | custom-call | flops 120000004096 | bytes 8000000 | tf_op jit(solution)/shard_map/backward_attention/pallas_call | solution.py:890
  336.0 3.2 fusion
  339.3 9.5 %unrotate.1.mixed_ref = bf16[2,512,2304]{2,1,0:T(8,128)(2,1)} custom-call(bf16[12,3,512,128]{3,2,1,0:T(8,128)(2,1)} %backward_attention.1.pack_ref, f32[2,512,128]{2,1,0:T(8,128)} %get-tuple-element.102.cos_ref, f32[2,512,128]{2,1,0:T(8,128)} %get-tuple-element.103.sin_ref), custom_call_target="tpu_custom_call" | custom-call | tf_op jit(solution)/shard_map/unrotate/pallas_call | solution.py:1067
  348.8 10.2 %input_pass.1 = (f32[2,512,768]{2,1,0:T(8,128)}, f32[8,768]{1,0:T(8,128)}) custom-call(bf16[2,512,2304]{2,1,0:T(8,128)(2,1)} %unrotate.1.mixed_ref, bf16[768,2304]{1,0:T(8,128)(2,1)} %w_ref.3, bf16[2,512,768]{2,1,0:T(8,128)(2,1)} %bitcast.107, f32[2,512,768]{2,1,0:T(8,128)} %get-tuple-element.54.mgrad_ref, f32[8,768]{1,0:T(8,128)} %stack.64.vec_ref), custom_call_target="tpu_custom_call" | custom-call | flops 6000000000 | bytes 20000000 | tf_op jit(solution)/shard_map/input_pass/pallas_call | solution.py:1108
  359.0 0.8 slice_reduce_fusion.5
  360.0 0.7 constant_dynamic-update-slice_fusion.18
  360.7 0.7 constant_dynamic-update-slice_fusion.17
  361.4 5.8 %convolution_convert_fusion = bf16[384,2304]{1,0:T(8,128)(2,1)} fusion(bf16[1024,2304]{1,0:T(8,128)(2,1)} %bitcast.117, bf16[2,384,1024]{2,1,0:T(8,128)(2,1)} %bitcast.121, s32[]{:T(128)S(6)} %select_n.100), kind=kOutput, calls=%fused_computation.3 | convolution fusion | flops 1812824064 | bytes 7274500 | tf_op jit(solution)/shard_map/dot_general | solution.py:1294
  367.2 1.3 dynamic-slice_bitcast_fusion.4
  368.6 2.5 collective-permute-start.8
  371.1 1.5 collective-permute-start.10
  372.8 1.0 convolution_bitcast_fusion
  373.8 0.7 constant_dynamic-update-slice_fusion.14
  374.5 0.7 constant_dynamic-update-slice_fusion.13
  375.2 0.6 reshape.226
  375.9 4.6 convolution_convert_fusion.1
  380.5 7.9 %collective-permute-done.8 = bf16[432,768]{1,0:T(8,128)(2,1)S(1)} collective-permute-done((bf16[432,768]{1,0:T(8,128)(2,1)}, bf16[432,768]{1,0:T(8,128)(2,1)S(1)}, u32[]{:S(2)}, u32[]{:S(2)}) %collective-permute-start.8) | collective-permute-done | bytes 663584 | tf_op jit(solution)/shard_map/ppermute | solution.py:1215
  388.4 13.8 %collective-permute-done.10 = bf16[432,768]{1,0:T(8,128)(2,1)S(1)} collective-permute-done((bf16[432,768]{1,0:T(8,128)(2,1)}, bf16[432,768]{1,0:T(8,128)(2,1)S(1)}, u32[]{:S(2)}, u32[]{:S(2)}) %collective-permute-start.10) | collective-permute-done | bytes 663584 | tf_op jit(solution)/shard_map/ppermute | solution.py:1215
  402.1 29.3 %collective-permute-done.9 = bf16[432,768]{1,0:T(8,128)(2,1)S(1)} collective-permute-done((bf16[432,768]{1,0:T(8,128)(2,1)}, bf16[432,768]{1,0:T(8,128)(2,1)S(1)}, u32[]{:S(2)}, u32[]{:S(2)}) %collective-permute-start.9) | collective-permute-done | bytes 663584 | tf_op jit(solution)/shard_map/ppermute | solution.py:1215
  431.5 1.5 fusion.5
  432.9 26.6 %collective-permute-start.11 = (bf16[432,768]{1,0:T(8,128)(2,1)S(1)}, bf16[432,768]{1,0:T(8,128)(2,1)S(1)}, u32[]{:S(2)}, u32[]{:S(2)}) collective-permute-start(bf16[432,768]{1,0:T(8,128)(2,1)S(1)} %fusion.5), channel_id=1, source_target_pairs={{0,16},{16,0},{1,17},{17,1},{2,18},{18,2},{3,19},{19,3},{4,20},{20... | collective-permute-start | bytes 1990664 | tf_op jit(solution)/shard_map/ppermute | solution.py:1182
  459.5 1.9 fusion.1
  461.5 1.0 dynamic-slice_bitcast_fusion.1
  462.8 14.2 %collective-permute-done.11 = bf16[432,768]{1,0:T(8,128)(2,1)S(1)} collective-permute-done((bf16[432,768]{1,0:T(8,128)(2,1)S(1)}, bf16[432,768]{1,0:T(8,128)(2,1)S(1)}, u32[]{:S(2)}, u32[]{:S(2)}) %collective-permute-start.11) | collective-permute-done | bytes 663584 | tf_op jit(solution)/shard_map/ppermute | solution.py:1182
  477.1 0.7 slice.62
  477.8 1.1 slice_bitcast_fusion
  478.9 2.5 all-gather.8.cloned.1.call-done
  481.4 1.4 copy.40
  482.8 1.5 dynamic-slice_reduce_fusion
  484.3 1.5 dynamic-slice_reduce_fusion.1
  485.9 1.6 fusion.39
  487.5 1.4 fusion.2
  489.0 0.6 collective-permute-start.4
  489.6 3.2 collective-permute-start.6
  492.8 1.0 fusion.14
  493.8 5.3 %collective-permute-done.4 = bf16[48,2304]{1,0:T(8,128)(2,1)S(1)} collective-permute-done((bf16[48,2304]{1,0:T(8,128)(2,1)S(1)}, bf16[48,2304]{1,0:T(8,128)(2,1)S(1)}, u32[]{:S(2)}, u32[]{:S(2)}) %collective-permute-start.4) | collective-permute-done | bytes 221216 | tf_op jit(solution)/shard_map/ppermute | solution.py:1215
  499.1 2.7 collective-permute-done.6
  501.8 9.9 %collective-permute-done.5 = bf16[48,2304]{1,0:T(8,128)(2,1)S(1)} collective-permute-done((bf16[48,2304]{1,0:T(8,128)(2,1)S(1)}, bf16[48,2304]{1,0:T(8,128)(2,1)S(1)}, u32[]{:S(2)}, u32[]{:S(2)}) %collective-permute-start.5) | collective-permute-done | bytes 221216 | tf_op jit(solution)/shard_map/ppermute | solution.py:1215
  511.8 1.4 collective-permute-start.7
  513.2 0.8 fusion.17
  514.0 4.7 collective-permute-done.7
  518.6 0.8 convert_add_fusion.6
  (79 shorter events, 2.6 us)
Async XLA Ops:
  7.2 7.3 %copy-start = (bf16[128,4608]{1,0:T(8,128)(2,1)S(1)}, bf16[128,4608]{1,0:T(8,128)(2,1)}, u32[]{:S(2)}) copy-start(bf16[128,4608]{1,0:T(8,128)(2,1)} %param.17) | copy-start | bytes 3538948
  7.2 108.2 %all-gather.6.cloned.1.call-start = ((), (), s32[]{:S(2)}) async-start(), calls=%async_computation | async-start | bytes 11919360 | tf_op jit(solution)/shard_map/all_gather | solution.py:1238
  11.2 0.7 copy-start.15
  11.2 2.6 copy-start.14
  11.2 2.6 copy-start.10
  11.2 2.6 copy-start.12
  11.2 4.3 copy-start.8
  11.3 470.1 %all-gather.8.cloned.1.call-start = ((), (), s32[]{:S(2)}) async-start(), calls=%async_computation.1 | async-start | bytes 1368576 | tf_op jit(solution)/shard_map/all_gather | solution.py:1324
  15.5 0.6 copy-start.3
  166.8 19.9 %collective-permute-start = (bf16[2,4,432,768]{3,2,1,0:T(8,128)(2,1)}, bf16[2,4,432,768]{3,2,1,0:T(8,128)(2,1)}, u32[]{:S(2)}, u32[]{:S(2)}) collective-permute-start(bf16[2,4,432,768]{3,2,1,0:T(8,128)(2,1)} %weight_grads.3), channel_id=1, source_target_pairs={{0,1},{1,0},{2,3},{3,2},{4,5},{5,4},{6,7},{7,6},{8,9},{9,8},{10,11... | collective-permute-start | bytes 15925256 | tf_op jit(solution)/shard_map/ppermute | solution.py:1182
  169.2 3.4 copy-start.9
  192.0 2.3 copy-start.1
  194.3 141.7 %collective-permute-start.1 = (bf16[4,432,768]{2,1,0:T(8,128)(2,1)S(1)}, bf16[4,432,768]{2,1,0:T(8,128)(2,1)}, u32[]{:S(2)}, u32[]{:S(2)}) collective-permute-start(bf16[4,432,768]{2,1,0:T(8,128)(2,1)S(1)} %dynamic-slice_bitcast_fusion), channel_id=1, source_target_pairs={{0,2},{1,3},{2,0},{3,1},{4,6},{5,7},{6,4},{7,5},{8,10},{9,11},{10,... | collective-permute-start | bytes 7962632 | tf_op jit(solution)/shard_map/ppermute | solution.py:1182
  339.3 28.0 %copy-start.2 = (bf16[4,432,768]{2,1,0:T(8,128)(2,1)}, bf16[4,432,768]{2,1,0:T(8,128)(2,1)S(1)}, u32[]{:S(2)}) copy-start(bf16[4,432,768]{2,1,0:T(8,128)(2,1)S(1)} %fusion) | copy-start | bytes 7962628
  348.8 11.1 %copy-start.5 = (f32[10368]{0:T(1024)S(1)}, f32[10368]{0:T(1024)}, u32[]{:S(2)}) copy-start(f32[10368]{0:T(1024)} %custom-call) | copy-start | bytes 124420
  348.8 11.1 %copy-start.6 = (f32[4608]{0:T(1024)S(1)}, f32[4608]{0:T(1024)}, u32[]{:S(2)}) copy-start(f32[4608]{0:T(1024)} %custom-call.1) | copy-start | bytes 55300
  348.8 11.1 %copy-start.11 = (bf16[768]{0:T(1024)(128)(2,1)S(1)}, bf16[768]{0:T(1024)(128)(2,1)}, u32[]{:S(2)}) copy-start(bf16[768]{0:T(1024)(128)(2,1)} %param.19) | copy-start | bytes 4612
  348.8 11.2 %copy-start.13 = (bf16[768]{0:T(1024)(128)(2,1)S(1)}, bf16[768]{0:T(1024)(128)(2,1)}, u32[]{:S(2)}) copy-start(bf16[768]{0:T(1024)(128)(2,1)} %param.22) | copy-start | bytes 4612
  367.2 5.5 %copy-start.4 = (f32[1,3072]{1,0:T(1,128)S(1)}, f32[1,3072]{1,0:T(1,128)}, u32[]{:S(2)}) copy-start(f32[1,3072]{1,0:T(1,128)} %slice.51) | copy-start | bytes 36868
  367.2 5.5 %copy-start.7 = (f32[768]{0:T(1024)S(1)}, f32[768]{0:T(1024)}, u32[]{:S(2)}) copy-start(f32[768]{0:T(1024)} %get-tuple-element.64) | copy-start | bytes 9220
  367.2 92.3 %collective-permute-start.2 = (bf16[2,4,48,2304]{3,2,1,0:T(8,128)(2,1)}, bf16[2,4,48,2304]{3,2,1,0:T(8,128)(2,1)}, u32[]{:S(2)}, u32[]{:S(2)}) collective-permute-start(bf16[2,4,48,2304]{3,2,1,0:T(8,128)(2,1)} %bitcast.32), channel_id=1, source_target_pairs={{0,1},{1,0},{2,3},{3,2},{4,5},{5,4},{6,7},{7,6},{8,9},{9,8},{10,11... | collective-permute-start | bytes 5308424 | tf_op jit(solution)/shard_map/ppermute | solution.py:1182
  368.6 19.8 %collective-permute-start.8 = (bf16[432,768]{1,0:T(8,128)(2,1)}, bf16[432,768]{1,0:T(8,128)(2,1)S(1)}, u32[]{:S(2)}, u32[]{:S(2)}) collective-permute-start(bf16[432,768]{1,0:T(8,128)(2,1)} %get-tuple-element.73), channel_id=1, source_target_pairs={{0,4},{4,8},{8,12},{12,0},{1,5},{5,9},{9,13},{13,1},{2,6},{6,10},{... | collective-permute-start | bytes 1990664 | tf_op jit(solution)/shard_map/ppermute | solution.py:1215
  371.1 31.0 %collective-permute-start.10 = (bf16[432,768]{1,0:T(8,128)(2,1)}, bf16[432,768]{1,0:T(8,128)(2,1)S(1)}, u32[]{:S(2)}, u32[]{:S(2)}) collective-permute-start(bf16[432,768]{1,0:T(8,128)(2,1)} %get-tuple-element.74), channel_id=1, source_target_pairs={{0,12},{4,0},{8,4},{12,8},{1,13},{5,1},{9,5},{13,9},{2,14},{6,2},{... | collective-permute-start | bytes 1990664 | tf_op jit(solution)/shard_map/ppermute | solution.py:1215
  372.6 58.9 %collective-permute-start.9 = (bf16[432,768]{1,0:T(8,128)(2,1)}, bf16[432,768]{1,0:T(8,128)(2,1)S(1)}, u32[]{:S(2)}, u32[]{:S(2)}) collective-permute-start(bf16[432,768]{1,0:T(8,128)(2,1)} %get-tuple-element.75), channel_id=1, source_target_pairs={{0,8},{4,12},{8,0},{12,4},{1,9},{5,13},{9,1},{13,5},{2,10},{6,14},... | collective-permute-start | bytes 1990664 | tf_op jit(solution)/shard_map/ppermute | solution.py:1215
  432.9 44.0 %collective-permute-start.11 = (bf16[432,768]{1,0:T(8,128)(2,1)S(1)}, bf16[432,768]{1,0:T(8,128)(2,1)S(1)}, u32[]{:S(2)}, u32[]{:S(2)}) collective-permute-start(bf16[432,768]{1,0:T(8,128)(2,1)S(1)} %fusion.5), channel_id=1, source_target_pairs={{0,16},{16,0},{1,17},{17,1},{2,18},{18,2},{3,19},{19,3},{4,20},{20... | collective-permute-start | bytes 1990664 | tf_op jit(solution)/shard_map/ppermute | solution.py:1182
  462.5 25.1 %collective-permute-start.3 = (bf16[4,48,2304]{2,1,0:T(8,128)(2,1)}, bf16[4,48,2304]{2,1,0:T(8,128)(2,1)}, u32[]{:S(2)}, u32[]{:S(2)}) collective-permute-start(bf16[4,48,2304]{2,1,0:T(8,128)(2,1)} %dynamic-slice_bitcast_fusion.1), channel_id=1, source_target_pairs={{0,2},{1,3},{2,0},{3,1},{4,6},{5,7},{6,4},{7,5},{8,10},{9,11},{10,... | collective-permute-start | bytes 2654216 | tf_op jit(solution)/shard_map/ppermute | solution.py:1182
  489.0 10.2 %collective-permute-start.4 = (bf16[48,2304]{1,0:T(8,128)(2,1)S(1)}, bf16[48,2304]{1,0:T(8,128)(2,1)S(1)}, u32[]{:S(2)}, u32[]{:S(2)}) collective-permute-start(bf16[48,2304]{1,0:T(8,128)(2,1)S(1)} %get-tuple-element.78), channel_id=1, source_target_pairs={{0,4},{4,8},{8,12},{12,0},{1,5},{5,9},{9,13},{13,1},{2,6},{6,10},{... | collective-permute-start | bytes 663560 | tf_op jit(solution)/shard_map/ppermute | solution.py:1215
  489.6 12.2 %collective-permute-start.6 = (bf16[48,2304]{1,0:T(8,128)(2,1)S(1)}, bf16[48,2304]{1,0:T(8,128)(2,1)S(1)}, u32[]{:S(2)}, u32[]{:S(2)}) collective-permute-start(bf16[48,2304]{1,0:T(8,128)(2,1)S(1)} %get-tuple-element.79), channel_id=1, source_target_pairs={{0,12},{4,0},{8,4},{12,8},{1,13},{5,1},{9,5},{13,9},{2,14},{6,2},{... | collective-permute-start | bytes 663560 | tf_op jit(solution)/shard_map/ppermute | solution.py:1215
  492.8 18.8 %collective-permute-start.5 = (bf16[48,2304]{1,0:T(8,128)(2,1)S(1)}, bf16[48,2304]{1,0:T(8,128)(2,1)S(1)}, u32[]{:S(2)}, u32[]{:S(2)}) collective-permute-start(bf16[48,2304]{1,0:T(8,128)(2,1)S(1)} %get-tuple-element.80), channel_id=1, source_target_pairs={{0,8},{4,12},{8,0},{12,4},{1,9},{5,13},{9,1},{13,5},{2,10},{6,14},... | collective-permute-start | bytes 663560 | tf_op jit(solution)/shard_map/ppermute | solution.py:1215
  511.8 6.9 %collective-permute-start.7 = (bf16[48,2304]{1,0:T(8,128)(2,1)S(1)}, bf16[48,2304]{1,0:T(8,128)(2,1)S(1)}, u32[]{:S(2)}, u32[]{:S(2)}) collective-permute-start(bf16[48,2304]{1,0:T(8,128)(2,1)S(1)} %fusion.12), channel_id=1, source_target_pairs={{0,16},{16,0},{1,17},{17,1},{2,18},{18,2},{3,19},{19,3},{4,20},{20... | collective-permute-start | bytes 663560 | tf_op jit(solution)/shard_map/ppermute | solution.py:1182
Sparse Core Ops, SparseCore 0:
  11.4 67.4 all-gather.5
  376.0 105.3 all-gather.7

commit v3 on v2

--- a/solution.py
+++ b/solution.py
@@ -460,24 +460,147 @@
     return jnp.concatenate([value, swap_heads(value)]).astype(BF16)
 
 
-def reach(src, dst, sems, index, group, place):
+def push(src, dst, sems, index, where):
     return pltpu.make_async_remote_copy(
         src_ref=src, dst_ref=dst, send_sem=sems[0].at[index], recv_sem=sems[1].at[index],
-        device_id={"grp": group, "seq": place}, device_id_type=pl.DeviceIdType.MESH,
-    )
-
-
-def greet(group, place):
+        device_id=where, device_id_type=pl.DeviceIdType.MESH,
+    )
+
+
+def reach(src, dst, sems, index, group, place):
+    return push(src, dst, sems, index, {"grp": group, "seq": place})
+
+
+def neighbours(group, place, others):
+    found = [
+        {"grp": (group + other) % 2, "seq": (place + steps) % 4}
+        for other in range(2)
+        for steps in range(4)
+        if other or steps
+    ]
+    return found + [{"mlp": other} for other in others]
+
+
+def greet(devices):
     barrier = pltpu.get_barrier_semaphore()
-    for other in range(2):
-        for steps in range(4):
-            if other or steps:
-                pl.semaphore_signal(
-                    barrier, 1,
-                    device_id={"grp": (group + other) % 2, "seq": (place + steps) % 4},
-                    device_id_type=pl.DeviceIdType.MESH,
-                )
-    pl.semaphore_wait(barrier, 7)
+    for where in devices:
+        pl.semaphore_signal(barrier, 1, device_id=where, device_id_type=pl.DeviceIdType.MESH)
+    pl.semaphore_wait(barrier, len(devices))
+
+
+def mlp_place():
+    mlp = lax.axis_index("mlp")
+    row, core = mlp // 2, mlp % 2
+    return row, core, (1 - row) * 2 + core, row * 2 + 1 - core
+
+
+BLOCKS = 18
+
+
+def added(left, right):
+    return (left.astype(F32) + right.astype(F32)).astype(BF16)
+
+
+def sum_steps(held, one_p, one_q, two, others, three, out, sems, base):
+    group = lax.axis_index("grp")
+    place = lax.axis_index("seq")
+    row, _, other_row, _ = mlp_place()
+    by_row = {"mlp": other_row}
+    by_group = {"grp": 1 - group}
+    ahead = lambda s: (place + s) % 4
+
+    def copies(stage):
+        if stage == 1:
+            return [
+                push(held.at[1 - row, :, pl.ds(0, 10)], one_p, sems, base, by_row),
+                push(
+                    held.at[:, :, pl.ds(10 + 4 * (1 - group), 4)], one_q, sems, base + 1, by_group
+                ),
+            ]
+        if stage == 2:
+            return [
+                push(
+                    one_p.at[:, pl.ds(5 * (1 - group), 5)], two.at[:, pl.ds(0, 5)], sems,
+                    base + 2, by_group,
+                ),
+                push(one_q.at[1 - row], two.at[:, pl.ds(5, 4)], sems, base + 3, by_row),
+            ]
+        if stage == 3:
+            return [
+                push(two.at[ahead(s)], others.at[s - 1], sems, base + 3 + s, {"seq": ahead(s)})
+                for s in (1, 2, 3)
+            ]
+        return [
+            push(three.at[pl.ds(0, 5)], out.at[pl.ds(5 * group, 5)], sems, base + 7, by_group),
+            push(
+                three.at[pl.ds(5, 4)], out.at[pl.ds(10 + 4 * group, 4)], sems, base + 8, by_group
+            ),
+        ]
+
+    def start(stage):
+        for copy in copies(stage):
+            copy.start()
+
+    def arrive(stage):
+        for copy in copies(stage):
+            copy.wait()
+
+    def step_one():
+        start(1)
+
+    def step_two():
+        arrive(1)
+
+        def add(z, carry):
+            one_p[z] = added(held[row, z, 0:10], one_p[z])
+            for y in range(2):
+                one_q[y, z] = added(held[y, z, pl.ds(10 + 4 * group, 4)], one_q[y, z])
+            return carry
+
+        lax.fori_loop(0, 4, add, 0)
+        start(2)
+
+    def step_three():
+        arrive(2)
+
+        def add(z, carry):
+            two[z, 0:5] = added(one_p[z, pl.ds(5 * group, 5)], two[z, 0:5])
+            two[z, 5:9] = added(one_q[row, z], two[z, 5:9])
+            return carry
+
+        lax.fori_loop(0, 4, add, 0)
+
+    def step_over():
+        start(3)
+
+    def step_four():
+        arrive(3)
+
+        def add(block, carry):
+            total = two[place, block].astype(F32)
+            for s in range(3):
+                total = total + others[s, block].astype(F32)
+            three[block] = total.astype(BF16)
+            return carry
+
+        lax.fori_loop(0, 9, add, 0)
+        start(4)
+        out[pl.ds(5 * group, 5)] = three[0:5]
+        out[pl.ds(10 + 4 * group, 4)] = three[5:9]
+
+    def step_five():
+        arrive(4)
+
+    return step_one, step_two, step_three, step_over, step_four, step_five
+
+
+def sum_scratch(rows, shapes):
+    return [pltpu.VMEM(shape + (rows, 2 * HD), BF16) for shape in shapes]
+
+
+EARLY = [(4, 10), (2, 4, 4)]
+MIDDLE = [(4, 9)]
+LATE = [(3, 9), (9,)]
 
 
 def forward_kernel(
@@ -514,7 +637,7 @@
             results.at[min(kind, 1), s], att.at[head], sems, start + s, 1, behind(s)
         )
 
-    greet(group, place)
+    greet(neighbours(group, place, []))
 
     def full(kind, head, before, after):
         sel = min(kind, 1)
@@ -701,8 +824,9 @@
 
 
 def backward_kernel(
-    packs, gatt, att, pieces, results, logs, logs_own, back,
-    dos, crossed, staged, q_s, k_s, v_s, do_s, delta_s, dq_s, send_sems, recv_sems,
+    packs, gatt, att, pieces, results, logs, logs_own, dos, held, back, two,
+    staged, q_s, k_s, v_s, do_s, delta_s, dq_s, one_p, one_q,
+    send_sems, recv_sems,
 ):
     group = lax.axis_index("grp")
     place = lax.axis_index("seq")
@@ -714,29 +838,21 @@
     behind = lambda s: (place + 4 - s) % 4
     stores = (q_s, k_s, v_s, do_s, delta_s)
 
-    def first(s):
-        return reach(gatt.at[2 * ahead(s)], dos.at[0, s], sems, s - 1, 1, ahead(s))
-
-    def second(s):
-        return reach(gatt.at[2 * ahead(s) + 1], dos.at[1, s], sems, 2 + s, 1, ahead(s))
-
-    def cross(s):
-        return reach(gatt.at[8 + ahead(s)], crossed.at[s], sems, 6 + s, 0, place)
-
-    def onward(s):
-        return reach(crossed.at[s], dos.at[1, s], sems, 9 + s, 0, ahead(s))
-
     def home_values(kind, s, head):
         source = staged.at[min(kind, 1), s, pl.ds(1, 2)]
         return reach(
-            source, back.at[head, pl.ds(1, 2)], sems, (13, 17, 21)[kind] + s, 1, behind(s)
+            source, back.at[head, pl.ds(1, 2)], sems, (0, 4, 8)[kind] + s, 1, behind(s)
         )
 
     def home_queries(kind, s, head):
         source = staged.at[min(kind, 1), s, 0]
-        return reach(source, back.at[head, 0], sems, (25, 29, 33)[kind] + s, 1, behind(s))
-
-    greet(group, place)
+        return reach(source, back.at[head, 0], sems, (12, 16, 20)[kind] + s, 1, behind(s))
+
+    greet(neighbours(group, place, [mlp_place()[2]]))
+    sum_one, sum_two, sum_three, _, _, _ = sum_steps(
+        held, one_p, one_q, two, None, None, None, sems, 24
+    )
+    sum_one()
 
     def full(sel, put_values, put_queries):
         for s in range(4):
@@ -771,16 +887,6 @@
 
     @pl.when(group == 1)
     def _():
-        for s in (1, 2, 3):
-            first(s).start()
-        for s in (1, 2, 3, 0):
-            cross(s).start()
-        for s in (1, 2, 3):
-            second(s).start()
-        dos[0, 0] = gatt[2 * place]
-        dos[1, 0] = gatt[2 * place + 1]
-        for s in (1, 2, 3):
-            first(s).wait_recv()
         head = 2 * place
 
         def put_values(s):
@@ -793,6 +899,10 @@
             def _():
                 home_values(0, s, head).start()
 
+            @pl.when(s == 2)
+            def _():
+                sum_two()
+
         def put_queries(s):
             if s == 0:
                 back[head, 0] = staged[0, 0, 0]
@@ -800,18 +910,6 @@
                 home_queries(0, s, head).start()
 
         full(0, put_values, put_queries)
-        for s in (1, 2, 3):
-            second(s).wait_recv()
-
-    @pl.when(group == 0)
-    def _():
-        for s in (1, 2, 3):
-            cross(s).wait_recv()
-            onward(s).start()
-        cross(0).wait_recv()
-        dos[1, 0] = crossed[0]
-        for s in (1, 2, 3):
-            onward(s).wait_recv()
 
     def put_values(s):
         head = 2 * place + 1
@@ -828,6 +926,10 @@
         @pl.when(group == 0)
         def _():
             home_values(2, s, 8 + place).start()
+
+        @pl.when((group == 0) & (s == 2))
+        def _():
+            sum_two()
 
     def put_queries(s):
         head = 2 * place + 1
@@ -860,8 +962,11 @@
             return carry
 
         lax.fori_loop(0, heads, local, 0)
-        for s in (1, 2, 3):
-            onward(s).wait_send()
+
+    sum_three()
+
+    @pl.when(group == 0)
+    def _():
         for s in range(4):
             home_values(2, s, 8 + place).wait_send()
             home_queries(2, s, 8 + place).wait_send()
@@ -869,13 +974,9 @@
     @pl.when(group == 1)
     def _():
         for s in (1, 2, 3):
-            first(s).wait_send()
-            second(s).wait_send()
             for kind in (0, 1):
                 home_values(kind, s, 2 * place + kind).wait_send()
                 home_queries(kind, s, 2 * place + kind).wait_send()
-        for s in range(4):
-            cross(s).wait_send()
         for s in (1, 2, 3):
             for kind in (0, 1):
                 home_values(kind, s, 2 * ahead(s) + kind).wait_recv()
@@ -885,25 +986,22 @@
             home_queries(2, s, 8 + ahead(s)).wait_recv()
 
 
-def backward_attention(packs, gatt, att, pieces, results, logs, logs_own):
+def backward_attention(packs, gatt, att, pieces, results, logs, logs_own, dos, held):
     heads, _, half, lanes = packs.shape
+    share = held.shape[2:]
     return pl.pallas_call(
         backward_kernel,
-        in_specs=in_vmem(7),
-        out_specs=pl.BlockSpec(memory_space=pltpu.VMEM),
-        out_shape=jax.ShapeDtypeStruct((heads, 3, half, lanes), BF16),
-        scratch_shapes=[
-            pltpu.VMEM((2, 4, half, lanes), BF16),
-            pltpu.VMEM((4, half, lanes), BF16),
-            pltpu.VMEM((2, 4, 3, half, lanes), BF16),
-        ]
+        in_specs=in_vmem(9),
+        out_specs=in_vmem(2),
+        out_shape=[
+            jax.ShapeDtypeStruct((heads, 3, half, lanes), BF16),
+            jax.ShapeDtypeStruct((4, 9) + share[1:], BF16),
+        ],
+        scratch_shapes=[pltpu.VMEM((2, 4, 3, half, lanes), BF16)]
         + [pltpu.VMEM((8 * half, lanes), BF16)] * 4
-        + [
-            pltpu.VMEM((8, 8 * half), F32),
-            pltpu.VMEM((lanes, 8 * half), F32),
-            pltpu.SemaphoreType.DMA((37,)),
-            pltpu.SemaphoreType.DMA((37,)),
-        ],
+        + [pltpu.VMEM((8, 8 * half), F32), pltpu.VMEM((lanes, 8 * half), F32)]
+        + sum_scratch(share[1], EARLY)
+        + [pltpu.SemaphoreType.DMA((28,)), pltpu.SemaphoreType.DMA((28,))],
         compiler_params=pltpu.CompilerParams(
             collective_id=2, has_side_effects=True, vmem_limit_bytes=WHOLE_VMEM
         ),
@@ -911,7 +1009,7 @@
             flops=120_000_000_000, bytes_accessed=8_000_000, transcendentals=0
         ),
         name="backward_attention",
-    )(packs, gatt, att, pieces, results, logs, logs_own)
+    )(packs, gatt, att, pieces, results, logs, logs_own, dos, held)
 
 
 def whole(shape):
@@ -1043,180 +1141,386 @@
     )(x2, cot2, att, vecs, out_weight, feed_weights)
 
 
-def unrotate_kernel(pack_ref, cos_ref, sin_ref, mixed_ref):
-    rows = cos_ref.shape[1]
-    cosine = cos_ref[...].reshape(2 * rows, 2 * HD)
-    sine = -sin_ref[...].reshape(2 * rows, 2 * HD)
-    heads = pack_ref.shape[0]
-    width = heads * HD
-    for part in range(3):
-        for pair in range(heads // 2):
-            top, bottom = exchange(
-                pack_ref[2 * pair, part].astype(F32), pack_ref[2 * pair + 1, part].astype(F32)
-            )
-            value = jnp.concatenate([top, bottom], axis=0)
-            if part < 2:
-                value = turn(value, cosine, sine)
-            start = part * width + pair * 2 * HD
-            mixed_ref[:, :, start : start + 2 * HD] = value.astype(BF16).reshape(2, rows, 2 * HD)
-
-
-def unrotate(packs, cosine, sine, rows=128):
-    heads, _, half, lanes = packs.shape
-    tok = lambda last: pl.BlockSpec((2, rows, last), lambda i: (0, i, 0))
-    return pl.pallas_call(
-        unrotate_kernel,
-        grid=(half // rows,),
-        in_specs=[
-            pl.BlockSpec((heads, 3, rows, lanes), lambda i: (0, 0, i, 0)),
-            tok(lanes),
-            tok(lanes),
-        ],
-        out_specs=tok(3 * heads * HD),
-        out_shape=jax.ShapeDtypeStruct((2, half, 3 * heads * HD), BF16),
-        compiler_params=params("arbitrary"),
-        name="unrotate",
-    )(packs, cosine, sine)
-
-
-def input_kernel(mixed_ref, w_ref, x_ref, mgrad_ref, vec_ref, grad_ref, sums_ref):
-    step = pl.program_id(0)
-    rows, width = x_ref.shape[1:]
-    both = 2 * rows
-    gnormed = lax.dot_general(
-        mixed_ref[...].reshape(both, mixed_ref.shape[2]), w_ref[...], NT,
-        preferred_element_type=F32,
-    )
-    n, inverse = normalise(x_ref[...].reshape(both, width).astype(F32))
-    e = gnormed * ((1.0 + vec_ref[1:2, :]) * vec_ref[0:1, :])
-    grad = mgrad_ref[...].reshape(both, width) + inverse * (
-        e - jnp.mean(e, axis=-1, keepdims=True) - n * jnp.mean(e * n, axis=-1, keepdims=True)
-    )
-    grad_ref[...] = grad.reshape(2, rows, width)
-
-    @pl.when(step == 0)
+def feed_grads_kernel(
+    hidden_ref, gfeed_ref, att_ref, gbranch_ref, act_ref, gpre_ref, gatt, held, dos,
+    hidden_s, gfeed_s, att_s, sent, got, crossed, send_sems, recv_sems,
+):
+    group = lax.axis_index("grp")
+    place = lax.axis_index("seq")
+    _, core, _, other_core = mlp_place()
+    sems = (send_sems, recv_sems)
+    ahead = lambda s: (place + s) % 4
+
+    def first(s):
+        return reach(gatt.at[2 * ahead(s)], dos.at[0, s], sems, s - 1, 1, ahead(s))
+
+    def second(s):
+        return reach(gatt.at[2 * ahead(s) + 1], dos.at[1, s], sems, 2 + s, 1, ahead(s))
+
+    def cross(s):
+        return reach(gatt.at[8 + ahead(s)], crossed.at[s], sems, 6 + s, 0, place)
+
+    def onward(s):
+        return reach(crossed.at[s], dos.at[1, s], sems, 9 + s, 0, ahead(s))
+
+    def swap(y):
+        return push(sent.at[y], got.at[y], sems, 13 + y, {"mlp": other_core})
+
+    greet(neighbours(group, place, [other_core]))
+
+    @pl.when(group == 1)
     def _():
-        sums_ref[...] = jnp.zeros_like(sums_ref)
-
-    sums_ref[0:1, :] += jnp.sum(gnormed, axis=0, keepdims=True)
-    sums_ref[1:2, :] += jnp.sum(gnormed * n, axis=0, keepdims=True)
-
-
-def input_pass(mixed, weight, x2, mgrad, vecs, rows=128):
-    half, width = x2.shape[1:]
-    tok = lambda last: pl.BlockSpec((2, rows, last), lambda i: (0, i, 0))
-    return pl.pallas_call(
-        input_kernel,
-        grid=(half // rows,),
-        in_specs=[
-            tok(mixed.shape[2]), once(weight.shape), tok(width), tok(width), whole(vecs.shape)
-        ],
-        out_specs=[tok(width), whole((8, width))],
-        out_shape=[
-            jax.ShapeDtypeStruct((2, half, width), F32),
-            jax.ShapeDtypeStruct((8, width), F32),
-        ],
-        compiler_params=params("arbitrary"),
-        cost_estimate=pl.CostEstimate(
-            flops=6_000_000_000, bytes_accessed=20_000_000, transcendentals=0
-        ),
-        name="input_pass",
-    )(mixed, weight, x2, mgrad, vecs)
-
-
-def weight_grads_kernel(
-    pick_ref, hidden_ref, gfeed_ref, att_ref, gbranch_ref, act_ref, gpre_ref, out_ref,
-    hidden_s, gfeed_s, att_s,
-):
-    step = pl.program_id(0)
-
-    @pl.when(step == 0)
-    def _():
-        hidden_s[...] = hidden_ref[...].T
-        gfeed_s[...] = gfeed_ref[...].T
-        att_s[...] = att_ref[...].T
-
+        for s in (1, 2, 3):
+            cross(s).start()
+            first(s).start()
+            second(s).start()
+        cross(0).start()
+        dos[0, 0] = gatt[2 * place]
+        dos[1, 0] = gatt[2 * place + 1]
+
+    hidden_s[...] = hidden_ref[...].T
+    gfeed_s[...] = gfeed_ref[...].T
+    att_s[...] = att_ref[...].T
     width = hidden_s.shape[0]
     split = width // 4
     part = split // 4
-    up = jnp.dot(hidden_s[...], gpre_ref[...], preferred_element_type=F32).astype(BF16)
-    down = jnp.dot(gfeed_s[...], act_ref[...], preferred_element_type=F32).astype(BF16)
-    offset = pick_ref[step] * part
-    rows = jnp.concatenate(
-        [
-            att_s[pl.ds(pl.multiple_of(offset + index * split, 16), part), :]
-            for index in range(4)
+    rows = 3 * part
+
+    def blocks(target, y, index):
+        cols = pl.ds(pl.multiple_of(index * width, width), width)
+        up = jnp.dot(hidden_s[...], gpre_ref[:, cols], preferred_element_type=F32).astype(BF16)
+        down = jnp.dot(gfeed_s[...], act_ref[:, cols], preferred_element_type=F32).astype(BF16)
+        own = jnp.concatenate(
+            [
+                att_s[pl.ds(pl.multiple_of(index * part + z * split, 16), part), :]
+                for z in range(4)
+            ]
+        )
+        out = jnp.dot(own, gbranch_ref[...], preferred_element_type=F32).astype(BF16)
+        for z in range(4):
+            start = z * split
+            pieces = (
+                (up[start : start + rows],),
+                (up[start + rows : start + split], down[start : start + split - rows + part]),
+                (down[start + 2 * part : start + split], out[z * part : (z + 1) * part]),
+            )
+            for number, values in enumerate(pieces):
+                base = 0
+                for value in values:
+                    size = value.shape[0]
+                    for lane in range(width // (2 * HD)):
+                        target[y, z, number * 6 + lane, base : base + size, :] = value[
+                            :, lane * 2 * HD : (lane + 1) * 2 * HD
+                        ]
+                    base += size
+
+    def send_row(y, carry):
+        blocks(sent, y, 2 * y + 1 - core)
+        swap(y).start()
+        return carry
+
+    lax.fori_loop(0, 2, send_row, 0)
+
+    @pl.when(group == 0)
+    def _():
+        for s in (1, 2, 3):
+            cross(s).wait_recv()
+            onward(s).start()
+        cross(0).wait_recv()
+        dos[1, 0] = crossed[0]
+
+    def keep_row(y, carry):
+        blocks(held, y, 2 * y + core)
+        return carry
+
+    lax.fori_loop(0, 2, keep_row, 0)
+
+    def add_row(y, carry):
+        swap(y).wait()
+
+        def add(z, inner):
+            held[y, z] = added(held[y, z], got[y, z])
+            return inner
+
+        return lax.fori_loop(0, 4, add, carry)
+
+    lax.fori_loop(0, 2, add_row, 0)
+
+    @pl.when(group == 1)
+    def _():
+        for s in (1, 2, 3):
+            first(s).wait()
+            second(s).wait()
+        for s in range(4):
+            cross(s).wait_send()
+
+    @pl.when(group == 0)
+    def _():
+        for s in (1, 2, 3):
+            onward(s).wait()
+
+
+def feed_grads(hidden, gfeed, att, gbranch, act, gpre, gatt):
+    tokens, width = hidden.shape
+    _, half, lanes = gatt.shape
+    rows = 3 * width // 16
+    share = (2, 4, BLOCKS, rows, lanes)
+    return pl.pallas_call(
+        feed_grads_kernel,
+        in_specs=in_vmem(7),
+        out_specs=in_vmem(2),
+        out_shape=[
+            jax.ShapeDtypeStruct(share, BF16),
+            jax.ShapeDtypeStruct((2, 4, half, lanes), BF16),
+        ],
+        scratch_shapes=[pltpu.VMEM((width, tokens), BF16)] * 3
+        + [
+            pltpu.VMEM(share, BF16),
+            pltpu.VMEM(share, BF16),
+            pltpu.VMEM((4, half, lanes), BF16),
+            pltpu.SemaphoreType.DMA((15,)),
+            pltpu.SemaphoreType.DMA((15,)),
+        ],
+        compiler_params=pltpu.CompilerParams(
+            collective_id=3, has_side_effects=True, vmem_limit_bytes=WHOLE_VMEM
+        ),
+        cost_estimate=pl.CostEstimate(
+            flops=24_000_000_000, bytes_accessed=20_000_000, transcendentals=0
+        ),
+        name="feed_grads",
+    )(hidden, gfeed, att, gbranch, act, gpre, gatt)
+
+
+SMALL_ROWS = 40
+
+
+def finish_kernel(
+    packs, cosine, sine, normed_ref, vec_one, vec_two, middle_sums, up_sums, extra, feed_two,
+    w_ref, x_ref, mgrad_ref, ada_ref, total, feed_total, rows_all, grad_ref,
+    mixed, w_s, x_s, mgrad_s, ada_s, sums, small, sent, got, held, one_p, one_q, two, others,
+    three, feed_others, feed_three, send_sems, recv_sems, own_sems,
+):
+    group = lax.axis_index("grp")
+    place = lax.axis_index("seq")
+    row, core, _, other_core = mlp_place()
+    mlp = row * 2 + core
+    sems = (send_sems, recv_sems)
+    ahead = lambda s: (place + s) % 4
+    heads = packs.shape[0]
+    half = packs.shape[2]
+    width = heads * HD
+    lanes = 2 * HD
+    parts = 3
+    each = BLOCKS // parts
+
+    loads = [
+        pltpu.make_async_copy(source, target, own_sems.at[index])
+        for index, (source, target) in enumerate(
+            ((w_ref, w_s), (x_ref, x_s), (mgrad_ref, mgrad_s), (ada_ref, ada_s))
+        )
+    ]
+    for load in loads:
+        load.start()
+    greet(
+        [{"seq": ahead(s)} for s in (1, 2, 3)]
+        + [{"mlp": (mlp + s) % 4} for s in (1, 2, 3)]
+        + [{"grp": 1 - group}]
+    )
+    _, _, _, feed_over, feed_four, feed_five = sum_steps(
+        None, None, None, feed_two, feed_others, feed_three, feed_total, sems, 0
+    )
+    sum_one, sum_two, sum_three, sum_over, sum_four, sum_five = sum_steps(
+        held, one_p, one_q, two, others, three, total, sems, 9
+    )
+    feed_over()
+
+    def swap(index):
+        own = pl.ds(index * each, each)
+        return push(
+            sent.at[:, :, own], got.at[:, :, own], sems, 18 + index, {"mlp": other_core}
+        )
+
+    def unrotate(part):
+        def one_pair(pair, carry):
+            top, bottom = exchange(
+                packs[2 * pair, part].astype(F32), packs[2 * pair + 1, part].astype(F32)
+            )
+            if part < 2:
+                top = turn(top, cosine[0], -sine[0])
+                bottom = turn(bottom, cosine[1], -sine[1])
+            cols = pl.ds(pl.multiple_of(part * width + pair * lanes, lanes), lanes)
+            mixed[:half, cols] = top.astype(BF16)
+            mixed[half:, cols] = bottom.astype(BF16)
+            return carry
+
+        lax.fori_loop(0, heads // 2, one_pair, 0)
+
+    def blocks(target, which, index):
+        value = jnp.dot(
+            normed_ref[which], mixed[:, index * width : (index + 1) * width],
+            preferred_element_type=F32,
+        ).astype(BF16)
+        for lane in range(each):
+            target[:, :, index * each + lane] = value[
+                :, lane * lanes : (lane + 1) * lanes
+            ].reshape(2, 4, width // 16, lanes)
+
+    for index in (2, 0, 1):
+        unrotate(index)
+        blocks(sent, 1 - core, index)
+        swap(index).start()
+    for index in range(parts):
+        blocks(held, core, index)
+    for index in range(parts):
+        swap(index).wait()
+    for y in range(2):
+
+        def add(z, carry, y=y):
+            held[y, z] = added(held[y, z], got[y, z])
+            return carry
+
+        lax.fori_loop(0, 4, add, 0)
+    sum_one()
+    feed_four()
+    for load in loads:
+        load.wait()
+    chunk = half // 2
+    sums[...] = jnp.zeros_like(sums)
+
+    def store(index):
+        own = pl.ds(index * chunk, chunk)
+        return pltpu.make_async_copy(mgrad_s.at[own], grad_ref.at[own], own_sems.at[4 + index])
+
+    for index in range(4):
+        own = slice(index * chunk, (index + 1) * chunk)
+        gnormed = lax.dot_general(mixed[own, :], w_s[...], NT, preferred_element_type=F32)
+        n, inverse = normalise(x_s[own, :].astype(F32))
+        e = gnormed * ((1.0 + vec_one[1:2, :]) * vec_one[0:1, :])
+        mgrad_s[own, :] = mgrad_s[own, :] + inverse * (
+            e - jnp.mean(e, axis=-1, keepdims=True) - n * jnp.mean(e * n, axis=-1, keepdims=True)
+        )
+        store(index).start()
+        sums[0:1, :] += jnp.sum(gnormed, axis=0, keepdims=True)
+        sums[1:2, :] += jnp.sum(gnormed * n, axis=0, keepdims=True)
+        if index == 2:
+            sum_two()
+
+    first_sum, second_sum = sums[1:2, :], middle_sums[1:2, :]
+    mod = [
+        sums[0:1, :], vec_one[0:1, :] * first_sum, middle_sums[4:5, :], middle_sums[0:1, :],
+        vec_two[1:2, :] * second_sum, middle_sums[2:3, :],
+    ]
+    wholes = [
+        (1.0 + vec_one[1:2, :]) * first_sum, (1.0 + vec_two[2:3, :]) * second_sum,
+        middle_sums[3:4, :],
+    ]
+    weighted = None
+    for index, value in enumerate(mod):
+        part = jnp.sum(
+            ada_s[:, index * width : (index + 1) * width].astype(F32) * value, axis=1,
+            keepdims=True,
+        )
+        weighted = part if weighted is None else weighted + part
+    table_row = jnp.broadcast_to(weighted, (lanes, lanes)).T[0:1] * extra[2:3, :]
+    tiles = width // lanes
+    for z in range(4):
+        for line in range(9):
+            tile = 9 * z + line
+            value = mod[tile // tiles]
+            start = (tile % tiles) * lanes
+            small[z, line : line + 1, :] = value[:, start : start + lanes]
+        for line in range(tiles):
+            start = z * width + line * lanes
+            small[z, 9 + line : 10 + line, :] = up_sums[0:1, start : start + lanes]
+            for index, value in enumerate(wholes):
+                at = 15 + index * tiles + line
+                small[z, at : at + 1, :] = value[:, line * lanes : (line + 1) * lanes]
+        small[z, 33:34, :] = table_row
+        small[z, 34:36, :] = extra[0:2, :]
+        small[z, 36:40, :] = jnp.zeros((4, lanes), F32)
+
+    def hop_place(s):
+        return push(
+            small.at[ahead(s)], rows_all.at[group, mlp, place], sems, 20 + s, {"seq": ahead(s)}
+        )
+
+    def hop_place_in(s):
+        return push(
+            small.at[ahead(s)], rows_all.at[group, mlp, ahead(4 - s)], sems, 20 + s,
+            {"seq": ahead(s)},
+        )
+
+    def hop_mlp(s, from_place):
+        own = rows_all.at[group, from_place]
+        return push(own, own, sems, 23 + s, {"mlp": (mlp + s) % 4})
+
+    def hop_group(from_group):
+        own = rows_all.at[from_group]
+        return push(own, own, sems, 27, {"grp": 1 - group})
+
+    for s in (1, 2, 3):
+        hop_place(s).start()
+    rows_all[group, mlp, place] = small[place]
+    sum_three()
+    sum_over()
+    for s in (1, 2, 3):
+        hop_place_in(s).wait()
+    for s in (1, 2, 3):
+        hop_mlp(s, mlp).start()
+    sum_four()
+    for s in (1, 2, 3):
+        hop_mlp(s, mlp).wait_send()
+        hop_mlp(s, (mlp + 4 - s) % 4).wait_recv()
+    hop_group(group).start()
+    feed_five()
+    sum_five()
+    hop_group(group).wait_send()
+    hop_group(1 - group).wait_recv()
+    for index in range(4):
+        store(index).wait()
+
+
+def finish(
+    packs, cosine, sine, normed, vec_one, vec_two, middle_sums, up_sums, extra, feed_two, weight,
+    x, mgrad, ada_weight,
+):
+    rows = normed.shape[1] // 8
+    lanes = 2 * HD
+    share = (2, 4, BLOCKS, rows, lanes)
+    feed_rows = feed_two.shape[2]
+    tokens, width = x.shape
+    like = lambda value: pltpu.VMEM(value.shape, value.dtype)
+    apart = pl.BlockSpec(memory_space=pl.ANY)
+    return pl.pallas_call(
+        finish_kernel,
+        in_specs=in_vmem(10) + [apart] * 4,
+        out_specs=in_vmem(3) + [apart],
+        out_shape=[
+            jax.ShapeDtypeStruct(share[2:], BF16),
+            jax.ShapeDtypeStruct((BLOCKS, feed_rows, lanes), BF16),
+            jax.ShapeDtypeStruct((2, 4, 4, SMALL_ROWS, lanes), F32),
+            jax.ShapeDtypeStruct((tokens, width), F32),
+        ],
+        scratch_shapes=[
+            pltpu.VMEM((tokens, 3 * width), BF16), like(weight), like(x), like(mgrad),
+            like(ada_weight), pltpu.VMEM((8, width), F32), pltpu.VMEM((4, SMALL_ROWS, lanes), F32),
         ]
-    )
-    out = jnp.dot(rows, gbranch_ref[...], preferred_element_type=F32).astype(BF16)
-    for index in range(4):
-        out_ref[0, index, :split] = up[index * split : (index + 1) * split]
-        out_ref[0, index, split : 2 * split] = down[index * split : (index + 1) * split]
-        out_ref[0, index, 2 * split :] = out[index * part : (index + 1) * part]
-
-
-def weight_grads(picked, hidden, gfeed, att, gbranch, act, gpre):
-    tokens, width = hidden.shape
-    block = pl.BlockSpec((tokens, act.shape[1] // 4), lambda i, p: (0, p[i]))
-    shape = (2, 4, width // 2 + width // 16, width)
-    return pl.pallas_call(
-        weight_grads_kernel,
-        grid_spec=pltpu.PrefetchScalarGridSpec(
-            num_scalar_prefetch=1,
-            grid=(2,),
-            in_specs=[once(hidden.shape)] * 4 + [block, block],
-            out_specs=pl.BlockSpec((1,) + shape[1:], lambda i, p: (i, 0, 0, 0)),
-            scratch_shapes=[pltpu.VMEM((width, tokens), BF16)] * 3,
+        + [pltpu.VMEM(share, BF16)] * 3
+        + sum_scratch(rows, EARLY + MIDDLE + LATE)
+        + sum_scratch(feed_rows, LATE)
+        + [pltpu.SemaphoreType.DMA((28,))] * 2
+        + [pltpu.SemaphoreType.DMA((8,))],
+        compiler_params=pltpu.CompilerParams(
+            collective_id=4, has_side_effects=True, vmem_limit_bytes=WHOLE_VMEM
         ),
-        out_shape=jax.ShapeDtypeStruct(shape, BF16),
-        compiler_params=params("arbitrary"),
         cost_estimate=pl.CostEstimate(
-            flops=6_000_000_000, bytes_accessed=20_000_000, transcendentals=0
+            flops=60_000_000_000, bytes_accessed=20_000_000, transcendentals=0
         ),
-        name="weight_grads",
-    )(picked, hidden, gfeed, att, gbranch, act, gpre)
-
-
-def swapped(value, axis, bit):
-    count = lax.axis_size(axis)
-    return lax.ppermute(value, axis, [(place, place ^ bit) for place in range(count)])
-
-
-def wide(value):
-    return value.astype(F32)
-
-
-def over_cores(sent, kept):
-    return (wide(kept) + wide(swapped(sent, "mlp", 1))).astype(BF16)
-
-
-def over_rows(value, row):
-    other = swapped(pick(value, 1 - row), "mlp", 2)
-    return (wide(pick(value, row)) + wide(other)).astype(BF16)
-
-
-def over_places(value, place):
-    total = wide(pick(value, place))
-    for steps in (1, 2, 3):
-        total = total + wide(along(pick(value, (place + steps) % 4), steps))
-    return total.astype(BF16)
-
-
-def over_groups(value):
-    return wide(value) + wide(swapped(value, "grp", 1))
-
-
-def tie(*values):
-    return lax.optimization_barrier(values)
-
-
-def along(value, steps):
-    pairs = [(place, (place + steps) % 4) for place in range(4)]
-    return lax.ppermute(value, "seq", pairs)
-
-
-def pick(stack, index):
-    return lax.dynamic_index_in_dim(stack, index, 0, keepdims=False)
+        name="finish",
+    )(
+        packs, cosine, sine, normed, vec_one, vec_two, middle_sums, up_sums, extra, feed_two,
+        weight, x, mgrad, ada_weight,
+    )
 
 
 def four_shards(
@@ -1273,83 +1577,54 @@
         x2, cotangent.reshape(2, half, width), att, vec_two, out_weight, feed_weights
     )
     flat = lambda value: value.reshape(token_rows, value.shape[2])
-    core = lax.axis_index("mlp") % 2
-    row = lax.axis_index("mlp") // 2
-    factors = tuple(
-        flat(value) for value in (hidden, grad_feed, att_low, grad_branch, act, grad_pre)
-    )
-    feed_sent = weight_grads(jnp.stack([1 - core, 3 - core]).astype(jnp.int32), *factors)
-    feed_kept = weight_grads(jnp.stack([core, 2 + core]).astype(jnp.int32), *factors)
-    feed = over_cores(feed_sent, feed_kept)
-
-    feed, grad_att = tie(feed, grad_att)
-    feed = over_rows(feed, row)
-    grads = backward_attention(packs, grad_att, att, pieces, results, logs, logs_own)
-    feed, grads = tie(feed, grads)
-    feed = over_places(feed, place)
-    feed_total = over_groups(feed)
-    mixed_grad = unrotate(grads, cosine, sine)
+    feed_held, att_grads = feed_grads(
+        *(flat(value) for value in (hidden, grad_feed, att_low, grad_branch, act, grad_pre)),
+        grad_att,
+    )
+    grads, feed_two = backward_attention(
+        packs, grad_att, att, pieces, results, logs, logs_own, att_grads, feed_held
+    )
     blocks = flat(normed).T.reshape(4, 2, 2, width // 16, token_rows)
     blocks = jnp.transpose(blocks, (2, 1, 0, 3, 4)).reshape(2, width // 2, token_rows)
-    project_back = lambda part: jnp.dot(
-        part, flat(mixed_grad), preferred_element_type=F32
-    ).astype(BF16).reshape(2, 4, width // 16, 3 * width)
-    qkv = over_cores(
-        project_back(pick(blocks, 1 - core)), project_back(pick(blocks, core))
-    )
-    qkv_total = over_groups(over_places(over_rows(qkv, row), place))
-    input_grad, input_sums = input_pass(mixed_grad, qkv_weight, x2, middle_grad, vec_one)
-
-    shift_one_grad = input_sums[0]
-    first_gain_grad = (1.0 + scale_one) * input_sums[1]
-    scale_one_grad = gain_one * input_sums[1]
-    shift_two_grad = middle_sums[0]
-    second_gain_grad = (1.0 + scale_two) * middle_sums[1]
-    scale_two_grad = gain_two * middle_sums[1]
-    mod_grad = jnp.concatenate(
+    lanes = 2 * HD
+    extra = jnp.stack(
         [
-            shift_one_grad, scale_one_grad, middle_sums[4], shift_two_grad, scale_two_grad,
-            middle_sums[2],
+            condition, jnp.full(condition.shape, step_value, F32),
+            silu_back(jnp.ones_like(condition))[0],
         ]
-    )
-    cond_grad = jnp.dot(ada_weight.astype(F32), mod_grad, precision=highest)
-    table_row = silu_back(cond_grad)[0]
-    cond_size = condition.shape[0]
-    small = jnp.concatenate(
-        [
-            mod_grad, first_gain_grad, second_gain_grad, up_sums[0], middle_sums[3],
-            table_row, condition, jnp.full((cond_size,), step_value, F32),
-        ]
-    )
-    small_all = lax.all_gather(small, ("grp", "seq", "mlp"), axis=0)
-    rank = place * mlp_count + lax.axis_index("mlp")
+        + [jnp.zeros_like(condition)] * 5
+    )
+    qkv_blocks, feed_blocks, rows_all, input_grad = finish(
+        grads, cosine, sine, blocks, vec_one, vec_two, middle_sums, up_sums, extra,
+        feed_two, qkv_weight, flat(x2), flat(middle_grad), ada_weight,
+    )
+    feed_total = feed_blocks.reshape(3, 6, 3 * width // 16, lanes)
+    feed_total = jnp.transpose(feed_total, (0, 2, 1, 3)).reshape(9 * width // 16, width)
+    feed_total = feed_total.astype(F32)
+    qkv_total = jnp.transpose(qkv_blocks, (1, 0, 2)).reshape(width // 16, 3 * width).astype(F32)
+
+    mlp = lax.axis_index("mlp")
     ranks = 4 * mlp_count
-
-    def share(start, size):
-        each = size // ranks
-        return lax.dynamic_slice_in_dim(small_all, start + rank * each, each, 1)
-
-    mod_size = 6 * width
-    units = share_units * mlp_count
-    mod_share = share(0, mod_size)
-    start = mod_size
-    first_share = jnp.sum(share(start, width), axis=0)
-    start += width
-    second_share = jnp.sum(share(start, width), axis=0)
-    start += width
-    up_bias_share = jnp.sum(share(start, units), axis=0)
-    start += units
-    down_bias_share = jnp.sum(share(start, width), axis=0)
-    start += width
-    rows_all = small_all[:, start : start + cond_size]
-    cond_all = small_all[:, start + cond_size : start + 2 * cond_size].astype(BF16).astype(F32)
-    steps_all = small_all[:, start + 2 * cond_size].astype(jnp.int32)
+    rank = place * mlp_count + mlp
+    rows_all = rows_all.reshape(2 * ranks, SMALL_ROWS, lanes)
+    row_sums = jnp.sum(rows_all, axis=0)
+
+    def share(value, index, count):
+        value = value.reshape(value.shape[:-2] + (-1,))
+        each = value.shape[-1] // count
+        return lax.dynamic_slice_in_dim(value, index * each, each, value.ndim - 1)
+
+    mod_share = share(rows_all[:, 0:9], mlp, mlp_count)
+    up_bias_share = share(row_sums[9:15], mlp, mlp_count)
+    first_share, second_share, down_bias_share = (
+        share(row_sums[start : start + 6], rank, ranks) for start in (15, 21, 27)
+    )
+    cond_all = rows_all[:, 34].astype(BF16).astype(F32)
     ada_share = lax.dot_general(cond_all, mod_share, TN, precision=highest)
     table_each = time_table.shape[0] // ranks
     own_rows = rank * table_each + jnp.arange(table_each, dtype=jnp.int32)
-    chosen = (own_rows[:, None] == steps_all[None, :]).astype(F32)
-    table_share = jnp.dot(chosen, rows_all, precision=highest)
-
+    chosen = (own_rows[:, None] == rows_all[None, :, 35, 0].astype(jnp.int32)).astype(F32)
+    table_share = jnp.dot(chosen, rows_all[:, 33], precision=highest)
     split = width // 4
     up_total = feed_total[:split]
     down_total = feed_total[split : 2 * split].T

time: 533 us -> 438 us (0.82)
  waiting for transfers between devices: 90.2 us -> 0.04 us
  Pallas kernels: 318 us -> 381 us
  starting transfers between devices: 38 us -> 0.04 us
  other arithmetic: 30.8 us -> 14.7 us
  matrix products: 14.2 us -> 2.13 us
    ppermute x12 -> x0, waiting for transfers between devices: 87.7 us -> none  [the longest x6 68.9 us: along(): return lax.ppermute(value, 'seq', pairs)]
    pallas_call x5 -> x3, Pallas kernels: 187 us -> 250 us  [the longest x1 91.6 us: backward_attention(): pl.pallas_call(backward_kernel, in_specs=in_vmem(9), out_specs=in_vmem(2)...]
    ppermute x12 -> x0, starting transfers between devices: 37.9 us -> none  [the longest x6 29.9 us: swapped(): lax.ppermute(value, axis, [(place, place ^ bit) for place in range(count)])]
    dot_general x4 -> x1, matrix products: 12.2 us -> 0.82 us  [four_shards(): table_share = jnp.dot(chosen, rows_all[:, 33], precision=highest)]
    convert_element_type x7 -> x2, other arithmetic: 13.5 us -> 3.29 us  [the longest x1 1.73 us: four_shards(): jnp.transpose(qkv_blocks, (1, 0, 2)).reshape(width // 16, 3 * width)]
  transfers between devices with their start and end apart: 14 -> 1, of which waited for: 9 -> 0; matrix products, arithmetic and copies ran while one was open for 7% -> 3% of each run, Pallas kernels for 47% -> 21%
where the time goes in v3:
time: 438 us; the launch traced here: 432 us
  Pallas kernels  381 us (87%)
  between operations  17.1 us (4%)
  local copies, waits for them, and re-layouts  16.6 us (4%)
  other arithmetic  14.7 us (3%)
    pallas_call x1, Pallas kernels, backward_attention(): pl.pallas_call(backward_kernel, in_specs=in_vmem(9), out_specs=in_vmem(2)...  91.6 us
    pallas_call x1, Pallas kernels, finish(): pl.pallas_call(finish_kernel, in_specs=in_vmem(10) + [apart] * 4, out_spe...  90.1 us
    pallas_call x1, Pallas kernels, forward_attention(): pl.pallas_call(forward_kernel, in_specs=in_vmem(1), out_specs=in_vmem(len...  80.8 us
    pallas_call x1, Pallas kernels, feed_grads(): pl.pallas_call(feed_grads_kernel, in_specs=in_vmem(7), out_specs=in_vmem(...  68.4 us
    pallas_call x1, Pallas kernels, middle_pass(): pl.pallas_call(middle_kernel, grid=(half // rows,), in_specs=[tok(width),...  38.4 us
    pallas_call x1, Pallas kernels, project(): pl.pallas_call(project_kernel, grid=(half // rows,), in_specs=[tok(width)...  11.8 us
  transfers between devices with their start and end apart: 1, of which 0 were waited for; matrix products, arithmetic and copies ran while one was open for 3% of the time, Pallas kernels for 21%

profile of v3, /device:TPU:0, one launch (start us, length us, event | category | flops | bytes accessed | tf_op | source)
XLA Modules:
  0.0 431.6 jit_solution(4157177343575702915)
XLA Ops:
  7.2 0.0 all-gather.3.cloned.1.call-start
  7.2 0.7 broadcast_in_dim.7
  7.9 3.2 pad_maximum_fusion
  11.1 0.0 copy-start.6
  11.1 0.0 copy-start.1
  11.1 0.0 copy-start.2
  11.1 0.0 copy-start.3
  11.1 0.0 copy-start.4
  11.1 0.0 copy-start.5
  11.1 0.0 all-gather.3.cloned.1.call-update
  11.2 0.6 copy-done.6
  11.8 0.6 fusion.12
  15.0 0.7 fusion.11
  15.7 0.7 convert_multiply_fusion
  16.4 0.0 copy-done.1
  16.4 0.3 convolution_reduce_fusion
  16.7 0.0 copy-done.2
  16.8 0.0 copy-done.3
  16.8 0.0 copy-done.4
  16.8 0.0 copy-done.5
  16.9 0.6 stack.61.vec_ref.vec_one
  17.5 1.9 fusion
  19.4 1.8 pad_maximum_fusion.1
  21.3 11.8 %project.1 = (bf16[2,512,768]{2,1,0:T(8,128)(2,1)}, bf16[12,3,512,128]{3,2,1,0:T(8,128)(2,1)}) custom-call(bf16[2,512,768]{2,1,0:T(8,128)(2,1)} %bitcast.63, f32[8,768]{1,0:T(8,128)} %stack.61.vec_ref.vec_one, bf16[768,2304]{1,0:T(8,128)(2,1)} %w_ref.3, f32[2,512,128]{2,1,0:T(8,128)} %get-tuple-element.82.cos_ref.cosine, ...), custom_call_target="tpu_custom_call" | custom-call | tf_op jit(solution)/shard_map/project/pallas_call | solution.py:418
  33.1 1.8 copy.34
  34.9 1.3 copy.35
  36.2 0.6 stack.73.extra
  36.9 0.6 stack.71.vec_ref.vec_two
  37.5 0.5 iota_add_fusion
  38.1 80.8 %forward_attention.1 = (bf16[12,512,128]{2,1,0:T(8,128)(2,1)}, bf16[2,4,3,512,128]{4,3,2,1,0:T(8,128)(2,1)}, bf16[2,4,512,128]{3,2,1,0:T(8,128)(2,1)}, f32[2,4,8,1024]{3,2,1,0:T(8,128)}, f32[12,8,1024]{2,1,0:T(8,128)}) custom-call(bf16[12,3,512,128]{3,2,1,0:T(8,128)(2,1)} %get-tuple-element.39.packs), custom_call_target="tpu_custom_call" | custom-call | flops 99999997952 | bytes 8000000 | tf_op jit(solution)/shard_map/forward_attention/pallas_call | solution.py:780
  118.8 0.0 all-gather.3.cloned.1.call-done
  118.8 38.4 %middle_pass.1 = (bf16[2,512,768]{2,1,0:T(8,128)(2,1)}, bf16[2,512,768]{2,1,0:T(8,128)(2,1)}, bf16[2,512,768]{2,1,0:T(8,128)(2,1)}, bf16[2,512,3072]{2,1,0:T(8,1...) custom-call(bf16[2,512,768]{2,1,0:T(8,128)(2,1)} %bitcast.64, ...), custom_call_target="tpu_custom_call" | custom-call | tf_op jit(solution)/shard_map/middle_pass/pallas_call | solution.py:1120
  157.2 68.4 %feed_grads.1 = (bf16[2,4,18,144,128]{4,3,2,1,0:T(8,128)(2,1)}, bf16[2,4,512,128]{3,2,1,0:T(8,128)(2,1)}) custom-call(bf16[1024,768]{1,0:T(8,128)(2,1)} %bitcast.87, bf16[1024,768]{1,0:T(8,128)(2,1)} %bitcast.88, bf16[1024,768]{1,0:T(8,128)(2,1)} %bitcast.86, bf16[1024,768]{1,0:T(8,128)(2,1)} %bitcast.89, bf16[1024,3072]{1,0:T(8,128)(2,1)} %bitcast.82, ...), custom_call_target="tpu_custom_call" | custom-call | flops 24000000000 | bytes 20000000 | tf_op jit(solution)/shard_map/feed_grads/pallas_call | solution.py:1268
  225.6 91.6 %backward_attention.1 = (bf16[12,3,512,128]{3,2,1,0:T(8,128)(2,1)}, bf16[4,9,144,128]{3,2,1,0:T(8,128)(2,1)}) custom-call(bf16[12,3,512,128]{3,2,1,0:T(8,128)(2,1)} %get-tuple-element.39.packs, bf16[12,512,128]{2,1,0:T(8,128)(2,1)} %get-tuple-element.42.gatt, bf16[12,512,128]{2,1,0:T(8,128)(2,1)} %get-tuple-element.40.att_ref.att, ...), custom_call_target="tpu_custom_call" | custom-call | flops 120000004096 | bytes 8000000 | tf_op jit(solution)/shard_map/backward_attention/pallas_call | solution.py:992
  317.2 90.1 %finish.1 = (bf16[18,48,128]{2,1,0:T(8,128)(2,1)}, bf16[18,144,128]{2,1,0:T(8,128)(2,1)}, f32[2,4,4,40,128]{4,3,2,1,0:T(8,128)}, f32[1024,768]{1,0:T(8,128)}) custom-call(bf16[12,3,512,128]{3,2,1,0:T(8,128)(2,1)} %get-tuple-element.55.packs, f32[2,512,128]{2,1,0:T(8,128)} %get-tuple-element.82.cos_ref.cosine, f32[2,512,128]{2,1,0:T(8,128)} %get-tuple-element.83.sin_ref.sine, ...), custom_call_target="tpu_custom_call" | custom-call | flops 60000002048 | bytes 20000000 | tf_op jit(solution)/shard_map/finish/pallas_call | solution.py:1494
  407.3 1.0 slice.48
  408.3 0.9 slice.47
  409.2 1.3 copy.38
  410.5 0.3 copy.50
  410.8 0.0 copy-start
  410.8 1.1 slice_bitcast_fusion
  411.9 0.0 copy-start.7
  411.9 0.7 slice.50
  412.6 0.9 slice.46
  413.5 1.6 fusion.5
  415.1 1.2 reduce_sum.29
  416.2 0.1 copy.51
  416.3 0.7 dynamic-slice_reduce_fusion
  417.0 1.0 fusion.1
  418.0 1.7 copy_bitcast_fusion.1
  419.7 0.6 dynamic_slice.20
  420.3 0.6 dynamic_slice.21
  420.9 0.6 dynamic_slice.23
  421.5 0.6 dynamic_slice.22
  422.1 0.0 copy-done.7
  422.1 0.8 fusion.3
  422.9 0.0 copy-done
  422.9 1.7 copy.53
  (20 shorter events, 0.1 us)
Async XLA Ops:
  7.2 111.7 %all-gather.3.cloned.1.call-start = ((), (), s32[]{:S(2)}) async-start(), calls=%async_computation | async-start | bytes 11919360 | tf_op jit(solution)/shard_map/all_gather | solution.py:1542
  11.1 0.7 copy-start.6
  11.1 5.3 %copy-start.1 = (bf16[128,4608]{1,0:T(8,128)(2,1)S(1)}, bf16[128,4608]{1,0:T(8,128)(2,1)}, u32[]{:S(2)}) copy-start(bf16[128,4608]{1,0:T(8,128)(2,1)} %ada_ref.1) | copy-start | bytes 3538948
  11.1 5.6 %copy-start.2 = (bf16[4608]{0:T(1024)(128)(2,1)S(1)}, bf16[4608]{0:T(1024)(128)(2,1)}, u32[]{:S(2)}) copy-start(bf16[4608]{0:T(1024)(128)(2,1)} %param.18) | copy-start | bytes 27652
  11.1 5.6 %copy-start.3 = (bf16[768]{0:T(1024)(128)(2,1)S(1)}, bf16[768]{0:T(1024)(128)(2,1)}, u32[]{:S(2)}) copy-start(bf16[768]{0:T(1024)(128)(2,1)} %param.22) | copy-start | bytes 4612
  11.1 5.7 %copy-start.4 = (bf16[768]{0:T(1024)(128)(2,1)S(1)}, bf16[768]{0:T(1024)(128)(2,1)}, u32[]{:S(2)}) copy-start(bf16[768]{0:T(1024)(128)(2,1)} %param.26) | copy-start | bytes 4612
  11.1 5.7 %copy-start.5 = (bf16[768]{0:T(1024)(128)(2,1)S(1)}, bf16[768]{0:T(1024)(128)(2,1)}, u32[]{:S(2)}) copy-start(bf16[768]{0:T(1024)(128)(2,1)} %param.19) | copy-start | bytes 4612
  410.8 12.1 %copy-start = (f32[1024,768]{1,0:T(8,128)S(1)}, f32[1024,768]{1,0:T(8,128)}, u32[]{:S(2)}) copy-start(f32[1024,768]{1,0:T(8,128)} %get-tuple-element.61) | copy-start | bytes 9437188
  411.9 10.2 %copy-start.7 = (s32[64]{0:T(128)S(1)}, s32[64]{0:T(128)}, u32[]{:S(2)}) copy-start(s32[64]{0:T(128)} %iota_add_fusion) | copy-start | bytes 772
Sparse Core Ops, SparseCore 0:
  11.3 67.5 all-gather.2

commit v4 on v3

--- a/solution.py
+++ b/solution.py
@@ -388,53 +388,6 @@
     return centred * inverse, inverse
 
 
-def project_kernel(x_ref, vec_ref, w_ref, cos_ref, sin_ref, normed_ref, pack_ref):
-    rows = x_ref.shape[1]
-    width = x_ref.shape[2]
-    x = x_ref[...].reshape(2 * rows, width).astype(F32)
-    n, _ = normalise(x)
-    normed = n * vec_ref[0:1, :] * (1.0 + vec_ref[1:2, :]) + vec_ref[2:3, :]
-    normed = normed.astype(BF16)
-    normed_ref[...] = normed.reshape(2, rows, width)
-    cosine = cos_ref[...].reshape(2 * rows, 2 * HD)
-    sine = sin_ref[...].reshape(2 * rows, 2 * HD)
-    for part in range(3):
-        mixed = jnp.dot(
-            normed, w_ref[:, part * width : (part + 1) * width], preferred_element_type=F32
-        )
-        for pair in range(width // (2 * HD)):
-            value = mixed[:, pair * 2 * HD : (pair + 1) * 2 * HD]
-            if part < 2:
-                value = turn(value, cosine, sine)
-            even, odd = exchange(value[:rows], value[rows:])
-            pack_ref[2 * pair, part] = even.astype(BF16)
-            pack_ref[2 * pair + 1, part] = odd.astype(BF16)
-
-
-def project(x2, vecs, weight, cosine, sine, rows=256):
-    half, width = x2.shape[1:]
-    heads = width // HD
-    tok = lambda last: pl.BlockSpec((2, rows, last), lambda i: (0, i, 0))
-    return pl.pallas_call(
-        project_kernel,
-        grid=(half // rows,),
-        in_specs=[
-            tok(width),
-            pl.BlockSpec(vecs.shape, lambda i: (0, 0)),
-            pl.BlockSpec(weight.shape, lambda i: (0, 0)),
-            tok(2 * HD),
-            tok(2 * HD),
-        ],
-        out_specs=[tok(width), pl.BlockSpec((heads, 3, rows, 2 * HD), lambda i: (0, 0, i, 0))],
-        out_shape=[
-            jax.ShapeDtypeStruct((2, half, width), BF16),
-            jax.ShapeDtypeStruct((heads, 3, half, 2 * HD), BF16),
-        ],
-        compiler_params=params("arbitrary"),
-        name="project",
-    )(x2, vecs, weight, cosine, sine)
-
-
 def attend_rows(q, k_ref, v_ref, keys, out_put, log_put, block=512):
     top = None
     for start in range(0, keys, block):
@@ -501,7 +454,8 @@
     return (left.astype(F32) + right.astype(F32)).astype(BF16)
 
 
-def sum_steps(held, one_p, one_q, two, others, three, out, sems, base):
+def sum_steps(held, one_p, one_q, two, others, three, out, sems, base, near=None):
+    near = held if near is None else near
     group = lax.axis_index("grp")
     place = lax.axis_index("seq")
     row, _, other_row, _ = mlp_place()
@@ -552,9 +506,9 @@
         arrive(1)
 
         def add(z, carry):
-            one_p[z] = added(held[row, z, 0:10], one_p[z])
+            one_p[z] = added(near[row, z, 0:10], one_p[z])
             for y in range(2):
-                one_q[y, z] = added(held[y, z, pl.ds(10 + 4 * group, 4)], one_q[y, z])
+                one_q[y, z] = added(near[y, z, pl.ds(10 + 4 * group, 4)], one_q[y, z])
             return carry
 
         lax.fori_loop(0, 4, add, 0)
@@ -604,7 +558,9 @@
 
 
 def forward_kernel(
-    packs, att, pieces, results, logs, logs_own, crossed, k_s, v_s, send_sems, recv_sems
+    x_ref, w_ref, near, far, step_ref, table, ada_ref, params_ref,
+    packs, att, pieces, results, logs, logs_own, cosine, sine, vec_one, vec_two, extra, bias_all,
+    blocks, crossed, normed_s, k_s, v_s, send_sems, recv_sems,
 ):
     group = lax.axis_index("grp")
     place = lax.axis_index("seq")
@@ -637,7 +593,98 @@
             results.at[min(kind, 1), s], att.at[head], sems, start + s, 1, behind(s)
         )
 
-    greet(neighbours(group, place, []))
+    row, core, _, _ = mlp_place()
+    mlp = row * 2 + core
+    greet(neighbours(group, place, [(mlp + s) % 4 for s in (1, 2, 3)]))
+    width = w_ref.shape[0]
+    vectors = params_ref[...].astype(F32)
+    vector = lambda index: vectors[:, index * width : (index + 1) * width]
+    first_gain, second_gain, down_bias = vector(6), vector(7), vector(8)
+    up_bias = vectors[:, 9 * width :]
+    bias_all[mlp] = jnp.broadcast_to(up_bias, bias_all.shape[1:])
+
+    def share_bias(s, owner):
+        own = bias_all.at[owner]
+        return push(own, own, sems, 27 + s, {"mlp": (mlp + s) % 4})
+
+    for s in (1, 2, 3):
+        share_bias(s, mlp).start()
+
+    half = packs.shape[2]
+    lanes = 2 * HD
+    quarters = step_ref[...].astype(F32)
+    own_quarter = lax.broadcasted_iota(jnp.int32, quarters.shape, 1) == place
+    step = jnp.sum(jnp.where(own_quarter, quarters, 0.0), axis=1, keepdims=True)
+    entries = lax.broadcasted_iota(jnp.int32, (16, table.shape[0]), 1).astype(F32)
+    chosen = jnp.where(entries == step, 1.0, 0.0).astype(BF16)
+    embedded = jnp.dot(chosen, table[...], preferred_element_type=F32)
+    gate = 1.0 / (1.0 + jnp.exp(-embedded))
+    condition = embedded * gate
+    modulation = jnp.dot(condition.astype(BF16), ada_ref[...], preferred_element_type=F32)
+    modulation = modulation[0:1] + vectors[:, : 6 * width]
+    part = lambda index: modulation[:, index * width : (index + 1) * width]
+    for target, values in (
+        (vec_one, (first_gain, part(1), part(0))),
+        (
+            vec_two,
+            (part(2), second_gain, part(4), part(3), part(5), down_bias),
+        ),
+        (
+            extra,
+            (
+                condition[0:1], jnp.broadcast_to(step, (1, condition.shape[1])),
+                (gate * (1.0 + embedded * (1.0 - gate)))[0:1],
+            ),
+        ),
+    ):
+        target[...] = jnp.zeros_like(target)
+        for index, value in enumerate(values):
+            target[index : index + 1, :] = value
+
+    near_rows = near.shape[1]
+    first_half = lax.broadcasted_iota(jnp.int32, near.shape[1:], 1) % HD < HD // 2
+    for index in range(far.shape[1]):
+        far_cos, far_sin = far[0, index : index + 1, :], far[1, index : index + 1, :]
+        start = index * near_rows
+        at = slice(start % half, start % half + near_rows)
+        value = far_sin * near[0] + far_cos * near[1]
+        cosine[start // half, at, :] = far_cos * near[0] - far_sin * near[1]
+        sine[start // half, at, :] = jnp.where(first_half, -value, value)
+
+    tile = half // 2
+
+    def normal(index, carry):
+        at = pl.ds(pl.multiple_of(index * tile, tile), tile)
+        for side in range(2):
+            n, _ = normalise(x_ref[side, at, :].astype(F32))
+            value = n * vec_one[0:1, :] * (1.0 + vec_one[1:2, :]) + vec_one[2:3, :]
+            normed_s[side, at, :] = value.astype(BF16)
+        return carry
+
+    lax.fori_loop(0, 2, normal, 0)
+
+    def project(low_pair, count):
+        def tokens(index, carry):
+            at = pl.ds(pl.multiple_of(index * tile, tile), tile)
+            normed = normed_s[:, at, :].reshape(2 * tile, width)
+            turn_cos = cosine[:, at, :].reshape(2 * tile, lanes)
+            turn_sin = sine[:, at, :].reshape(2 * tile, lanes)
+            for kind in range(3):
+                start = kind * width + low_pair * lanes
+                mixed = jnp.dot(
+                    normed, w_ref[:, start : start + count * lanes], preferred_element_type=F32
+                )
+                for pair in range(count):
+                    value = mixed[:, pair * lanes : (pair + 1) * lanes]
+                    if kind < 2:
+                        value = turn(value, turn_cos, turn_sin)
+                    even, odd = exchange(value[:tile], value[tile:])
+                    head = 2 * (low_pair + pair)
+                    packs[head, kind, at, :] = even.astype(BF16)
+                    packs[head + 1, kind, at, :] = odd.astype(BF16)
+            return carry
+
+        lax.fori_loop(0, 2, tokens, 0)
 
     def full(kind, head, before, after):
         sel = min(kind, 1)
@@ -660,12 +707,31 @@
 
         lax.fori_loop(0, 4, step, 0)
 
+    project(0, 4)
+
     @pl.when(group == 1)
     def _():
         for s in (1, 2, 3):
             first(s).start()
+
+    project(4, 2)
+
+    @pl.when(group == 1)
+    def _():
         for s in (1, 2, 3, 0):
             cross(s).start()
+
+    flipped = normed_s[...].reshape(2 * half, width).T
+    part_rows = width // 16
+    for which in range(2):
+        for y in range(2):
+            for z in range(4):
+                start = ((z * 2 + y) * 2 + which) * part_rows
+                at = (y * 4 + z) * part_rows
+                blocks[which, at : at + part_rows, :] = flipped[start : start + part_rows]
+
+    @pl.when(group == 1)
+    def _():
         pieces[0, 0] = packs[2 * place]
         pieces[1, 0] = packs[2 * place + 1]
         for s in (1, 2, 3):
@@ -676,7 +742,7 @@
             first(s).wait_recv()
 
         def before(s):
-            @pl.when(s == 2)
+            @pl.when(s == 3)
             def _():
                 for other in (1, 2, 3):
                     second_queries(other).start()
@@ -763,31 +829,45 @@
         for s in range(4):
             home(2, s, 8 + place).wait_send()
 
+    for s in (1, 2, 3):
+        share_bias(s, mlp).wait_send()
+        share_bias(s, (mlp + 4 - s) % 4).wait_recv()
+
 
 def in_vmem(count):
     return [pl.BlockSpec(memory_space=pltpu.VMEM)] * count
 
 
-def forward_attention(packs):
-    heads, _, half, lanes = packs.shape
+def forward_attention(x2, weight, *rest):
+    _, half, width = x2.shape
+    heads, lanes = width // HD, 2 * HD
     shapes = [
+        ((heads, 3, half, lanes), BF16),
         ((heads, half, lanes), BF16),
         ((2, 4, 3, half, lanes), BF16),
         ((2, 4, half, lanes), BF16),
         ((2, 4, 8, 2 * half), F32),
         ((heads, 8, 2 * half), F32),
+        ((2, half, lanes), F32),
+        ((2, half, lanes), F32),
+        ((8, width), F32),
+        ((8, width), F32),
+        ((8, rest[3].shape[1]), F32),
+        ((4, 8, rest[-1].shape[1] - 9 * width), F32),
+        ((2, width // 2, 2 * half), BF16),
     ]
     return pl.pallas_call(
         forward_kernel,
-        in_specs=in_vmem(1),
+        in_specs=in_vmem(2 + len(rest)),
         out_specs=in_vmem(len(shapes)),
         out_shape=[jax.ShapeDtypeStruct(shape, kind) for shape, kind in shapes],
         scratch_shapes=[
             pltpu.VMEM((4, 3, half, lanes), BF16),
+            pltpu.VMEM((2, half, width), BF16),
             pltpu.VMEM((8 * half, lanes), BF16),
             pltpu.VMEM((8 * half, lanes), BF16),
-            pltpu.SemaphoreType.DMA((28,)),
-            pltpu.SemaphoreType.DMA((28,)),
+            pltpu.SemaphoreType.DMA((31,)),
+            pltpu.SemaphoreType.DMA((31,)),
         ],
         compiler_params=pltpu.CompilerParams(
             collective_id=1, has_side_effects=True, vmem_limit_bytes=WHOLE_VMEM
@@ -796,7 +876,7 @@
             flops=100_000_000_000, bytes_accessed=8_000_000, transcendentals=0
         ),
         name="forward_attention",
-    )(packs)
+    )(x2, weight, *rest)
 
 
 def tile_grads(q, do, k, v, log_row, delta_row):
@@ -824,9 +904,9 @@
 
 
 def backward_kernel(
-    packs, gatt, att, pieces, results, logs, logs_own, dos, held, back, two,
-    staged, q_s, k_s, v_s, do_s, delta_s, dq_s, one_p, one_q,
-    send_sems, recv_sems,
+    packs_ref, gatt_ref, att_ref, held_ref, pieces, results, logs, logs_own, dos, back, two,
+    packs, gatt, att, held, staged, q_s, k_s, v_s, do_s, delta_s, dq_s, one_p, one_q,
+    send_sems, recv_sems, own_sems,
 ):
     group = lax.axis_index("grp")
     place = lax.axis_index("seq")
@@ -850,9 +930,22 @@
 
     greet(neighbours(group, place, [mlp_place()[2]]))
     sum_one, sum_two, sum_three, _, _, _ = sum_steps(
-        held, one_p, one_q, two, None, None, None, sems, 24
+        held_ref, one_p, one_q, two, None, None, None, sems, 24, held
     )
     sum_one()
+    load_held = pltpu.make_async_copy(held_ref, held, own_sems.at[3])
+    load_held.start()
+    local_loads = [
+        pltpu.make_async_copy(source, target, own_sems.at[index])
+        for index, (source, target) in enumerate(
+            ((packs_ref, packs), (gatt_ref, gatt), (att_ref, att))
+        )
+    ]
+
+    @pl.when(group == 0)
+    def _():
+        for load in local_loads:
+            load.start()
 
     def full(sel, put_values, put_queries):
         for s in range(4):
@@ -901,6 +994,7 @@
 
             @pl.when(s == 2)
             def _():
+                load_held.wait()
                 sum_two()
 
         def put_queries(s):
@@ -929,6 +1023,7 @@
 
         @pl.when((group == 0) & (s == 2))
         def _():
+            load_held.wait()
             sum_two()
 
     def put_queries(s):
@@ -949,6 +1044,9 @@
 
     @pl.when(group == 0)
     def _():
+        for load in local_loads:
+            load.wait()
+
         def local(head, carry):
             load_backward(packs.at[head], gatt[head], att[head], 0, *stores)
             own = slice(0, rows)
@@ -991,17 +1089,19 @@
     share = held.shape[2:]
     return pl.pallas_call(
         backward_kernel,
-        in_specs=in_vmem(9),
+        in_specs=[pl.BlockSpec(memory_space=pl.ANY)] * 4 + in_vmem(5),
         out_specs=in_vmem(2),
         out_shape=[
             jax.ShapeDtypeStruct((heads, 3, half, lanes), BF16),
             jax.ShapeDtypeStruct((4, 9) + share[1:], BF16),
         ],
-        scratch_shapes=[pltpu.VMEM((2, 4, 3, half, lanes), BF16)]
+        scratch_shapes=[pltpu.VMEM(value.shape, BF16) for value in (packs, gatt, att, held)]
+        + [pltpu.VMEM((2, 4, 3, half, lanes), BF16)]
         + [pltpu.VMEM((8 * half, lanes), BF16)] * 4
         + [pltpu.VMEM((8, 8 * half), F32), pltpu.VMEM((lanes, 8 * half), F32)]
         + sum_scratch(share[1], EARLY)
-        + [pltpu.SemaphoreType.DMA((28,)), pltpu.SemaphoreType.DMA((28,))],
+        + [pltpu.SemaphoreType.DMA((28,))] * 2
+        + [pltpu.SemaphoreType.DMA((4,))],
         compiler_params=pltpu.CompilerParams(
             collective_id=2, has_side_effects=True, vmem_limit_bytes=WHOLE_VMEM
         ),
@@ -1009,7 +1109,7 @@
             flops=120_000_000_000, bytes_accessed=8_000_000, transcendentals=0
         ),
         name="backward_attention",
-    )(packs, gatt, att, pieces, results, logs, logs_own, dos, held)
+    )(packs, gatt, att, held, pieces, results, logs, logs_own, dos)
 
 
 def whole(shape):
@@ -1018,7 +1118,7 @@
 
 
 def middle_kernel(
-    x_ref, cot_ref, att_ref, vec_ref, ow_ref, feed_ref,
+    x_ref, cot_ref, att_ref, vec_ref, ow_ref, up_ref, down_ref, bias_ref,
     out_ref, attlow_ref, hidden_ref, act_ref, gfeed_ref, gpre_ref, mgrad_ref, gbranch_ref,
     gatt_ref, sums_ref, upsum_ref, att_s, slope_s,
 ):
@@ -1042,12 +1142,12 @@
     n, inverse = normalise(middle)
     hidden = (n * gain * (1.0 + scale) + shift).astype(BF16)
     hidden_ref[...] = hidden.reshape(2, rows, width)
-    shares, _, chunk = feed_ref.shape
+    shares, _, chunk = up_ref.shape
     feed = None
     for index in range(shares):
         cols = slice(index * chunk, (index + 1) * chunk)
-        pre = jnp.dot(hidden, feed_ref[index, :width], preferred_element_type=F32)
-        pre = pre + feed_ref[index, 2 * width : 2 * width + 1].astype(F32)
+        pre = jnp.dot(hidden, up_ref[index], preferred_element_type=F32)
+        pre = pre + bias_ref[index, 0:1]
         square = pre * pre
         root = math.sqrt(2.0 / math.pi)
         tanh = jnp.tanh(pre * (root + (root * 0.044715) * square))
@@ -1057,7 +1157,7 @@
             root + (3.0 * root * 0.044715) * square
         )
         act_ref[:, :, cols] = act.reshape(2, rows, chunk)
-        part = jnp.dot(act, feed_ref[index, width : 2 * width], preferred_element_type=F32)
+        part = jnp.dot(act, down_ref[index], preferred_element_type=F32)
         feed = part if feed is None else feed + part
     feed = feed + down_bias
     out_ref[...] = (middle + gate_two * feed).astype(BF16).reshape(2, rows, width)
@@ -1068,13 +1168,11 @@
     up_sums = []
     for index in range(shares):
         cols = slice(index * chunk, (index + 1) * chunk)
-        gact = lax.dot_general(
-            gfeed, feed_ref[index, width : 2 * width], NT, preferred_element_type=F32
-        )
+        gact = lax.dot_general(gfeed, down_ref[index], NT, preferred_element_type=F32)
         gpre = (gact * slope_s[:, cols]).astype(BF16)
         gpre_ref[:, :, cols] = gpre.reshape(2, rows, chunk)
         up_sums.append(jnp.sum(gpre.astype(F32), axis=0, keepdims=True))
-        part = lax.dot_general(gpre, feed_ref[index, :width], NT, preferred_element_type=F32)
+        part = lax.dot_general(gpre, up_ref[index], NT, preferred_element_type=F32)
         ghidden = part if ghidden is None else ghidden + part
     e = ghidden * ((1.0 + scale) * gain)
     mgrad = cot + inverse * (
@@ -1110,10 +1208,10 @@
     return pl.BlockSpec(shape, lambda *_: zeros, pipeline_mode=pl.Buffered(1))
 
 
-def middle_pass(x2, cot2, att, vecs, out_weight, feed_weights, rows=128):
+def middle_pass(x2, cot2, att, vecs, out_weight, up_all, down_all, bias_all, rows=128):
     half, width = x2.shape[1:]
     heads = width // HD
-    units = feed_weights.shape[0] * feed_weights.shape[2]
+    units = up_all.shape[0] * up_all.shape[2]
     tok = lambda last: pl.BlockSpec((2, rows, last), lambda i: (0, i, 0))
     pack = pl.BlockSpec((heads, rows, 2 * HD), lambda i: (0, i, 0))
     token = lambda last, kind: jax.ShapeDtypeStruct((2, half, last), kind)
@@ -1122,7 +1220,7 @@
         grid=(half // rows,),
         in_specs=[
             tok(width), tok(width), pack, whole(vecs.shape), once(out_weight.shape),
-            once(feed_weights.shape),
+            once(up_all.shape), once(down_all.shape), once(bias_all.shape),
         ],
         out_specs=[
             tok(width), tok(width), tok(width), tok(units), tok(width), tok(units), tok(width),
@@ -1138,12 +1236,12 @@
         scratch_shapes=[pltpu.VMEM((2 * rows, width), BF16), pltpu.VMEM((2 * rows, units), F32)],
         compiler_params=params("arbitrary"),
         name="middle_pass",
-    )(x2, cot2, att, vecs, out_weight, feed_weights)
+    )(x2, cot2, att, vecs, out_weight, up_all, down_all, bias_all)
 
 
 def feed_grads_kernel(
     hidden_ref, gfeed_ref, att_ref, gbranch_ref, act_ref, gpre_ref, gatt, held, dos,
-    hidden_s, gfeed_s, att_s, sent, got, crossed, send_sems, recv_sems,
+    hidden_s, gfeed_s, att_s, act_s, gpre_s, sent, got, crossed, send_sems, recv_sems, own_sems,
 ):
     group = lax.axis_index("grp")
     place = lax.axis_index("seq")
@@ -1166,6 +1264,21 @@
     def swap(y):
         return push(sent.at[y], got.at[y], sems, 13 + y, {"mlp": other_core})
 
+    width = hidden_s.shape[0]
+
+    def loads(order, index):
+        cols = pl.ds(pl.multiple_of(index * width, width), width)
+        return (
+            pltpu.make_async_copy(gpre_ref.at[:, cols], gpre_s.at[order], own_sems.at[0, order]),
+            pltpu.make_async_copy(act_ref.at[:, cols], act_s.at[order], own_sems.at[1, order]),
+        )
+
+    for y in range(2):
+        for load in loads(y, 2 * y + 1 - core):
+            load.start()
+    for y in range(2):
+        for load in loads(2 + y, 2 * y + core):
+            load.start()
     greet(neighbours(group, place, [other_core]))
 
     @pl.when(group == 1)
@@ -1181,15 +1294,15 @@
     hidden_s[...] = hidden_ref[...].T
     gfeed_s[...] = gfeed_ref[...].T
     att_s[...] = att_ref[...].T
-    width = hidden_s.shape[0]
     split = width // 4
     part = split // 4
     rows = 3 * part
 
-    def blocks(target, y, index):
-        cols = pl.ds(pl.multiple_of(index * width, width), width)
-        up = jnp.dot(hidden_s[...], gpre_ref[:, cols], preferred_element_type=F32).astype(BF16)
-        down = jnp.dot(gfeed_s[...], act_ref[:, cols], preferred_element_type=F32).astype(BF16)
+    def blocks(target, y, index, order):
+        for load in loads(order, index):
+            load.wait()
+        up = jnp.dot(hidden_s[...], gpre_s[order], preferred_element_type=F32).astype(BF16)
+        down = jnp.dot(gfeed_s[...], act_s[order], preferred_element_type=F32).astype(BF16)
         own = jnp.concatenate(
             [
                 att_s[pl.ds(pl.multiple_of(index * part + z * split, 16), part), :]
@@ -1215,7 +1328,7 @@
                     base += size
 
     def send_row(y, carry):
-        blocks(sent, y, 2 * y + 1 - core)
+        blocks(sent, y, 2 * y + 1 - core, y)
         swap(y).start()
         return carry
 
@@ -1230,7 +1343,7 @@
         dos[1, 0] = crossed[0]
 
     def keep_row(y, carry):
-        blocks(held, y, 2 * y + core)
+        blocks(held, y, 2 * y + core, 2 + y)
         return carry
 
     lax.fori_loop(0, 2, keep_row, 0)
@@ -1267,19 +1380,21 @@
     share = (2, 4, BLOCKS, rows, lanes)
     return pl.pallas_call(
         feed_grads_kernel,
-        in_specs=in_vmem(7),
+        in_specs=in_vmem(4) + [pl.BlockSpec(memory_space=pl.ANY)] * 2 + in_vmem(1),
         out_specs=in_vmem(2),
         out_shape=[
             jax.ShapeDtypeStruct(share, BF16),
             jax.ShapeDtypeStruct((2, 4, half, lanes), BF16),
         ],
         scratch_shapes=[pltpu.VMEM((width, tokens), BF16)] * 3
+        + [pltpu.VMEM((4, tokens, width), BF16)] * 2
         + [
             pltpu.VMEM(share, BF16),
             pltpu.VMEM(share, BF16),
             pltpu.VMEM((4, half, lanes), BF16),
             pltpu.SemaphoreType.DMA((15,)),
             pltpu.SemaphoreType.DMA((15,)),
+            pltpu.SemaphoreType.DMA((2, 4)),
         ],
         compiler_params=pltpu.CompilerParams(
             collective_id=3, has_side_effects=True, vmem_limit_bytes=WHOLE_VMEM
@@ -1296,8 +1411,9 @@
 
 def finish_kernel(
     packs, cosine, sine, normed_ref, vec_one, vec_two, middle_sums, up_sums, extra, feed_two,
-    w_ref, x_ref, mgrad_ref, ada_ref, total, feed_total, rows_all, grad_ref,
-    mixed, w_s, x_s, mgrad_s, ada_s, sums, small, sent, got, held, one_p, one_q, two, others,
+    w_ref, x_ref, mgrad_ref, ada_ref,
+    qkv_out, up_out, down_out, out_out, sums_out, ada_out, table_out, grad_ref,
+    total, feed_total, rows_all, mixed, w_s, x_s, mgrad_s, ada_s, sums, small, sent, got, held, one_p, one_q, two, others,
     three, feed_others, feed_three, send_sems, recv_sems, own_sems,
 ):
     group = lax.axis_index("grp")
@@ -1473,16 +1589,41 @@
         hop_mlp(s, (mlp + 4 - s) % 4).wait_recv()
     hop_group(group).start()
     feed_five()
+    share_rows = feed_total.shape[1]
+    part_rows = share_rows // 3
+    for lane in range(tiles):
+        at = slice(lane * lanes, (lane + 1) * lanes)
+        one, two_, three_ = (feed_total[6 * index + lane].astype(F32) for index in range(3))
+        up_out[:share_rows, at] = one
+        up_out[share_rows:, at] = two_[:part_rows]
+        down_out[: 2 * part_rows, at] = two_[part_rows:]
+        down_out[2 * part_rows :, at] = three_[: 2 * part_rows]
+        out_out[:, at] = three_[2 * part_rows :]
     sum_five()
+    for block in range(BLOCKS):
+        qkv_out[:, block * lanes : (block + 1) * lanes] = total[block].astype(F32)
     hop_group(group).wait_send()
     hop_group(1 - group).wait_recv()
+    every = rows_all[...].reshape(32, SMALL_ROWS, lanes)
+    sums_out[...] = jnp.sum(every, axis=0)
+    conditions = every[:, 34].astype(BF16).astype(F32)
+    for line in range(9):
+        ada_out[:, line * lanes : (line + 1) * lanes] = lax.dot_general(
+            conditions, every[:, line], TN, precision=highest, preferred_element_type=F32
+        )
+    table_rows = table_out.shape[0]
+    first_row = (place * 4 + mlp) * table_rows
+    owned = first_row + lax.broadcasted_iota(jnp.int32, (table_rows, 32), 0)
+    steps = every[:, 35].T[:table_rows]
+    chosen = jnp.where(owned.astype(F32) == steps, 1.0, 0.0)
+    table_out[...] = jnp.dot(chosen, every[:, 33], precision=highest, preferred_element_type=F32)
     for index in range(4):
         store(index).wait()
 
 
 def finish(
     packs, cosine, sine, normed, vec_one, vec_two, middle_sums, up_sums, extra, feed_two, weight,
-    x, mgrad, ada_weight,
+    x, mgrad, ada_weight, table_rows,
 ):
     rows = normed.shape[1] // 8
     lanes = 2 * HD
@@ -1494,14 +1635,18 @@
     return pl.pallas_call(
         finish_kernel,
         in_specs=in_vmem(10) + [apart] * 4,
-        out_specs=in_vmem(3) + [apart],
+        out_specs=in_vmem(7) + [apart],
         out_shape=[
-            jax.ShapeDtypeStruct(share[2:], BF16),
-            jax.ShapeDtypeStruct((BLOCKS, feed_rows, lanes), BF16),
-            jax.ShapeDtypeStruct((2, 4, 4, SMALL_ROWS, lanes), F32),
-            jax.ShapeDtypeStruct((tokens, width), F32),
+            jax.ShapeDtypeStruct(shape, F32)
+            for shape in (
+                (width // 16, 3 * width), (width // 4, width), (width // 4, width),
+                (width // 16, width), (SMALL_ROWS, lanes), (lanes, 9 * lanes),
+                (table_rows, lanes), (tokens, width),
+            )
         ],
         scratch_shapes=[
+            pltpu.VMEM(share[2:], BF16), pltpu.VMEM((BLOCKS, feed_rows, lanes), BF16),
+            pltpu.VMEM((2, 4, 4, SMALL_ROWS, lanes), F32),
             pltpu.VMEM((tokens, 3 * width), BF16), like(weight), like(x), like(mgrad),
             like(ada_weight), pltpu.VMEM((8, width), F32), pltpu.VMEM((4, SMALL_ROWS, lanes), F32),
         ]
@@ -1530,51 +1675,38 @@
     place = lax.axis_index("seq")
     group = lax.axis_index("grp")
     mlp_count = lax.axis_size("mlp")
-    second = group == 1
     token_rows, width = tokens.shape[1:]
     half = token_rows // 2
-    heads = width // HD
-    slot = lambda steps: (place + steps) % 4
-    group_row = jnp.full((1,), group, jnp.int32)
-
-    share_units = up_weight.shape[1]
-    bias_rows = jnp.broadcast_to(up_bias[None, :], (16, share_units))
-    feed_weights = lax.all_gather(
-        jnp.concatenate([up_weight, down_weight, bias_rows]), "mlp", axis=0
-    )
-
-    step_value = jnp.sum(jnp.where(jnp.arange(4, dtype=jnp.int32) == place, step_index[0], 0))
-    embedded = lax.dynamic_slice_in_dim(time_table, step_value, 1, 0)[0].astype(F32)
-    condition, silu_back = jax.vjp(jax.nn.silu, embedded)
-    cond_low = condition.astype(BF16)
-    modulation = jnp.dot(cond_low[None, :], ada_weight, preferred_element_type=F32)[
-        0
-    ] + ada_bias.astype(F32)
-    shift_one, scale_one, gate_one, shift_two, scale_two, gate_two = jnp.split(modulation, 6)
-
-    positions = jnp.arange(token_rows, dtype=jnp.int32) + jnp.where(second, place * token_rows, 0)
+    lanes = 2 * HD
+    up_all = lax.all_gather(up_weight, "mlp", axis=0)
+    down_all = lax.all_gather(down_weight, "mlp", axis=0)
+
     frequency = jnp.exp(jnp.arange(HD // 2, dtype=F32) * (-2.0 * math.log(10000.0) / HD))
-    angles = positions.astype(F32)[:, None] * frequency[None, :]
-    cosine, sine = jnp.cos(angles), jnp.sin(angles)
-    cosine = jnp.concatenate([cosine] * 4, axis=1).reshape(2, half, 2 * HD)
-    sine = jnp.concatenate([-sine, sine] * 2, axis=1).reshape(2, half, 2 * HD)
+    frequency = jnp.concatenate([frequency] * 4)[None, :]
+    near_rows = 32
+    offset = jnp.where(group == 1, place * token_rows, 0)
+    far_rows = offset + near_rows * jnp.arange(token_rows // near_rows, dtype=jnp.int32)
+
+    def circle(positions):
+        angles = positions.astype(F32)[:, None] * frequency
+        return jnp.stack([jnp.cos(angles), jnp.sin(angles)])
 
     x2 = tokens.reshape(2, half, width)
-    blank = jnp.zeros((width,), F32)
-    gain_one = first_gain.astype(F32)
-    gain_two = second_gain.astype(F32)
-    vec_one = jnp.stack([gain_one, scale_one, shift_one] + [blank] * 5)
-    vec_two = jnp.stack(
-        [gate_one, gain_two, scale_two, shift_two, gate_two, down_bias.astype(F32), blank, blank]
-    )
-    normed, packs = project(x2, vec_one, qkv_weight, cosine, sine)
-
-    att, pieces, results, logs, logs_own = forward_attention(packs)
+    parameters = jnp.concatenate([ada_bias, first_gain, second_gain, down_bias, up_bias])[None, :]
+    (
+        packs, att, pieces, results, logs, logs_own, cosine, sine, vec_one, vec_two, extra,
+        bias_all, blocks,
+    ) = forward_attention(
+        x2, qkv_weight, circle(jnp.arange(near_rows, dtype=jnp.int32)), circle(far_rows),
+        step_index, time_table, ada_weight, parameters,
+    )
+
     (
         output, att_low, hidden, act, grad_feed, grad_pre, middle_grad, grad_branch, grad_att,
         middle_sums, up_sums,
     ) = middle_pass(
-        x2, cotangent.reshape(2, half, width), att, vec_two, out_weight, feed_weights
+        x2, cotangent.reshape(2, half, width), att, vec_two, out_weight, up_all, down_all,
+        bias_all,
     )
     flat = lambda value: value.reshape(token_rows, value.shape[2])
     feed_held, att_grads = feed_grads(
@@ -1584,65 +1716,38 @@
     grads, feed_two = backward_attention(
         packs, grad_att, att, pieces, results, logs, logs_own, att_grads, feed_held
     )
-    blocks = flat(normed).T.reshape(4, 2, 2, width // 16, token_rows)
-    blocks = jnp.transpose(blocks, (2, 1, 0, 3, 4)).reshape(2, width // 2, token_rows)
-    lanes = 2 * HD
-    extra = jnp.stack(
-        [
-            condition, jnp.full(condition.shape, step_value, F32),
-            silu_back(jnp.ones_like(condition))[0],
-        ]
-        + [jnp.zeros_like(condition)] * 5
-    )
-    qkv_blocks, feed_blocks, rows_all, input_grad = finish(
-        grads, cosine, sine, blocks, vec_one, vec_two, middle_sums, up_sums, extra,
-        feed_two, qkv_weight, flat(x2), flat(middle_grad), ada_weight,
-    )
-    feed_total = feed_blocks.reshape(3, 6, 3 * width // 16, lanes)
-    feed_total = jnp.transpose(feed_total, (0, 2, 1, 3)).reshape(9 * width // 16, width)
-    feed_total = feed_total.astype(F32)
-    qkv_total = jnp.transpose(qkv_blocks, (1, 0, 2)).reshape(width // 16, 3 * width).astype(F32)
-
+    ranks = 4 * mlp_count
+    (
+        qkv_total, up_total, down_total, out_total, row_sums, ada_rows, table_share, input_grad,
+    ) = finish(
+        grads, cosine, sine, blocks, vec_one, vec_two, middle_sums, up_sums, extra, feed_two,
+        qkv_weight, flat(x2), flat(middle_grad), ada_weight, time_table.shape[0] // ranks,
+    )
     mlp = lax.axis_index("mlp")
-    ranks = 4 * mlp_count
     rank = place * mlp_count + mlp
-    rows_all = rows_all.reshape(2 * ranks, SMALL_ROWS, lanes)
-    row_sums = jnp.sum(rows_all, axis=0)
 
     def share(value, index, count):
-        value = value.reshape(value.shape[:-2] + (-1,))
         each = value.shape[-1] // count
         return lax.dynamic_slice_in_dim(value, index * each, each, value.ndim - 1)
 
-    mod_share = share(rows_all[:, 0:9], mlp, mlp_count)
-    up_bias_share = share(row_sums[9:15], mlp, mlp_count)
-    first_share, second_share, down_bias_share = (
-        share(row_sums[start : start + 6], rank, ranks) for start in (15, 21, 27)
-    )
-    cond_all = rows_all[:, 34].astype(BF16).astype(F32)
-    ada_share = lax.dot_general(cond_all, mod_share, TN, precision=highest)
-    table_each = time_table.shape[0] // ranks
-    own_rows = rank * table_each + jnp.arange(table_each, dtype=jnp.int32)
-    chosen = (own_rows[:, None] == rows_all[None, :, 35, 0].astype(jnp.int32)).astype(F32)
-    table_share = jnp.dot(chosen, rows_all[:, 33], precision=highest)
-    split = width // 4
-    up_total = feed_total[:split]
-    down_total = feed_total[split : 2 * split].T
-    out_total = feed_total[2 * split :]
+    mod_sums, up_bias_sums, first_sums, second_sums, down_bias_sums = (
+        row_sums[start:end].reshape(-1)
+        for start, end in ((0, 9), (9, 15), (15, 21), (21, 27), (27, 33))
+    )
     return (
         output.reshape(1, token_rows, width),
         input_grad.reshape(1, token_rows, width),
         table_share,
-        ada_share,
-        jnp.sum(mod_share, axis=0),
-        first_share,
+        share(ada_rows, mlp, mlp_count),
+        share(mod_sums, mlp, mlp_count),
+        share(first_sums, rank, ranks),
         qkv_total,
         out_total,
-        second_share,
+        share(second_sums, rank, ranks),
         up_total,
-        up_bias_share,
-        down_total,
-        down_bias_share,
+        share(up_bias_sums, mlp, mlp_count),
+        down_total.T,
+        share(down_bias_sums, rank, ranks),
     )
 
 

time: 438 us -> 412 us (0.941)
  other arithmetic: 14.7 us -> 0.92 us
  Pallas kernels: 381 us -> 372 us
    pallas_call x4 -> x3, Pallas kernels: 253 us -> 243 us  [the longest x1 92.1 us: forward_attention(): pl.pallas_call(forward_kernel, in_specs=in_vmem(2 + len(rest)), out_specs...]
    unnamed x19 -> x31, local copies, waits for them, and re-layouts: 2.63 us -> 9.27 us
    concatenate x2 -> x1, other arithmetic: 5.04 us -> 0.08 us  [four_shards(): frequency = jnp.concatenate([frequency] * 4)[None, :]]
  transfers between devices with their start and end apart: 1 -> 2, of which waited for: 0 -> 0; matrix products, arithmetic and copies ran while one was open for 3% -> 1% of each run, Pallas kernels for 21% -> 23%
where the time goes in v4:
time: 412 us; the launch traced here: 405 us
  Pallas kernels  372 us (90%)
  local copies, waits for them, and re-layouts  15.7 us (4%)
  between operations  14.4 us (3%)
    pallas_call x1, Pallas kernels, forward_attention(): pl.pallas_call(forward_kernel, in_specs=in_vmem(2 + len(rest)), out_specs...  92.1 us
    pallas_call x1, Pallas kernels, backward_attention(): pl.pallas_call(backward_kernel, in_specs=[pl.BlockSpec(memory_space=pl.AN...  91.1 us
    pallas_call x1, Pallas kernels, finish(): pl.pallas_call(finish_kernel, in_specs=in_vmem(10) + [apart] * 4, out_spe...  90.6 us
    pallas_call x1, Pallas kernels, feed_grads(): pl.pallas_call(feed_grads_kernel, in_specs=in_vmem(4) + [pl.BlockSpec(mem...  60.3 us
    pallas_call x1, Pallas kernels, middle_pass(): pl.pallas_call(middle_kernel, grid=(half // rows,), in_specs=[tok(width),...  38.2 us
    unnamed x31, local copies, waits for them, and re-layouts  9.27 us
  transfers between devices with their start and end apart: 2, of which 0 were waited for; matrix products, arithmetic and copies ran while one was open for 1% of the time, Pallas kernels for 23%

profile of v4, /device:TPU:0, one launch (start us, length us, event | category | flops | bytes accessed | tf_op | source)
XLA Modules:
  0.0 404.8 jit_solution(12814052971104101944)
XLA Ops:
  7.2 0.0 copy-start.5
  7.2 0.0 copy-start.6
  7.2 0.0 copy-start.7
  7.2 0.0 copy-start.8
  7.2 0.0 copy-start.9
  7.2 0.0 all-gather.5.cloned.1.call-start
  7.3 0.7 all-gather.5.cloned.1.call-update
  8.0 0.0 all-gather.7.cloned.1.call-start
  8.0 0.7 all-gather.7.cloned.1.call-update
  8.8 0.1 pad_maximum_fusion.2
  8.9 0.0 copy-done.5
  8.9 0.3 dynamic-update-slice
  9.2 0.0 copy-done.6
  9.2 0.2 dynamic-update-slice.1
  9.4 0.0 copy-done.7
  9.4 0.2 dynamic-update-slice.2
  9.6 0.0 copy-done.8
  9.6 0.2 dynamic-update-slice.3
  9.8 0.0 copy-done.9
  9.9 0.2 dynamic-update-slice.4
  10.1 0.6 broadcast_in_dim.2.params_ref
  10.7 0.2 multiply_cosine_fusion
  10.9 0.6 pad_maximum_fusion
  11.5 92.1 %forward_attention.1 = (bf16[12,3,512,128]{3,2,1,0:T(8,128)(2,1)}, bf16[12,512,128]{2,1,0:T(8,128)(2,1)}, bf16[2,4,3,512,128]{4,3,2,1,0:T(8,128)(2,1)}, bf16[2,4...) custom-call(bf16[2,512,768]{2,1,0:T(8,128)(2,1)} %bitcast.29, ...), custom_call_target="tpu_custom_call" | custom-call | flops 99999997952 | bytes 8000000 | tf_op jit(solution)/shard_map/forward_attention/pallas_call | solution.py:859
  103.6 0.0 all-gather.5.cloned.1.call-done
  103.6 0.0 all-gather.7.cloned.1.call-done
  103.7 38.2 %middle_pass.1 = (bf16[2,512,768]{2,1,0:T(8,128)(2,1)}, bf16[2,512,768]{2,1,0:T(8,128)(2,1)}, bf16[2,512,768]{2,1,0:T(8,128)(2,1)}, bf16[2,512,3072]{2,1,0:T(8,1...) custom-call(bf16[2,512,768]{2,1,0:T(8,128)(2,1)} %bitcast.30, ...), custom_call_target="tpu_custom_call" | custom-call | tf_op jit(solution)/shard_map/middle_pass/pallas_call | solution.py:1218
  141.9 60.3 %feed_grads.1 = (bf16[2,4,18,144,128]{4,3,2,1,0:T(8,128)(2,1)}, bf16[2,4,512,128]{3,2,1,0:T(8,128)(2,1)}) custom-call(bf16[1024,768]{1,0:T(8,128)(2,1)} %bitcast.38, bf16[1024,768]{1,0:T(8,128)(2,1)} %bitcast.39, bf16[1024,768]{1,0:T(8,128)(2,1)} %bitcast.37, bf16[1024,768]{1,0:T(8,128)(2,1)} %bitcast.40, bf16[1024,3072]{1,0:T(8,128)(2,1)} %bitcast.33, ...), custom_call_target="tpu_custom_call" | custom-call | flops 24000000000 | bytes 20000000 | tf_op jit(solution)/shard_map/feed_grads/pallas_call | solution.py:1381
  202.2 91.1 %backward_attention.1 = (bf16[12,3,512,128]{3,2,1,0:T(8,128)(2,1)}, bf16[4,9,144,128]{3,2,1,0:T(8,128)(2,1)}) custom-call(bf16[12,3,512,128]{3,2,1,0:T(8,128)(2,1)} %get-tuple-element.53.packs_ref, bf16[12,512,128]{2,1,0:T(8,128)(2,1)} %get-tuple-element.54.gatt.gatt_ref, bf16[12,512,128]{2,1,0:T(8,128)(2,1)} %get-tuple-element.49.att_ref, ...), custom_call_target="tpu_custom_call" | custom-call | flops 120000004096 | bytes 8000000 | tf_op jit(solution)/shard_map/backward_attention/pallas_call | solution.py:1090
  293.3 90.6 %finish.1 = (f32[48,2304]{1,0:T(8,128)}, f32[192,768]{1,0:T(8,128)}, f32[192,768]{1,0:T(8,128)}, f32[48,768]{1,0:T(8,128)}, f32[40,128]{1,0:T(8,128)}, /*index=5...) custom-call(bf16[12,3,512,128]{3,2,1,0:T(8,128)(2,1)} %get-tuple-element.67.packs, ...), custom_call_target="tpu_custom_call" | custom-call | flops 60000002048 | bytes 20000000 | tf_op jit(solution)/shard_map/finish/pallas_call | solution.py:1635
  383.9 0.8 slice_bitcast_fusion.1
  384.7 0.7 slice_bitcast_fusion
  385.4 1.1 constant_dynamic-slice_fusion
  386.5 0.8 copy.27
  387.2 0.6 dynamic_slice.20
  387.8 0.6 dynamic_slice.21
  388.4 0.6 dynamic_slice.23
  389.0 0.7 dynamic_slice.19
  389.6 0.6 dynamic_slice.22
  390.3 0.0 copy-start.4
  390.3 0.0 copy-start.2
  390.3 0.0 copy-start.3
  390.3 3.8 copy.39
  394.1 0.0 copy-done.4
  394.1 0.0 copy-start.1
  394.1 0.0 copy-start
  394.1 0.6 copy.40
  394.7 0.0 copy-done.2
  394.7 0.8 copy.41
  395.5 0.0 copy-done.3
  395.5 0.7 copy.42
  396.2 0.0 copy-done.1
  396.2 0.8 copy.43
  397.0 0.0 copy-done
  397.0 0.8 copy.44
  (4 shorter events, 0.0 us)
Async XLA Ops:
  7.2 1.7 copy-start.5
  7.2 2.0 copy-start.6
  7.2 2.2 copy-start.7
  7.2 2.4 copy-start.8
  7.2 2.6 copy-start.9
  7.2 96.4 %all-gather.5.cloned.1.call-start = ((), (), s32[]{:S(2)}) async-start(), calls=%async_computation | async-start | bytes 5898240 | tf_op jit(solution)/shard_map/all_gather | solution.py:1681
  8.0 95.7 %all-gather.7.cloned.1.call-start = ((), (), s32[]{:S(2)}) async-start(), calls=%async_computation.1 | async-start | bytes 5898240 | tf_op jit(solution)/shard_map/all_gather | solution.py:1682
  390.3 3.8 copy-start.4
  390.3 4.4 %copy-start.2 = (f32[48,2304]{1,0:T(8,128)S(1)}, f32[48,2304]{1,0:T(8,128)}, u32[]{:S(2)}) copy-start(f32[48,2304]{1,0:T(8,128)} %get-tuple-element.129) | copy-start | bytes 1327108
  390.3 5.2 %copy-start.3 = (f32[48,768]{1,0:T(8,128)S(1)}, f32[48,768]{1,0:T(8,128)}, u32[]{:S(2)}) copy-start(f32[48,768]{1,0:T(8,128)} %get-tuple-element.130) | copy-start | bytes 442372
  394.1 2.1 copy-start.1
  394.1 2.9 copy-start
Sparse Core Ops, SparseCore 0:
  9.6 40.6 all-gather.4
  51.9 36.9 all-gather.6

commit v5 on v4

--- a/solution.py
+++ b/solution.py
@@ -455,7 +455,6 @@
 
 
 def sum_steps(held, one_p, one_q, two, others, three, out, sems, base, near=None):
-    near = held if near is None else near
     group = lax.axis_index("grp")
     place = lax.axis_index("seq")
     row, _, other_row, _ = mlp_place()
@@ -506,9 +505,11 @@
         arrive(1)
 
         def add(z, carry):
-            one_p[z] = added(near[row, z, 0:10], one_p[z])
+            own = held[row, z, 0:10] if near is None else near[0][z]
+            one_p[z] = added(own, one_p[z])
             for y in range(2):
-                one_q[y, z] = added(near[y, z, pl.ds(10 + 4 * group, 4)], one_q[y, z])
+                own = held[y, z, pl.ds(10 + 4 * group, 4)] if near is None else near[1][y, z]
+                one_q[y, z] = added(own, one_q[y, z])
             return carry
 
         lax.fori_loop(0, 4, add, 0)
@@ -559,8 +560,9 @@
 
 def forward_kernel(
     x_ref, w_ref, near, far, step_ref, table, ada_ref, params_ref,
-    packs, att, pieces, results, logs, logs_own, cosine, sine, vec_one, vec_two, extra, bias_all,
-    blocks, crossed, normed_s, k_s, v_s, send_sems, recv_sems,
+    packs_out, att, pieces, results, logs, logs_own, cosine, sine, vec_one, vec_two, extra,
+    bias_all, blocks_out, packs, blocks, crossed, normed_s, k_s, v_s, send_sems, recv_sems,
+    own_sems,
 ):
     group = lax.axis_index("grp")
     place = lax.axis_index("seq")
@@ -729,32 +731,32 @@
                 start = ((z * 2 + y) * 2 + which) * part_rows
                 at = (y * 4 + z) * part_rows
                 blocks[which, at : at + part_rows, :] = flipped[start : start + part_rows]
+    stores = (
+        pltpu.make_async_copy(packs, packs_out, own_sems.at[0]),
+        pltpu.make_async_copy(blocks, blocks_out, own_sems.at[1]),
+    )
+    for store in stores:
+        store.start()
 
     @pl.when(group == 1)
     def _():
         pieces[0, 0] = packs[2 * place]
         pieces[1, 0] = packs[2 * place + 1]
-        for s in (1, 2, 3):
+        for s in (1, 3, 2):
             first(s).wait_send()
-        for s in (1, 2, 3):
             second_values(s).start()
         for s in (1, 2, 3):
+            second_queries(s).start()
+        for s in (1, 2, 3):
             first(s).wait_recv()
 
         def before(s):
-            @pl.when(s == 3)
-            def _():
-                for other in (1, 2, 3):
-                    second_queries(other).start()
+            pass
 
         def after(s):
             @pl.when(s == 0)
             def _():
                 att[2 * place] = results[0, 0]
-
-            @pl.when(s > 0)
-            def _():
-                home(0, s, 2 * place).start()
 
         full(0, 2 * place, before, after)
         for s in (1, 2, 3):
@@ -796,6 +798,8 @@
         @pl.when((group == 1) & (s == 0))
         def _():
             att[2 * place + 1] = results[1, 0]
+            for other in (1, 2, 3):
+                home(0, other, 2 * place).start()
 
         @pl.when((group == 1) & (s > 0))
         def _():
@@ -832,6 +836,8 @@
     for s in (1, 2, 3):
         share_bias(s, mlp).wait_send()
         share_bias(s, (mlp + 4 - s) % 4).wait_recv()
+    for store in stores:
+        store.wait()
 
 
 def in_vmem(count):
@@ -859,15 +865,20 @@
     return pl.pallas_call(
         forward_kernel,
         in_specs=in_vmem(2 + len(rest)),
-        out_specs=in_vmem(len(shapes)),
+        out_specs=[pl.BlockSpec(memory_space=pl.ANY)]
+        + in_vmem(len(shapes) - 2)
+        + [pl.BlockSpec(memory_space=pl.ANY)],
         out_shape=[jax.ShapeDtypeStruct(shape, kind) for shape, kind in shapes],
         scratch_shapes=[
+            pltpu.VMEM(shapes[0][0], BF16),
+            pltpu.VMEM(shapes[-1][0], BF16),
             pltpu.VMEM((4, 3, half, lanes), BF16),
             pltpu.VMEM((2, half, width), BF16),
             pltpu.VMEM((8 * half, lanes), BF16),
             pltpu.VMEM((8 * half, lanes), BF16),
             pltpu.SemaphoreType.DMA((31,)),
             pltpu.SemaphoreType.DMA((31,)),
+            pltpu.SemaphoreType.DMA((2,)),
         ],
         compiler_params=pltpu.CompilerParams(
             collective_id=1, has_side_effects=True, vmem_limit_bytes=WHOLE_VMEM
@@ -904,14 +915,14 @@
 
 
 def backward_kernel(
-    packs_ref, gatt_ref, att_ref, held_ref, pieces, results, logs, logs_own, dos, back, two,
-    packs, gatt, att, held, staged, q_s, k_s, v_s, do_s, delta_s, dq_s, one_p, one_q,
+    packs_ref, gatt_ref, att_ref, logs_ref, held_ref, pieces, results, logs, dos, back, two,
+    packs, gatt, att, logs_own, near_p, near_q, staged, q_s, k_s, v_s, do_s, delta_s, dq_s, one_p, one_q,
     send_sems, recv_sems, own_sems,
 ):
     group = lax.axis_index("grp")
     place = lax.axis_index("seq")
     sems = (send_sems, recv_sems)
-    heads = packs.shape[0]
+    heads = packs_ref.shape[0]
     rows = 2 * packs.shape[2]
     scale = 1.0 / math.sqrt(HD)
     ahead = lambda s: (place + s) % 4
@@ -930,22 +941,33 @@
 
     greet(neighbours(group, place, [mlp_place()[2]]))
     sum_one, sum_two, sum_three, _, _, _ = sum_steps(
-        held_ref, one_p, one_q, two, None, None, None, sems, 24, held
+        held_ref, one_p, one_q, two, None, None, None, sems, 24, (near_p, near_q)
     )
     sum_one()
-    load_held = pltpu.make_async_copy(held_ref, held, own_sems.at[3])
-    load_held.start()
-    local_loads = [
-        pltpu.make_async_copy(source, target, own_sems.at[index])
-        for index, (source, target) in enumerate(
-            ((packs_ref, packs), (gatt_ref, gatt), (att_ref, att))
-        )
-    ]
-
-    @pl.when(group == 0)
-    def _():
-        for load in local_loads:
-            load.start()
+    held_loads = (
+        pltpu.make_async_copy(
+            held_ref.at[mlp_place()[0], :, pl.ds(0, 10)], near_p, own_sems.at[0]
+        ),
+        pltpu.make_async_copy(
+            held_ref.at[:, :, pl.ds(10 + 4 * group, 4)], near_q, own_sems.at[1]
+        ),
+    )
+    for load in held_loads:
+        load.start()
+
+    def sum_over_rows():
+        for load in held_loads:
+            load.wait()
+        sum_two()
+
+    def local_loads(head):
+        slot = head % 2
+        return [
+            pltpu.make_async_copy(source.at[head], target.at[slot], own_sems.at[2 + 4 * slot + n])
+            for n, (source, target) in enumerate(
+                ((packs_ref, packs), (gatt_ref, gatt), (att_ref, att), (logs_ref, logs_own))
+            )
+        ]
 
     def full(sel, put_values, put_queries):
         for s in range(4):
@@ -953,12 +975,13 @@
                 pieces.at[sel, s], dos[sel, s], results[sel, s], s * rows, *stores
             )
 
-        def step(s, carry):
-            block = pl.ds(pl.multiple_of(s * rows, rows), rows)
+        def step(turn_index, last):
+            s = 0 if last else (turn_index + 1) % 4
+            block = pl.ds(0 if last else pl.multiple_of(s * rows, rows), rows)
             k = k_s[block, :]
             v = v_s[block, :]
             dk = dv = None
-            for index in range(4):
+            for index in (1, 2, 3, 0):
                 chunk = slice(index * rows, (index + 1) * rows)
                 dq, dk_part, dv_part = tile_grads(
                     q_s[chunk, :], do_s[chunk, :], k, v, logs[sel, index, 0:1, :],
@@ -966,17 +989,29 @@
                 )
                 dk = dk_part if dk is None else dk + dk_part
                 dv = dv_part if dv is None else dv + dv_part
-                dq_s[:, chunk] = jnp.where(s == 0, dq, dq_s[:, chunk] + dq)
+                if last:
+                    dq = dq_s[:, chunk] + dq
+                    staged[sel, index, 0] = fold(dq.T * scale).astype(BF16)
+                    put_queries(index)
+                else:
+                    dq_s[:, chunk] = jnp.where(turn_index == 0, dq, dq_s[:, chunk] + dq)
             staged[sel, s, 1] = fold(dk * scale).astype(BF16)
             staged[sel, s, 2] = fold(dv).astype(BF16)
             put_values(s)
+
+        def one_turn(turn_index, carry):
+            step(turn_index, False)
             return carry
 
-        lax.fori_loop(0, 4, step, 0)
-        for s in (3, 2, 1, 0):
-            chunk = slice(s * rows, (s + 1) * rows)
-            staged[sel, s, 0] = fold(dq_s[:, chunk].T * scale).astype(BF16)
-            put_queries(s)
+        if sel:
+            lax.fori_loop(0, 3, one_turn, 0)
+            step(3, True)
+        else:
+            lax.fori_loop(0, 4, one_turn, 0)
+            for index in (1, 2, 3, 0):
+                chunk = slice(index * rows, (index + 1) * rows)
+                staged[sel, index, 0] = fold(dq_s[:, chunk].T * scale).astype(BF16)
+                put_queries(index)
 
     @pl.when(group == 1)
     def _():
@@ -992,10 +1027,9 @@
             def _():
                 home_values(0, s, head).start()
 
-            @pl.when(s == 2)
+            @pl.when(s == 0)
             def _():
-                load_held.wait()
-                sum_two()
+                sum_over_rows()
 
         def put_queries(s):
             if s == 0:
@@ -1021,38 +1055,47 @@
         def _():
             home_values(2, s, 8 + place).start()
 
-        @pl.when((group == 0) & (s == 2))
+        @pl.when((group == 0) & (s == 3))
         def _():
-            load_held.wait()
-            sum_two()
+            sum_over_rows()
 
     def put_queries(s):
-        head = 2 * place + 1
+        if s:
+            head = group * (2 * place + 1) + (1 - group) * (8 + place)
+            reach(
+                staged.at[1, s, 0], back.at[head, 0], sems, 20 - 4 * group + s, 1, behind(s)
+            ).start()
+            return
 
         @pl.when(group == 1)
         def _():
-            if s == 0:
-                back[head, 0] = staged[1, 0, 0]
-            else:
-                home_queries(1, s, head).start()
+            back[2 * place + 1, 0] = staged[1, 0, 0]
 
         @pl.when(group == 0)
         def _():
-            home_queries(2, s, 8 + place).start()
+            home_queries(2, 0, 8 + place).start()
 
     full(1, put_values, put_queries)
 
     @pl.when(group == 0)
     def _():
-        for load in local_loads:
-            load.wait()
+        for load in local_loads(0):
+            load.start()
 
         def local(head, carry):
-            load_backward(packs.at[head], gatt[head], att[head], 0, *stores)
+            @pl.when(head + 1 < heads)
+            def _():
+                for load in local_loads(head + 1):
+                    load.start()
+
+            for load in local_loads(head):
+                load.wait()
+            slot = head % 2
+            load_backward(packs.at[slot], gatt[slot], att[slot], 0, *stores)
             own = slice(0, rows)
             dq, dk, dv = tile_grads(
                 q_s[own, :], do_s[own, :], k_s[own, :], v_s[own, :],
-                logs_own[head, 0:1, :], delta_s[0:1, own],
+                logs_own[slot, 0:1, :], delta_s[0:1, own],
             )
             back[head, 0] = fold(dq.T * scale).astype(BF16)
             back[head, 1] = fold(dk * scale).astype(BF16)
@@ -1089,19 +1132,23 @@
     share = held.shape[2:]
     return pl.pallas_call(
         backward_kernel,
-        in_specs=[pl.BlockSpec(memory_space=pl.ANY)] * 4 + in_vmem(5),
+        in_specs=[pl.BlockSpec(memory_space=pl.ANY)] * 5 + in_vmem(4),
         out_specs=in_vmem(2),
         out_shape=[
             jax.ShapeDtypeStruct((heads, 3, half, lanes), BF16),
             jax.ShapeDtypeStruct((4, 9) + share[1:], BF16),
         ],
-        scratch_shapes=[pltpu.VMEM(value.shape, BF16) for value in (packs, gatt, att, held)]
+        scratch_shapes=[
+            pltpu.VMEM((2,) + value.shape[1:], value.dtype)
+            for value in (packs, gatt, att, logs_own)
+        ]
+        + sum_scratch(share[1], EARLY)
         + [pltpu.VMEM((2, 4, 3, half, lanes), BF16)]
         + [pltpu.VMEM((8 * half, lanes), BF16)] * 4
         + [pltpu.VMEM((8, 8 * half), F32), pltpu.VMEM((lanes, 8 * half), F32)]
         + sum_scratch(share[1], EARLY)
         + [pltpu.SemaphoreType.DMA((28,))] * 2
-        + [pltpu.SemaphoreType.DMA((4,))],
+        + [pltpu.SemaphoreType.DMA((10,))],
         compiler_params=pltpu.CompilerParams(
             collective_id=2, has_side_effects=True, vmem_limit_bytes=WHOLE_VMEM
         ),
@@ -1109,7 +1156,7 @@
             flops=120_000_000_000, bytes_accessed=8_000_000, transcendentals=0
         ),
         name="backward_attention",
-    )(packs, gatt, att, held, pieces, results, logs, logs_own, dos)
+    )(packs, gatt, att, logs_own, held, pieces, results, logs, dos)
 
 
 def whole(shape):
@@ -1144,10 +1191,12 @@
     hidden_ref[...] = hidden.reshape(2, rows, width)
     shares, _, chunk = up_ref.shape
     feed = None
+    following = jnp.dot(hidden, up_ref[0], preferred_element_type=F32)
     for index in range(shares):
         cols = slice(index * chunk, (index + 1) * chunk)
-        pre = jnp.dot(hidden, up_ref[index], preferred_element_type=F32)
-        pre = pre + bias_ref[index, 0:1]
+        pre = following + bias_ref[index, 0:1]
+        if index + 1 < shares:
+            following = jnp.dot(hidden, up_ref[index + 1], preferred_element_type=F32)
         square = pre * pre
         root = math.sqrt(2.0 / math.pi)
         tanh = jnp.tanh(pre * (root + (root * 0.044715) * square))
@@ -1497,7 +1546,6 @@
 
         lax.fori_loop(0, 4, add, 0)
     sum_one()
-    feed_four()
     for load in loads:
         load.wait()
     chunk = half // 2
@@ -1518,6 +1566,8 @@
         store(index).start()
         sums[0:1, :] += jnp.sum(gnormed, axis=0, keepdims=True)
         sums[1:2, :] += jnp.sum(gnormed * n, axis=0, keepdims=True)
+        if index == 1:
+            feed_four()
         if index == 2:
             sum_two()
 
@@ -1579,15 +1629,6 @@
     rows_all[group, mlp, place] = small[place]
     sum_three()
     sum_over()
-    for s in (1, 2, 3):
-        hop_place_in(s).wait()
-    for s in (1, 2, 3):
-        hop_mlp(s, mlp).start()
-    sum_four()
-    for s in (1, 2, 3):
-        hop_mlp(s, mlp).wait_send()
-        hop_mlp(s, (mlp + 4 - s) % 4).wait_recv()
-    hop_group(group).start()
     feed_five()
     share_rows = feed_total.shape[1]
     part_rows = share_rows // 3
@@ -1599,6 +1640,15 @@
         down_out[: 2 * part_rows, at] = two_[part_rows:]
         down_out[2 * part_rows :, at] = three_[: 2 * part_rows]
         out_out[:, at] = three_[2 * part_rows :]
+    for s in (1, 2, 3):
+        hop_place_in(s).wait()
+    for s in (1, 2, 3):
+        hop_mlp(s, mlp).start()
+    sum_four()
+    for s in (1, 2, 3):
+        hop_mlp(s, mlp).wait_send()
+        hop_mlp(s, (mlp + 4 - s) % 4).wait_recv()
+    hop_group(group).start()
     sum_five()
     for block in range(BLOCKS):
         qkv_out[:, block * lanes : (block + 1) * lanes] = total[block].astype(F32)

time: 412 us -> 399 us (0.968)
  Pallas kernels: 372 us -> 358 us
    pallas_call x1, Pallas kernels: 90.6 us -> 70.3 us  [finish(): pl.pallas_call(finish_kernel, in_specs=in_vmem(10) + [apart] * 4, out_spe...]
    pallas_call x1, Pallas kernels: 91.1 us -> 100 us  [backward_attention(): pl.pallas_call(backward_kernel, in_specs=[pl.BlockSpec(memory_space=pl.AN...]
where the time goes in v5:
time: 399 us; the launch traced here: 391 us
  Pallas kernels  358 us (90%)
  local copies, waits for them, and re-layouts  15.7 us (4%)
  between operations  14.4 us (4%)
    pallas_call x1, Pallas kernels, backward_attention(): pl.pallas_call(backward_kernel, in_specs=[pl.BlockSpec(memory_space=pl.AN...  100 us
    pallas_call x1, Pallas kernels, forward_attention(): pl.pallas_call(forward_kernel, in_specs=in_vmem(2 + len(rest)), out_specs...  89.9 us
    pallas_call x1, Pallas kernels, finish(): pl.pallas_call(finish_kernel, in_specs=in_vmem(10) + [apart] * 4, out_spe...  70.3 us
    pallas_call x1, Pallas kernels, feed_grads(): pl.pallas_call(feed_grads_kernel, in_specs=in_vmem(4) + [pl.BlockSpec(mem...  59.2 us
    pallas_call x1, Pallas kernels, middle_pass(): pl.pallas_call(middle_kernel, grid=(half // rows,), in_specs=[tok(width),...  38.5 us
    unnamed x31, local copies, waits for them, and re-layouts  9.27 us
  transfers between devices with their start and end apart: 2, of which 0 were waited for; matrix products, arithmetic and copies ran while one was open for 1% of the time, Pallas kernels for 23%

profile of v5, /device:TPU:0, one launch (start us, length us, event | category | flops | bytes accessed | tf_op | source)
XLA Modules:
  0.0 390.9 jit_solution(16789540427137007796)
XLA Ops:
  7.2 0.0 copy-start.5
  7.2 0.0 copy-start.6
  7.2 0.0 copy-start.7
  7.2 0.0 copy-start.8
  7.2 0.0 copy-start.9
  7.2 0.0 all-gather.5.cloned.1.call-start
  7.3 0.7 all-gather.5.cloned.1.call-update
  8.0 0.0 all-gather.7.cloned.1.call-start
  8.0 0.7 all-gather.7.cloned.1.call-update
  8.8 0.1 pad_maximum_fusion.2
  8.9 0.0 copy-done.5
  8.9 0.3 dynamic-update-slice
  9.2 0.0 copy-done.6
  9.2 0.2 dynamic-update-slice.1
  9.4 0.0 copy-done.7
  9.4 0.2 dynamic-update-slice.2
  9.6 0.0 copy-done.8
  9.6 0.2 dynamic-update-slice.3
  9.8 0.0 copy-done.9
  9.9 0.2 dynamic-update-slice.4
  10.1 0.6 broadcast_in_dim.2.params_ref
  10.7 0.2 multiply_cosine_fusion
  10.9 0.6 pad_maximum_fusion
  11.5 89.9 %forward_attention.1 = (bf16[12,3,512,128]{3,2,1,0:T(8,128)(2,1)}, bf16[12,512,128]{2,1,0:T(8,128)(2,1)}, bf16[2,4,3,512,128]{4,3,2,1,0:T(8,128)(2,1)}, bf16[2,4...) custom-call(bf16[2,512,768]{2,1,0:T(8,128)(2,1)} %bitcast.29, ...), custom_call_target="tpu_custom_call" | custom-call | flops 99999997952 | bytes 8000000 | tf_op jit(solution)/shard_map/forward_attention/pallas_call | solution.py:865
  101.5 0.0 all-gather.5.cloned.1.call-done
  101.5 0.0 all-gather.7.cloned.1.call-done
  101.5 38.5 %middle_pass.1 = (bf16[2,512,768]{2,1,0:T(8,128)(2,1)}, bf16[2,512,768]{2,1,0:T(8,128)(2,1)}, bf16[2,512,768]{2,1,0:T(8,128)(2,1)}, bf16[2,512,3072]{2,1,0:T(8,1...) custom-call(bf16[2,512,768]{2,1,0:T(8,128)(2,1)} %bitcast.30, ...), custom_call_target="tpu_custom_call" | custom-call | tf_op jit(solution)/shard_map/middle_pass/pallas_call | solution.py:1267
  140.0 59.2 %feed_grads.1 = (bf16[2,4,18,144,128]{4,3,2,1,0:T(8,128)(2,1)}, bf16[2,4,512,128]{3,2,1,0:T(8,128)(2,1)}) custom-call(bf16[1024,768]{1,0:T(8,128)(2,1)} %bitcast.38, bf16[1024,768]{1,0:T(8,128)(2,1)} %bitcast.39, bf16[1024,768]{1,0:T(8,128)(2,1)} %bitcast.37, bf16[1024,768]{1,0:T(8,128)(2,1)} %bitcast.40, bf16[1024,3072]{1,0:T(8,128)(2,1)} %bitcast.33, ...), custom_call_target="tpu_custom_call" | custom-call | flops 24000000000 | bytes 20000000 | tf_op jit(solution)/shard_map/feed_grads/pallas_call | solution.py:1430
  199.3 100.4 %backward_attention.1 = (bf16[12,3,512,128]{3,2,1,0:T(8,128)(2,1)}, bf16[4,9,144,128]{3,2,1,0:T(8,128)(2,1)}) custom-call(bf16[12,3,512,128]{3,2,1,0:T(8,128)(2,1)} %get-tuple-element.53.packs_ref, bf16[12,512,128]{2,1,0:T(8,128)(2,1)} %get-tuple-element.54.gatt.gatt_ref, bf16[12,512,128]{2,1,0:T(8,128)(2,1)} %get-tuple-element.49.att_ref, ...), custom_call_target="tpu_custom_call" | custom-call | flops 120000004096 | bytes 8000000 | tf_op jit(solution)/shard_map/backward_attention/pallas_call | solution.py:1133
  299.7 70.3 %finish.1 = (f32[48,2304]{1,0:T(8,128)}, f32[192,768]{1,0:T(8,128)}, f32[192,768]{1,0:T(8,128)}, f32[48,768]{1,0:T(8,128)}, f32[40,128]{1,0:T(8,128)}, /*index=5...) custom-call(bf16[12,3,512,128]{3,2,1,0:T(8,128)(2,1)} %get-tuple-element.67.packs, ...), custom_call_target="tpu_custom_call" | custom-call | flops 60000002048 | bytes 20000000 | tf_op jit(solution)/shard_map/finish/pallas_call | solution.py:1685
  370.0 0.8 slice_bitcast_fusion.1
  370.8 0.7 slice_bitcast_fusion
  371.5 1.1 constant_dynamic-slice_fusion
  372.6 0.8 copy.27
  373.4 0.6 dynamic_slice.20
  373.9 0.6 dynamic_slice.21
  374.5 0.6 dynamic_slice.23
  375.1 0.7 dynamic_slice.19
  375.8 0.6 dynamic_slice.22
  376.4 0.0 copy-start.4
  376.4 0.0 copy-start.2
  376.4 0.0 copy-start.3
  376.4 3.8 copy.39
  380.2 0.0 copy-done.4
  380.2 0.0 copy-start.1
  380.2 0.0 copy-start
  380.2 0.6 copy.40
  380.8 0.0 copy-done.2
  380.8 0.8 copy.41
  381.6 0.0 copy-done.3
  381.6 0.7 copy.42
  382.3 0.0 copy-done.1
  382.3 0.8 copy.43
  383.1 0.0 copy-done
  383.1 0.8 copy.44
  (4 shorter events, 0.0 us)
Async XLA Ops:
  7.2 1.7 copy-start.5
  7.2 2.0 copy-start.6
  7.2 2.2 copy-start.7
  7.2 2.4 copy-start.8
  7.2 2.6 copy-start.9
  7.2 94.3 %all-gather.5.cloned.1.call-start = ((), (), s32[]{:S(2)}) async-start(), calls=%async_computation | async-start | bytes 5898240 | tf_op jit(solution)/shard_map/all_gather | solution.py:1731
  8.0 93.5 %all-gather.7.cloned.1.call-start = ((), (), s32[]{:S(2)}) async-start(), calls=%async_computation.1 | async-start | bytes 5898240 | tf_op jit(solution)/shard_map/all_gather | solution.py:1732
  376.4 3.8 copy-start.4
  376.4 4.4 %copy-start.2 = (f32[48,2304]{1,0:T(8,128)S(1)}, f32[48,2304]{1,0:T(8,128)}, u32[]{:S(2)}) copy-start(f32[48,2304]{1,0:T(8,128)} %get-tuple-element.129) | copy-start | bytes 1327108
  376.4 5.2 %copy-start.3 = (f32[48,768]{1,0:T(8,128)S(1)}, f32[48,768]{1,0:T(8,128)}, u32[]{:S(2)}) copy-start(f32[48,768]{1,0:T(8,128)} %get-tuple-element.130) | copy-start | bytes 442372
  380.2 2.1 copy-start.1
  380.2 2.9 copy-start
Sparse Core Ops, SparseCore 0:
  9.6 40.6 all-gather.4
  51.9 36.9 all-gather.6

commit v6 on v5

--- a/solution.py
+++ b/solution.py
@@ -1566,8 +1566,6 @@
         store(index).start()
         sums[0:1, :] += jnp.sum(gnormed, axis=0, keepdims=True)
         sums[1:2, :] += jnp.sum(gnormed * n, axis=0, keepdims=True)
-        if index == 1:
-            feed_four()
         if index == 2:
             sum_two()
 
@@ -1629,6 +1627,16 @@
     rows_all[group, mlp, place] = small[place]
     sum_three()
     sum_over()
+    feed_four()
+    for s in (1, 2, 3):
+        hop_place_in(s).wait()
+    for s in (1, 2, 3):
+        hop_mlp(s, mlp).start()
+    sum_four()
+    for s in (1, 2, 3):
+        hop_mlp(s, mlp).wait_send()
+        hop_mlp(s, (mlp + 4 - s) % 4).wait_recv()
+    hop_group(group).start()
     feed_five()
     share_rows = feed_total.shape[1]
     part_rows = share_rows // 3
@@ -1640,15 +1648,6 @@
         down_out[: 2 * part_rows, at] = two_[part_rows:]
         down_out[2 * part_rows :, at] = three_[: 2 * part_rows]
         out_out[:, at] = three_[2 * part_rows :]
-    for s in (1, 2, 3):
-        hop_place_in(s).wait()
-    for s in (1, 2, 3):
-        hop_mlp(s, mlp).start()
-    sum_four()
-    for s in (1, 2, 3):
-        hop_mlp(s, mlp).wait_send()
-        hop_mlp(s, (mlp + 4 - s) % 4).wait_recv()
-    hop_group(group).start()
     sum_five()
     for block in range(BLOCKS):
         qkv_out[:, block * lanes : (block + 1) * lanes] = total[block].astype(F32)

time: 399 us -> 389 us (0.975)
  Pallas kernels: 358 us -> 351 us
    pallas_call x1, Pallas kernels: 70.3 us -> 62.9 us  [finish(): pl.pallas_call(finish_kernel, in_specs=in_vmem(10) + [apart] * 4, out_spe...]
where the time goes in v6:
time: 389 us; the launch traced here: 383 us
  Pallas kernels  351 us (90%)
  local copies, waits for them, and re-layouts  15.7 us (4%)
  between operations  14.4 us (4%)
    pallas_call x1, Pallas kernels, backward_attention(): pl.pallas_call(backward_kernel, in_specs=[pl.BlockSpec(memory_space=pl.AN...  100 us
    pallas_call x1, Pallas kernels, forward_attention(): pl.pallas_call(forward_kernel, in_specs=in_vmem(2 + len(rest)), out_specs...  89.9 us
    pallas_call x1, Pallas kernels, finish(): pl.pallas_call(finish_kernel, in_specs=in_vmem(10) + [apart] * 4, out_spe...  62.9 us
    pallas_call x1, Pallas kernels, feed_grads(): pl.pallas_call(feed_grads_kernel, in_specs=in_vmem(4) + [pl.BlockSpec(mem...  59.2 us
    pallas_call x1, Pallas kernels, middle_pass(): pl.pallas_call(middle_kernel, grid=(half // rows,), in_specs=[tok(width),...  38.5 us
    unnamed x31, local copies, waits for them, and re-layouts  9.27 us
  transfers between devices with their start and end apart: 2, of which 0 were waited for; matrix products, arithmetic and copies ran while one was open for 1% of the time, Pallas kernels for 23%

profile of v6, /device:TPU:0, one launch (start us, length us, event | category | flops | bytes accessed | tf_op | source)
XLA Modules:
  0.0 383.5 jit_solution(11490875065832113170)
XLA Ops:
  7.2 0.0 copy-start.5
  7.2 0.0 copy-start.6
  7.2 0.0 copy-start.7
  7.2 0.0 copy-start.8
  7.2 0.0 copy-start.9
  7.2 0.0 all-gather.5.cloned.1.call-start
  7.3 0.7 all-gather.5.cloned.1.call-update
  8.0 0.0 all-gather.7.cloned.1.call-start
  8.0 0.7 all-gather.7.cloned.1.call-update
  8.8 0.1 pad_maximum_fusion.2
  8.9 0.0 copy-done.5
  8.9 0.3 dynamic-update-slice
  9.2 0.0 copy-done.6
  9.2 0.2 dynamic-update-slice.1
  9.4 0.0 copy-done.7
  9.4 0.2 dynamic-update-slice.2
  9.6 0.0 copy-done.8
  9.6 0.2 dynamic-update-slice.3
  9.8 0.0 copy-done.9
  9.9 0.2 dynamic-update-slice.4
  10.1 0.6 broadcast_in_dim.2.params_ref
  10.7 0.2 multiply_cosine_fusion
  10.9 0.6 pad_maximum_fusion
  11.5 89.9 %forward_attention.1 = (bf16[12,3,512,128]{3,2,1,0:T(8,128)(2,1)}, bf16[12,512,128]{2,1,0:T(8,128)(2,1)}, bf16[2,4,3,512,128]{4,3,2,1,0:T(8,128)(2,1)}, bf16[2,4...) custom-call(bf16[2,512,768]{2,1,0:T(8,128)(2,1)} %bitcast.29, ...), custom_call_target="tpu_custom_call" | custom-call | flops 99999997952 | bytes 8000000 | tf_op jit(solution)/shard_map/forward_attention/pallas_call | solution.py:865
  101.5 0.0 all-gather.5.cloned.1.call-done
  101.5 0.0 all-gather.7.cloned.1.call-done
  101.5 38.5 %middle_pass.1 = (bf16[2,512,768]{2,1,0:T(8,128)(2,1)}, bf16[2,512,768]{2,1,0:T(8,128)(2,1)}, bf16[2,512,768]{2,1,0:T(8,128)(2,1)}, bf16[2,512,3072]{2,1,0:T(8,1...) custom-call(bf16[2,512,768]{2,1,0:T(8,128)(2,1)} %bitcast.30, ...), custom_call_target="tpu_custom_call" | custom-call | tf_op jit(solution)/shard_map/middle_pass/pallas_call | solution.py:1267
  140.0 59.2 %feed_grads.1 = (bf16[2,4,18,144,128]{4,3,2,1,0:T(8,128)(2,1)}, bf16[2,4,512,128]{3,2,1,0:T(8,128)(2,1)}) custom-call(bf16[1024,768]{1,0:T(8,128)(2,1)} %bitcast.38, bf16[1024,768]{1,0:T(8,128)(2,1)} %bitcast.39, bf16[1024,768]{1,0:T(8,128)(2,1)} %bitcast.37, bf16[1024,768]{1,0:T(8,128)(2,1)} %bitcast.40, bf16[1024,3072]{1,0:T(8,128)(2,1)} %bitcast.33, ...), custom_call_target="tpu_custom_call" | custom-call | flops 24000000000 | bytes 20000000 | tf_op jit(solution)/shard_map/feed_grads/pallas_call | solution.py:1430
  199.3 100.4 %backward_attention.1 = (bf16[12,3,512,128]{3,2,1,0:T(8,128)(2,1)}, bf16[4,9,144,128]{3,2,1,0:T(8,128)(2,1)}) custom-call(bf16[12,3,512,128]{3,2,1,0:T(8,128)(2,1)} %get-tuple-element.53.packs_ref, bf16[12,512,128]{2,1,0:T(8,128)(2,1)} %get-tuple-element.54.gatt.gatt_ref, bf16[12,512,128]{2,1,0:T(8,128)(2,1)} %get-tuple-element.49.att_ref, ...), custom_call_target="tpu_custom_call" | custom-call | flops 120000004096 | bytes 8000000 | tf_op jit(solution)/shard_map/backward_attention/pallas_call | solution.py:1133
  299.7 62.9 %finish.1 = (f32[48,2304]{1,0:T(8,128)}, f32[192,768]{1,0:T(8,128)}, f32[192,768]{1,0:T(8,128)}, f32[48,768]{1,0:T(8,128)}, f32[40,128]{1,0:T(8,128)}, /*index=5...) custom-call(bf16[12,3,512,128]{3,2,1,0:T(8,128)(2,1)} %get-tuple-element.67.packs, ...), custom_call_target="tpu_custom_call" | custom-call | flops 60000002048 | bytes 20000000 | tf_op jit(solution)/shard_map/finish/pallas_call | solution.py:1684
  362.6 0.8 slice_bitcast_fusion.1
  363.4 0.7 slice_bitcast_fusion
  364.1 1.1 constant_dynamic-slice_fusion
  365.1 0.8 copy.27
  365.9 0.6 dynamic_slice.20
  366.5 0.6 dynamic_slice.21
  367.1 0.6 dynamic_slice.23
  367.7 0.7 dynamic_slice.19
  368.3 0.6 dynamic_slice.22
  368.9 0.0 copy-start.4
  368.9 0.0 copy-start.2
  368.9 0.0 copy-start.3
  368.9 3.8 copy.39
  372.8 0.0 copy-done.4
  372.8 0.0 copy-start.1
  372.8 0.0 copy-start
  372.8 0.6 copy.40
  373.4 0.0 copy-done.2
  373.4 0.8 copy.41
  374.2 0.0 copy-done.3
  374.2 0.7 copy.42
  374.8 0.0 copy-done.1
  374.8 0.8 copy.43
  375.6 0.0 copy-done
  375.6 0.8 copy.44
  (4 shorter events, 0.0 us)
Async XLA Ops:
  7.2 1.7 copy-start.5
  7.2 2.0 copy-start.6
  7.2 2.2 copy-start.7
  7.2 2.4 copy-start.8
  7.2 2.6 copy-start.9
  7.2 94.3 %all-gather.5.cloned.1.call-start = ((), (), s32[]{:S(2)}) async-start(), calls=%async_computation | async-start | bytes 5898240 | tf_op jit(solution)/shard_map/all_gather | solution.py:1730
  8.0 93.5 %all-gather.7.cloned.1.call-start = ((), (), s32[]{:S(2)}) async-start(), calls=%async_computation.1 | async-start | bytes 5898240 | tf_op jit(solution)/shard_map/all_gather | solution.py:1731
  368.9 3.8 copy-start.4
  368.9 4.4 %copy-start.2 = (f32[48,2304]{1,0:T(8,128)S(1)}, f32[48,2304]{1,0:T(8,128)}, u32[]{:S(2)}) copy-start(f32[48,2304]{1,0:T(8,128)} %get-tuple-element.129) | copy-start | bytes 1327108
  368.9 5.2 %copy-start.3 = (f32[48,768]{1,0:T(8,128)S(1)}, f32[48,768]{1,0:T(8,128)}, u32[]{:S(2)}) copy-start(f32[48,768]{1,0:T(8,128)} %get-tuple-element.130) | copy-start | bytes 442372
  372.8 2.1 copy-start.1
  372.8 2.9 copy-start
Sparse Core Ops, SparseCore 0:
  9.6 40.6 all-gather.4
  51.9 36.9 all-gather.6
